TPU v7x, 32 devices: a whole 2x2x4 slice. The times are simulated.
32 devices in a mesh: section: 2 (over y), expert: 16 (over z, x, core).
Axes of the slice: x: 2, y: 2, z: 4, core: 2. Of those that a mesh axis runs over, the one named last changes fastest.
Arguments:
- embedded: bfloat16 [2048, 3584], P('expert'), may hold values from -6 to 6
- forward_held: bfloat16 [2, 2048, 3584], P('section', 'expert'), may hold values from -6 to 6
- forward_route: int32 [2, 2048, 1], P('section', 'expert'), may hold values from 0 to 3; in each aligned block of 128 rows (0 to 127, 128 to 255, ..., all dimensions but the last counted through in order) at most 48 rows name the same one
- forward_weight: float32 [2, 2048], P('section', 'expert'), may hold values from 0.2 to 1
- loss_cotangent: bfloat16 [2048, 3584], P('expert'), may hold values from -6 to 6
- backward_held: bfloat16 [2, 2048, 3584], P('section', 'expert'), may hold values from -6 to 6
- backward_route: int32 [2, 2048, 1], P('section', 'expert'), may hold values from 0 to 3; in each aligned block of 128 rows (0 to 127, 128 to 255, ..., all dimensions but the last counted through in order) at most 48 rows name the same one
- backward_weight: float32 [2, 2048], P('section', 'expert'), may hold values from 0.2 to 1
- saved_gate: bfloat16 [2, 768, 4096], P('section', None, 'expert'), may hold values from -6 to 6
- saved_up: bfloat16 [2, 768, 4096], P('section', None, 'expert'), may hold values from -6 to 6
- gate_weight: bfloat16 [2, 3584, 4096], P('section', None, 'expert'), may hold values from -0.09375 to 0.09375
- up_weight: bfloat16 [2, 3584, 4096], P('section', None, 'expert'), may hold values from -0.09375 to 0.09375
- down_weight: bfloat16 [2, 4096, 3584], P('section', 'expert'), may hold values from -0.1875 to 0.1875
- steering: float32 [2, 3584], P('section'), may hold values from -6 to 6
Outputs:
- forward_out: bfloat16 [2, 2048, 3584], P('section', 'expert')
- forward_coefficient: float32 [2, 2048], P('section', 'expert')
- backward_out: bfloat16 [2, 2048, 3584], P('section', 'expert')
Inputs may be any that keep to these rules, and one draw needn't show every extreme that they name: `forward_route`: in each aligned block of 128 tokens of a layer (the tokens of one device) no expert is chosen more than 48 times, and some expert is chosen exactly 48 times in some block. `backward_route`: in each aligned block of 128 tokens of a layer (the tokens of one device) no expert is chosen more than 48 times, and some expert is chosen exactly 48 times in some block.
All inputs are finite; a program needn't handle non-finite values.
Results may differ from a plain program's by a relative error of at most 0.0058.
Values may be sent and summed in bfloat16 or wider, within the bound.
No kernel may reach another device: no remote copies, remote signals or barrier semaphores. Data moves between devices by JAX's collectives and lax.ppermute only.
A program may use at most 64 MiB of HBM per device.

v0:
```python
import jax
import jax.numpy as jnp
from jax import lax
from jax.sharding import PartitionSpec as P

H = 1024


def shifted(value, axis, by):
    devices = lax.axis_size(axis)
    pairs = [(i, i + by) for i in range(devices) if 0 <= i + by < devices]
    return lax.ppermute(value, axis, pairs)


def dispatch_layout(expert_ids, expert_count, capacity):
    onehot = (expert_ids[:, None] == jnp.arange(expert_count, dtype=jnp.int32)[None, :]).astype(
        jnp.int32
    )
    earlier = jnp.cumsum(onehot, axis=0) - onehot
    position = jnp.sum(earlier * onehot, axis=1)
    target = expert_ids * capacity + position
    return (
        jnp.arange(expert_count * capacity, dtype=jnp.int32)[:, None] == target[None, :]
    ).astype(jnp.bfloat16)


def spread_rows(layout, tokens, holder_count, capacity):
    chosen = jnp.dot(layout, tokens, preferred_element_type=jnp.float32).astype(jnp.bfloat16)
    feature_count = tokens.shape[1]
    grouped = chosen.reshape(-1, 1, capacity, feature_count)
    copies = jnp.broadcast_to(grouped, (grouped.shape[0], holder_count, capacity, feature_count))
    return copies.reshape(-1, capacity, feature_count)


def merge_holders(arrived, expert_count, holder_count):
    capacity = arrived.shape[1]
    feature_count = arrived.shape[2]
    grouped = arrived.reshape(expert_count, holder_count, capacity, feature_count).astype(
        jnp.float32
    )
    return (
        jnp.sum(grouped, axis=1)
        .astype(jnp.bfloat16)
        .reshape(expert_count * capacity, feature_count)
    )


def expert_forward(slot_rows, weights):
    gate_cols, up_cols, down_rows = weights
    gate_pre = jnp.dot(slot_rows, gate_cols, preferred_element_type=jnp.float32)
    up_pre = jnp.dot(slot_rows, up_cols, preferred_element_type=jnp.float32)
    hidden = (jax.nn.silu(gate_pre) * up_pre).astype(jnp.bfloat16)
    return jnp.dot(hidden, down_rows, preferred_element_type=jnp.float32).astype(jnp.bfloat16)


def expert_backward(slot_rows, gate_saved, up_saved, weights):
    gate_cols, up_cols, down_rows = weights
    contract = (((1,), (1,)), ((), ()))
    grad_hidden = lax.dot_general(
        slot_rows, down_rows, contract, preferred_element_type=jnp.float32
    )
    gate_pre = gate_saved.astype(jnp.float32)
    up_pre = up_saved.astype(jnp.float32)
    sigmoid_gate = jax.nn.sigmoid(gate_pre)
    grad_gate = (
        grad_hidden * up_pre * sigmoid_gate * (1.0 + gate_pre * (1.0 - sigmoid_gate))
    ).astype(jnp.bfloat16)
    grad_up = (grad_hidden * gate_pre * sigmoid_gate).astype(jnp.bfloat16)
    grad_part = lax.dot_general(grad_gate, gate_cols, contract, preferred_element_type=jnp.float32)
    grad_part = grad_part + lax.dot_general(
        grad_up, up_cols, contract, preferred_element_type=jnp.float32
    )
    return grad_part.astype(jnp.bfloat16)


def over_slots(compute, inputs, feature_count):
    device_count = inputs[0].shape[0]
    capacity = inputs[0].shape[1]
    flattened = tuple(
        (member.reshape(device_count * capacity, member.shape[2]) for member in inputs)
    )
    return compute(*flattened).reshape(device_count, capacity, feature_count)


def body(
    embedded,
    forward_held,
    forward_route,
    forward_weight,
    loss_cotangent,
    backward_held,
    backward_route,
    backward_weight,
    saved_gate,
    saved_up,
    gate_weight,
    up_weight,
    down_weight,
    steering,
):
    section_count = lax.axis_size("section")
    section_index = lax.axis_index("section")
    device_count = lax.axis_size("expert")
    local_hidden = gate_weight.shape[2]
    holder_count = H // local_hidden
    expert_count = device_count // holder_count
    capacity = saved_gate.shape[1] // device_count
    feature_count = embedded.shape[1]
    arriving = shifted(forward_held, "section", 1)[0]
    forward_in = jnp.where(section_index == 0, embedded, arriving)
    returning = shifted(backward_held, "section", -1)[0]
    backward_in = jnp.where(section_index == section_count - 1, loss_cotangent, returning)
    direction = steering[0]
    unit_dir = direction / jnp.sqrt(jnp.sum(direction * direction) + 1e-06)
    weights = (gate_weight[0], up_weight[0], down_weight[0])
    forward_layout = dispatch_layout(forward_route[0, :, 0], expert_count, capacity)
    forward_send = spread_rows(forward_layout, forward_in, holder_count, capacity)
    backward_dy = backward_in.astype(jnp.float32)
    along_dir = jnp.sum(backward_dy * unit_dir[None, :], axis=1)
    sent_rows = (
        backward_weight[0][:, None] * (backward_dy - along_dir[:, None] * unit_dir[None, :])
    ).astype(jnp.bfloat16)
    backward_layout = dispatch_layout(backward_route[0, :, 0], expert_count, capacity)
    backward_send = spread_rows(backward_layout, sent_rows, holder_count, capacity)
    gate_saved = saved_gate[0].reshape(device_count, capacity, local_hidden)
    up_saved = saved_up[0].reshape(device_count, capacity, local_hidden)

    def forward_compute(slot_rows):
        return expert_forward(slot_rows, weights)

    def backward_compute(slot_rows, gate_rows, up_rows):
        return expert_backward(slot_rows, gate_rows, up_rows, weights)

    forward_arrived = lax.all_to_all(
        forward_send, "expert", split_axis=0, concat_axis=0, tiled=True
    )
    forward_part = over_slots(forward_compute, (forward_arrived,), feature_count)
    forward_back = lax.all_to_all(forward_part, "expert", split_axis=0, concat_axis=0, tiled=True)
    backward_arrived = lax.all_to_all(
        backward_send, "expert", split_axis=0, concat_axis=0, tiled=True
    )
    backward_part = over_slots(
        backward_compute, (backward_arrived, gate_saved, up_saved), feature_count
    )
    backward_back = lax.all_to_all(backward_part, "expert", split_axis=0, concat_axis=0, tiled=True)
    contract = (((0,), (0,)), ((), ()))
    forward_rows = merge_holders(forward_back, expert_count, holder_count)
    picked = lax.dot_general(
        forward_layout, forward_rows, contract, preferred_element_type=jnp.float32
    )
    mixed_rows = forward_weight[0][:, None] * picked
    coefficient = jnp.sum(mixed_rows * unit_dir[None, :], axis=1)
    forward_out = (
        forward_in.astype(jnp.float32) + mixed_rows - coefficient[:, None] * unit_dir[None, :]
    ).astype(jnp.bfloat16)
    backward_rows = merge_holders(backward_back, expert_count, holder_count)
    returned = lax.dot_general(
        backward_layout, backward_rows, contract, preferred_element_type=jnp.float32
    )
    backward_out = (backward_dy + returned).astype(jnp.bfloat16)
    return (forward_out[None], coefficient[None], backward_out[None])


def solution(mesh):
    in_specs = (
        P("expert", None),
        P("section", "expert", None),
        P("section", "expert", None),
        P("section", "expert"),
        P("expert", None),
        P("section", "expert", None),
        P("section", "expert", None),
        P("section", "expert"),
        P("section", None, "expert"),
        P("section", None, "expert"),
        P("section", None, "expert"),
        P("section", None, "expert"),
        P("section", "expert", None),
        P("section", None),
    )
    out_specs = (P("section", "expert", None), P("section", "expert"), P("section", "expert", None))
    return jax.shard_map(body, mesh=mesh, in_specs=in_specs, out_specs=out_specs, check_vma=False)
```

profile of v0, /device:TPU:8, one launch (start us, length us, event | category | flops | bytes accessed | tf_op | source)
XLA Modules:
  0.0 565.5 jit_solution(2343572222953437301)
XLA Ops:
  0.6 0.0 copy-start
  0.6 3.6 collective-permute-start
  4.3 0.7 fusion.51
  5.0 0.2 reduce_window_sum.17
  5.2 0.8 select_reduce_fusion.1
  6.0 0.7 multiply_add_fusion.1
  6.7 17.4 %collective-permute-done = bf16[1,128,3584]{2,1,0:T(8,128)(2,1)S(1)} collective-permute-done((bf16[1,128,3584]{2,1,0:T(8,128)(2,1)}, bf16[1,128,3584]{2,1,0:T(8,128)(2,1)S(1)}, u32[]{:S(2)}, u32[]{:S(2)}) %collective-permute-start) | collective-permute-done | bytes 917536 | tf_op jit(solution)/shard_map/ppermute | solution.py:12
  24.1 0.0 copy-start.2
  24.1 2.0 convolution_convert_fusion.2
  26.1 0.5 broadcast_in_dim.15
  26.7 0.0 copy-done.2
  26.7 0.0 copy-start.3
  26.7 126.9 %all_to_all.20 = bf16[16,48,3584]{2,1,0:T(8,128)(2,1)S(1)} all-to-all(bf16[16,48,3584]{2,1,0:T(8,128)(2,1)S(1)} %bitcast.76), channel_id=1, replica_groups=mesh['section'=2,'expert'=16] {'expert'}, dimensions={0} | all-to-all | bytes 11010048 | tf_op jit(solution)/shard_map/all_to_all | solution.py:134
  153.6 0.0 copy-start.1
  153.6 2.5 copy-done.1
  156.1 0.0 copy-done.3
  156.1 1.6 fusion.13
  157.7 0.0 copy-done
  157.7 11.3 %convolution_convert_fusion = bf16[768,3584]{1,0:T(8,128)(2,1)} fusion(bf16[1,256,3584]{2,1,0:T(8,128)(2,1)} %param.26, bf16[768,3584]{1,0:T(8,128)(2,1)} %bitcast.80, bf16[1,3584,256]{2,1,0:T(8,128)(2,1)S(1)} %copy-done, f32[768,256]{1,0:T(8,128)S(1)} %fusion.13), kind=kOutput, calls=%fused_computation.1 | convolution fusion | flops 2822504448 | bytes 15466496 | tf_op jit(solution)/shard_map/dot_general | solution.py:53
  169.0 0.0 copy-start.10
  169.0 0.0 copy-start.9
  169.0 5.3 all-to-all-start.1
  174.2 1.3 collective-permute-start.1
  175.5 0.0 copy-done.10
  175.5 0.1 fusion.50
  175.6 0.0 copy-done.9
  175.6 0.6 multiply_reduce_fusion.1
  177.0 0.2 reduce_window_sum.18
  177.1 0.2 select_reduce_fusion
  177.3 0.1 divide_reduce_fusion
  177.4 0.0 copy-start.12
  177.4 115.8 %all-to-all-done.1 = bf16[16,48,3584]{2,1,0:T(8,128)(2,1)} async-done(((bf16[16,48,3584]{2,1,0:T(8,128)(2,1)}), bf16[16,48,3584]{2,1,0:T(8,128)(2,1)}, u32[]{:S(2)}, u32[]{:S(2)}) %all-to-all-start.1) | async-done | bytes 5505056 | tf_op jit(solution)/shard_map/all_to_all | solution.py:138
  293.1 0.0 copy-start.6
  293.1 3.5 bitcast_reduce_fusion.1
  296.6 0.0 collective-permute-done.1
  296.6 0.0 copy-start.7
  296.6 0.9 copy-done.7
  297.5 0.0 copy-done.12
  297.6 0.0 copy-done.6
  297.6 0.0 copy-start.13
  297.6 3.2 fusion.2
  300.8 0.0 copy-start.11
  300.8 0.0 copy-done.13
  300.8 0.6 convolution_convert_fusion.1
  301.4 0.5 broadcast_in_dim.19
  301.9 0.0 copy-start.14
  301.9 127.2 %all_to_all.21 = bf16[16,48,3584]{2,1,0:T(8,128)(2,1)S(1)} all-to-all(bf16[16,48,3584]{2,1,0:T(8,128)(2,1)S(1)} %bitcast.77), channel_id=1, replica_groups=mesh['section'=2,'expert'=16] {'expert'}, dimensions={0} | all-to-all | bytes 11010048 | tf_op jit(solution)/shard_map/all_to_all | solution.py:139
  429.2 0.0 copy-done.14
  429.2 0.0 copy-start.4
  429.2 0.0 copy-start.5
  429.2 0.0 copy-start.8
  429.2 1.6 fusion.5
  430.8 0.0 copy-done.4
  430.8 0.0 copy-done.5
  430.8 0.0 copy-done.8
  430.8 1.8 fusion.11
  432.6 4.2 add_convert_fusion
  436.8 5.1 all-to-all-start.3
  441.9 0.0 copy-done.11
  441.9 3.3 fusion.23
  445.2 115.6 %all-to-all-done.3 = bf16[16,48,3584]{2,1,0:T(8,128)(2,1)} async-done(((bf16[16,48,3584]{2,1,0:T(8,128)(2,1)}), bf16[16,48,3584]{2,1,0:T(8,128)(2,1)}, u32[]{:S(2)}, u32[]{:S(2)}) %all-to-all-start.3) | async-done | bytes 5505056 | tf_op jit(solution)/shard_map/all_to_all | solution.py:145
  560.8 3.4 bitcast_reduce_fusion
  564.2 1.4 fusion.1
  (1 shorter events, 0.0 us)
Async XLA Ops:
  0.6 157.0 %copy-start = (bf16[1,3584,256]{2,1,0:T(8,128)(2,1)S(1)}, bf16[1,3584,256]{2,1,0:T(8,128)(2,1)}, u32[]{:S(2)}) copy-start(bf16[1,3584,256]{2,1,0:T(8,128)(2,1)} %param.25) | copy-start | bytes 5505028
  0.6 23.5 %collective-permute-start = (bf16[1,128,3584]{2,1,0:T(8,128)(2,1)}, bf16[1,128,3584]{2,1,0:T(8,128)(2,1)S(1)}, u32[]{:S(2)}, u32[]{:S(2)}) collective-permute-start(bf16[1,128,3584]{2,1,0:T(8,128)(2,1)} %param.15), channel_id=1, source_target_pairs={{0,16},{1,17},{2,18},{3,19},{4,20},{5,21},{6,22},{7,23},{8,24},{9,... | collective-permute-start | bytes 2752520 | tf_op jit(solution)/shard_map/ppermute | solution.py:12
  24.1 2.6 copy-start.2
  26.7 129.4 %copy-start.3 = (bf16[1,3584,256]{2,1,0:T(8,128)(2,1)S(1)}, bf16[1,3584,256]{2,1,0:T(8,128)(2,1)}, u32[]{:S(2)}) copy-start(bf16[1,3584,256]{2,1,0:T(8,128)(2,1)} %param.24) | copy-start | bytes 5505028
  153.6 2.5 copy-start.1
  169.0 6.6 %copy-start.10 = (s32[1,128,1]{1,2,0:T(1,128)S(1)}, s32[1,128,1]{1,2,0:T(1,128)}, u32[]{:S(2)}) copy-start(s32[1,128,1]{1,2,0:T(1,128)} %param.20) | copy-start | bytes 1540
  169.0 6.7 %copy-start.9 = (f32[1,3584]{1,0:T(1,128)S(1)}, f32[1,3584]{1,0:T(1,128)}, u32[]{:S(2)}) copy-start(f32[1,3584]{1,0:T(1,128)} %param.27) | copy-start | bytes 43012
  169.0 124.2 %all-to-all-start.1 = ((bf16[16,48,3584]{2,1,0:T(8,128)(2,1)}), bf16[16,48,3584]{2,1,0:T(8,128)(2,1)}, u32[]{:S(2)}, u32[]{:S(2)}) async-start(bf16[16,48,3584]{2,1,0:T(8,128)(2,1)} %bitcast.78), calls=%async_computation.1 | async-start | bytes 11010048 | tf_op jit(solution)/shard_map/all_to_all | solution.py:138
  174.2 122.4 %collective-permute-start.1 = (bf16[1,128,3584]{2,1,0:T(8,128)(2,1)}, bf16[1,128,3584]{2,1,0:T(8,128)(2,1)S(1)}, u32[]{:S(2)}, u32[]{:S(2)}) collective-permute-start(bf16[1,128,3584]{2,1,0:T(8,128)(2,1)} %param.19), channel_id=1, source_target_pairs={{16,0},{17,1},{18,2},{19,3},{20,4},{21,5},{22,6},{23,7},{24,8},{25... | collective-permute-start | bytes 2752520 | tf_op jit(solution)/shard_map/ppermute | solution.py:12
  177.4 120.2 %copy-start.12 = (f32[1,128]{1,0:T(1,128)S(1)}, f32[1,128]{1,0:T(1,128)}, u32[]{:S(2)}) copy-start(f32[1,128]{1,0:T(1,128)} %param.17) | copy-start | bytes 1540
  293.1 4.4 copy-start.6
  296.6 0.9 copy-start.7
  297.6 3.2 copy-start.13
  300.8 141.1 %copy-start.11 = (f32[128]{0:T(128)}, f32[128]{0:T(128)S(1)}, u32[]{:S(2)}) copy-start(f32[128]{0:T(128)S(1)} %get-tuple-element.4) | copy-start | bytes 1540
  301.9 127.2 %copy-start.14 = (bf16[1,256,3584]{2,1,0:T(8,128)(2,1)S(1)}, bf16[1,256,3584]{2,1,0:T(8,128)(2,1)}, u32[]{:S(2)}) copy-start(bf16[1,256,3584]{2,1,0:T(8,128)(2,1)} %param.26) | copy-start | bytes 5505028
  429.2 1.6 copy-start.4
  429.2 1.6 copy-start.5
  429.2 1.7 copy-start.8
  436.8 124.0 %all-to-all-start.3 = ((bf16[16,48,3584]{2,1,0:T(8,128)(2,1)}), bf16[16,48,3584]{2,1,0:T(8,128)(2,1)}, u32[]{:S(2)}, u32[]{:S(2)}) async-start(bf16[16,48,3584]{2,1,0:T(8,128)(2,1)} %bitcast.75), calls=%async_computation.3 | async-start | bytes 11010048 | tf_op jit(solution)/shard_map/all_to_all | solution.py:145
where the time goes:
time: 568 us; the launch traced here: 566 us
  blocking collectives  254 us (45%)
  waiting for transfers between devices  249 us (44%)
  matrix products  27.6 us (5%)
  starting transfers between devices  15.3 us (3%)
  other arithmetic  13.7 us (2%)
    all_to_all x1, blocking collectives, body(): lax.all_to_all(backward_send, 'expert', split_axis=0, concat_axis=0, tile...  127 us
    all_to_all x1, blocking collectives, body(): lax.all_to_all(forward_send, 'expert', split_axis=0, concat_axis=0, tiled...  127 us
    all_to_all x1, waiting for transfers between devices, body(): lax.all_to_all(forward_part, 'expert', split_axis=0, concat_axis=0, tiled...  116 us
    all_to_all x1, waiting for transfers between devices, body(): lax.all_to_all(backward_part, 'expert', split_axis=0, concat_axis=0, tile...  116 us
    ppermute x2, waiting for transfers between devices, shifted(): return lax.ppermute(value, axis, pairs)  17.4 us
  transfers between devices with their start and end apart: 4, of which 3 were waited for; matrix products, arithmetic and copies ran while one was open for 2% of the time, Pallas kernels for 0%

commit v1 on v0

v1 whole, which is shorter than its diff:
```python
import jax
import jax.numpy as jnp
from jax import lax
from jax.sharding import PartitionSpec as P

H = 1024
CORES = 2
BF16 = jnp.bfloat16
F32 = jnp.float32
ROWS_BY_ROWS = (((1,), (1,)), ((), ()))
COLS_BY_COLS = (((0,), (0,)), ((), ()))


def shifted(value, axis, by):
    devices = lax.axis_size(axis)
    pairs = [(i, i + by) for i in range(devices) if 0 <= i + by < devices]
    return lax.ppermute(value, axis, pairs)


def dispatch_layout(expert_ids, first_expert, expert_count, capacity):
    onehot = (expert_ids[:, None] == jnp.arange(expert_count, dtype=jnp.int32)[None, :]).astype(jnp.int32)
    earlier = jnp.cumsum(onehot, axis=0) - onehot
    position = jnp.sum(earlier * onehot, axis=1)
    target = lax.rem(expert_ids - first_expert + expert_count, expert_count) * capacity + position
    slots = jnp.arange(expert_count * capacity, dtype=jnp.int32)
    return (slots[:, None] == target[None, :]).astype(BF16)


def body(
    embedded,
    forward_held,
    forward_route,
    forward_weight,
    loss_cotangent,
    backward_held,
    backward_route,
    backward_weight,
    saved_gate,
    saved_up,
    gate_weight,
    up_weight,
    down_weight,
    steering,
):
    section_count = lax.axis_size("section")
    section_index = lax.axis_index("section")
    device_count = lax.axis_size("expert")
    device_index = lax.axis_index("expert")
    local_hidden = gate_weight.shape[2]
    holders = H // local_hidden
    experts = device_count // holders
    chips = holders // CORES
    capacity = saved_gate.shape[1] // device_count
    plane = device_index // holders
    chip = lax.rem(device_index, holders) // CORES
    core = lax.rem(device_index, CORES)

    def to_plane(value, by):
        pairs = [(i, (i + by * holders) % device_count) for i in range(device_count)]
        return lax.ppermute(value, "expert", pairs)

    def to_chip(value, by):
        pairs = [(i, i // holders * holders + (i + by * CORES) % holders) for i in range(device_count)]
        return lax.ppermute(value, "expert", pairs)

    def to_core(value):
        return lax.ppermute(value, "expert", [(i, i ^ 1) for i in range(device_count)])

    arriving = shifted(forward_held, "section", 1)[0]
    returning = shifted(backward_held, "section", -1)[0]
    forward_in = jnp.where(section_index == 0, embedded, arriving)
    backward_in = jnp.where(section_index == section_count - 1, loss_cotangent, returning)

    gate, up, down = gate_weight[0], up_weight[0], down_weight[0]
    gate_chip = jnp.concatenate([gate, to_core(gate)], axis=1)
    up_chip = jnp.concatenate([up, to_core(up)], axis=1)
    down_of = [down] + [to_chip(down, -s) for s in range(1, chips)]
    down_chips = [jnp.concatenate([d, to_core(d)], axis=0) for d in down_of]

    sources = (
        lax.rem(plane - jnp.arange(experts, dtype=jnp.int32) + experts, experts)[None, :] * holders
        + lax.rem(chip + jnp.arange(chips, dtype=jnp.int32), chips)[:, None] * CORES
    ).reshape(-1)

    def rows_of(core_index):
        wanted = ((sources + core_index)[:, None] * capacity + jnp.arange(capacity, dtype=jnp.int32)[None, :]).reshape(-1)
        return (wanted[:, None] == jnp.arange(saved_gate.shape[1], dtype=jnp.int32)[None, :]).astype(BF16)

    saved = jnp.concatenate([saved_gate[0], saved_up[0]], axis=1)
    saved_kept = jnp.dot(rows_of(core), saved, preferred_element_type=F32).astype(BF16)
    saved_got = to_core(jnp.dot(rows_of(1 - core), saved, preferred_element_type=F32).astype(BF16))
    gate_saved = jnp.concatenate([saved_kept[:, :local_hidden], saved_got[:, :local_hidden]], axis=1)
    up_saved = jnp.concatenate([saved_kept[:, local_hidden:], saved_got[:, local_hidden:]], axis=1)

    direction = steering[0]
    unit_dir = direction / jnp.sqrt(jnp.sum(direction * direction) + 1e-06)

    def dispatched(layout, tokens):
        chosen = jnp.dot(layout, tokens, preferred_element_type=F32).astype(BF16)
        blocks = [chosen[k * capacity : (k + 1) * capacity] for k in range(experts)]
        return [blocks[0]] + [to_plane(blocks[k], k) for k in range(1, experts)]

    def returned(blocks):
        back = [blocks[0]] + [to_plane(blocks[k], -k) for k in range(1, experts)]
        return jnp.concatenate(back, axis=0)

    def split(rows):
        return [rows[k * capacity : (k + 1) * capacity] for k in range(experts)]

    forward_layout = dispatch_layout(forward_route[0, :, 0], plane, experts, capacity)
    forward_blocks = dispatched(forward_layout, forward_in)
    backward_dy = backward_in.astype(F32)
    along_dir = jnp.sum(backward_dy * unit_dir[None, :], axis=1)
    sent_rows = (backward_weight[0][:, None] * (backward_dy - along_dir[:, None] * unit_dir[None, :])).astype(BF16)
    backward_layout = dispatch_layout(backward_route[0, :, 0], plane, experts, capacity)
    backward_blocks = dispatched(backward_layout, sent_rows)

    def hidden_of(rows):
        gate_pre = jnp.dot(rows, gate_chip, preferred_element_type=F32)
        up_pre = jnp.dot(rows, up_chip, preferred_element_type=F32)
        return (jax.nn.silu(gate_pre) * up_pre).astype(BF16)

    forward_rows = jnp.concatenate(forward_blocks, axis=0)
    hidden = [hidden_of(forward_rows)]
    for s in range(1, chips):
        across = jnp.concatenate([to_chip(block, s) for block in forward_blocks], axis=0)
        hidden.append(to_chip(hidden_of(across), -s))
    forward_part = sum(jnp.dot(hidden[s], down_chips[s], preferred_element_type=F32) for s in range(chips))
    forward_back = returned(split(forward_part.astype(BF16)))

    backward_rows = jnp.concatenate(backward_blocks, axis=0)
    grad_hidden = []
    for s in range(chips):
        grads = lax.dot_general(backward_rows, down_chips[s], ROWS_BY_ROWS, preferred_element_type=F32)
        grad_hidden.append(grads if s == 0 else to_chip(grads.astype(BF16), s).astype(F32))
    row_count = experts * capacity
    parts = []
    for s in range(chips):
        at = (chips - s) % chips
        gate_pre = gate_saved[at * row_count : (at + 1) * row_count].astype(F32)
        up_pre = up_saved[at * row_count : (at + 1) * row_count].astype(F32)
        sigmoid_gate = jax.nn.sigmoid(gate_pre)
        grad_gate = (grad_hidden[s] * up_pre * sigmoid_gate * (1.0 + gate_pre * (1.0 - sigmoid_gate))).astype(BF16)
        grad_up = (grad_hidden[s] * gate_pre * sigmoid_gate).astype(BF16)
        part = lax.dot_general(grad_gate, gate_chip, ROWS_BY_ROWS, preferred_element_type=F32)
        part = part + lax.dot_general(grad_up, up_chip, ROWS_BY_ROWS, preferred_element_type=F32)
        parts.append(part)
    mine = split(parts[0])
    for s in range(1, chips):
        got = [to_chip(block, -s) for block in split(parts[s].astype(BF16))]
        mine = [a + b.astype(F32) for a, b in zip(mine, got)]
    backward_back = returned([block.astype(BF16) for block in mine])

    picked = lax.dot_general(forward_layout, forward_back, COLS_BY_COLS, preferred_element_type=F32)
    mixed_rows = forward_weight[0][:, None] * picked
    coefficient = jnp.sum(mixed_rows * unit_dir[None, :], axis=1)
    forward_out = (forward_in.astype(F32) + mixed_rows - coefficient[:, None] * unit_dir[None, :]).astype(BF16)
    grad_rows = lax.dot_general(backward_layout, backward_back, COLS_BY_COLS, preferred_element_type=F32)
    backward_out = (backward_dy + grad_rows).astype(BF16)
    return (forward_out[None], coefficient[None], backward_out[None])


def solution(mesh):
    in_specs = (
        P("expert", None),
        P("section", "expert", None),
        P("section", "expert", None),
        P("section", "expert"),
        P("expert", None),
        P("section", "expert", None),
        P("section", "expert", None),
        P("section", "expert"),
        P("section", None, "expert"),
        P("section", None, "expert"),
        P("section", None, "expert"),
        P("section", None, "expert"),
        P("section", "expert", None),
        P("section", None),
    )
    out_specs = (P("section", "expert", None), P("section", "expert"), P("section", "expert", None))
    return jax.shard_map(body, mesh=mesh, in_specs=in_specs, out_specs=out_specs, check_vma=False)
```

time: 568 us -> 263 us (0.46)
  blocking collectives: 254 us -> 0 us
  waiting for transfers between devices: 249 us -> 165 us
  starting transfers between devices: 15.3 us -> 43.7 us
  matrix products: 27.6 us -> 39.7 us
  other arithmetic: 13.7 us -> 7.35 us
    all_to_all x2 -> x0, blocking collectives: 254 us -> none  [the longest x1 127 us: body(): lax.all_to_all(backward_send, 'expert', split_axis=0, concat_axis=0, tile...]
    all_to_all x2 -> x0, waiting for transfers between devices: 231 us -> none  [the longest x1 116 us: body(): lax.all_to_all(forward_part, 'expert', split_axis=0, concat_axis=0, tiled...]
    ppermute x0 -> x28, waiting for transfers between devices: none -> 152 us  [the longest x12 95.4 us: to_plane(): return lax.ppermute(value, 'expert', pairs)]
    ppermute x0 -> x28, starting transfers between devices: none -> 38.9 us  [the longest x12 22.9 us: to_plane(): return lax.ppermute(value, 'expert', pairs)]
    dot_general x9 -> x17, matrix products: 27.6 us -> 39.7 us  [the longest x2 8.46 us: body(): jnp.dot(hidden[s], down_chips[s], preferred_element_type=F32)]
    all_to_all x2 -> x0, starting transfers between devices: 10.4 us -> none  [the longest x1 5.27 us: body(): lax.all_to_all(forward_part, 'expert', split_axis=0, concat_axis=0, tiled...]
    reduce_sum x2 -> x0, other arithmetic: 6.84 us -> none  [merge_holders(): jnp.sum(grouped, axis=1).astype(jnp.bfloat16)]
  transfers between devices with their start and end apart: 4 -> 30, of which waited for: 3 -> 17; matrix products, arithmetic and copies ran while one was open for 2% -> 15% of each run, Pallas kernels for 0% -> 0%
where the time goes in v1:
time: 263 us; the launch traced here: 259 us
  waiting for transfers between devices  165 us (63%)
  starting transfers between devices  43.7 us (17%)
  matrix products  39.7 us (15%)
  other arithmetic  7.35 us (3%)
    ppermute x12, waiting for transfers between devices, to_plane(): return lax.ppermute(value, 'expert', pairs)  95.4 us
    ppermute x11, waiting for transfers between devices, to_chip(): return lax.ppermute(value, 'expert', pairs)  56.7 us
    ppermute x12, starting transfers between devices, to_plane(): return lax.ppermute(value, 'expert', pairs)  22.9 us
    ppermute x11, starting transfers between devices, to_chip(): return lax.ppermute(value, 'expert', pairs)  14.8 us
    ppermute x2, waiting for transfers between devices, shifted(): return lax.ppermute(value, axis, pairs)  12.4 us
    dot_general x2, matrix products, body(): jnp.dot(hidden[s], down_chips[s], preferred_element_type=F32)  8.46 us
    dot_general x2, matrix products, body(): lax.dot_general(grad_up, up_chip, ROWS_BY_ROWS, preferred_element_type=F32)  5.83 us
    dot_general x2, matrix products, body(): lax.dot_general(grad_gate, gate_chip, ROWS_BY_ROWS, preferred_element_typ...  5.71 us
  transfers between devices with their start and end apart: 30, of which 17 were waited for; matrix products, arithmetic and copies ran while one was open for 15% of the time, Pallas kernels for 0%

profile of v1, /device:TPU:8, one launch (start us, length us, event | category | flops | bytes accessed | tf_op | source)
XLA Modules:
  0.0 259.2 jit_solution(4684016566492292499)
XLA Ops:
  0.6 3.5 %collective-permute-start = (bf16[1,128,3584]{2,1,0:T(8,128)(2,1)}, bf16[1,128,3584]{2,1,0:T(8,128)(2,1)S(1)}, u32[]{:S(2)}, u32[]{:S(2)}) collective-permute-start(bf16[1,128,3584]{2,1,0:T(8,128)(2,1)} %param.15), channel_id=1, source_target_pairs={{0,16},{1,17},{2,18},{3,19},{4,20},{5,21},{6,22},{7,23},{8,24},{9,... | collective-permute-start | bytes 2752520 | tf_op jit(solution)/shard_map/ppermute | solution.py:17
  4.7 1.5 collective-permute-start.12
  6.2 0.7 fusion.67
  6.9 0.7 fusion.66
  8.5 0.8 select_reduce_fusion.1
  9.3 0.8 select_reduce_fusion
  10.2 0.7 fusion.76
  10.8 0.7 fusion.79
  11.6 12.4 %collective-permute-done = bf16[1,128,3584]{2,1,0:T(8,128)(2,1)S(1)} collective-permute-done((bf16[1,128,3584]{2,1,0:T(8,128)(2,1)}, bf16[1,128,3584]{2,1,0:T(8,128)(2,1)S(1)}, u32[]{:S(2)}, u32[]{:S(2)}) %collective-permute-start) | collective-permute-done | bytes 917536 | tf_op jit(solution)/shard_map/ppermute | solution.py:17
  24.0 1.7 convolution_convert_fusion.1
  25.7 1.0 fusion.108
  26.7 1.5 collective-permute-start.7
  28.2 1.6 collective-permute-start.1
  29.8 1.3 convolution_convert_fusion.2
  31.0 0.6 multiply_reduce_fusion.1
  32.4 21.9 %collective-permute-done.7 = bf16[48,3584]{1,0:T(8,128)(2,1)S(1)} collective-permute-done((bf16[48,3584]{1,0:T(8,128)(2,1)S(1)}, bf16[48,3584]{1,0:T(8,128)(2,1)S(1)}, u32[]{:S(2)}, u32[]{:S(2)}) %collective-permute-start.7) | collective-permute-done | bytes 344096 | tf_op jit(solution)/shard_map/ppermute | solution.py:64
  54.3 2.6 collective-permute-start.2
  56.9 1.5 collective-permute-start.8
  58.4 12.8 %collective-permute-done.2 = bf16[48,3584]{1,0:T(8,128)(2,1)S(1)} collective-permute-done((bf16[48,3584]{1,0:T(8,128)(2,1)}, bf16[48,3584]{1,0:T(8,128)(2,1)S(1)}, u32[]{:S(2)}, u32[]{:S(2)}) %collective-permute-start.2) | collective-permute-done | bytes 344096 | tf_op jit(solution)/shard_map/ppermute | solution.py:60
  71.2 1.2 collective-permute-start.3
  72.4 1.5 collective-permute-start.9
  73.9 7.4 %collective-permute-done.3 = bf16[48,3584]{1,0:T(8,128)(2,1)S(1)} collective-permute-done((bf16[48,3584]{1,0:T(8,128)(2,1)}, bf16[48,3584]{1,0:T(8,128)(2,1)S(1)}, u32[]{:S(2)}, u32[]{:S(2)}) %collective-permute-start.3) | collective-permute-done | bytes 344096 | tf_op jit(solution)/shard_map/ppermute | solution.py:60
  81.4 1.6 collective-permute-start.10
  83.0 8.9 %collective-permute-done.10 = bf16[48,3584]{1,0:T(8,128)(2,1)S(1)} collective-permute-done((bf16[48,3584]{1,0:T(8,128)(2,1)S(1)}, bf16[48,3584]{1,0:T(8,128)(2,1)S(1)}, u32[]{:S(2)}, u32[]{:S(2)}) %collective-permute-start.10) | collective-permute-done | bytes 344096 | tf_op jit(solution)/shard_map/ppermute | solution.py:64
  91.9 1.3 collective-permute-start.17
  93.8 2.4 fusion.104
  96.2 2.4 multiply_convert_fusion
  98.6 1.6 collective-permute-start.11
  100.2 3.3 %fusion.51 = f32[192,512]{1,0:T(8,128)} fusion(bf16[48,3584]{1,0:T(8,128)(2,1)S(1)} %collective-permute-done.3, bf16[48,3584]{1,0:T(8,128)(2,1)S(1)} %collective-permute-done.2, bf16[48,3584]{1,0:T(8,128)(2,1)} %collective-permute-done.1, bf16[48,3584]{1,0:T(8,128)(2,1)S(1)} %get-tuple-element.25, bf16[3584,256]{1,0:T(8,128)(2,1)} %collective-permute-done.4, ...), kind=kOutput, calls=%fused_computation.91 | convolution fusion | flops 717488128 | bytes 5439488 | tf_op jit(solution)/shard_map/dot_general | solution.py:119
  103.7 1.9 collective-permute-done.11
  105.6 2.5 fusion.111
  108.1 6.0 %fusion = bf16[192,3584]{1,0:T(8,128)(2,1)S(1)} fusion(f32[192,3584]{1,0:T(8,128)} %fusion.111, bf16[256,3584]{1,0:T(8,128)(2,1)} %collective-permute-done.6, bf16[256,3584]{1,0:T(8,128)(2,1)} %bitcast.37, f32[192,512]{1,0:T(8,128)} %fusion.51, bf16[48,3584]{1,0:T(8,128)(2,1)} %copy-done.18, bf16[48,3584]{1,0:T(8,128)(2,1)S(1)} %copy-done.17, ...), kind=kOutput, calls=%fused_computation.3 | convolution fusion | flops 1431437312 | bytes 13238272 | tf_op jit(solution)/shard_map/dot_general | solution.py:128
  114.3 2.6 %collective-permute-start.14 = (bf16[48,3584]{1,0:T(8,128)(2,1)S(1)}, bf16[48,3584]{1,0:T(8,128)(2,1)S(1)}, u32[]{:S(2)}, u32[]{:S(2)}) collective-permute-start(bf16[48,3584]{1,0:T(8,128)(2,1)S(1)} %get-tuple-element.21), channel_id=1, source_target_pairs={{0,12},{1,13},{2,14},{3,15},{4,0},{5,1},{6,2},{7,3},{8,4},{9,5},{1... | collective-permute-start | bytes 1032200 | tf_op jit(solution)/shard_map/ppermute | solution.py:60
  116.9 2.6 collective-permute-start.15
  119.5 2.8 %collective-permute-start.16 = (bf16[48,3584]{1,0:T(8,128)(2,1)S(1)}, bf16[48,3584]{1,0:T(8,128)(2,1)S(1)}, u32[]{:S(2)}, u32[]{:S(2)}) collective-permute-start(bf16[48,3584]{1,0:T(8,128)(2,1)S(1)} %get-tuple-element.19), channel_id=1, source_target_pairs={{0,4},{1,5},{2,6},{3,7},{4,8},{5,9},{6,10},{7,11},{8,12},{9,13},{1... | collective-permute-start | bytes 1032200 | tf_op jit(solution)/shard_map/ppermute | solution.py:60
  122.9 3.2 %collective-permute-done.14 = bf16[48,3584]{1,0:T(8,128)(2,1)S(1)} collective-permute-done((bf16[48,3584]{1,0:T(8,128)(2,1)S(1)}, bf16[48,3584]{1,0:T(8,128)(2,1)S(1)}, u32[]{:S(2)}, u32[]{:S(2)}) %collective-permute-start.14) | collective-permute-done | bytes 344096 | tf_op jit(solution)/shard_map/ppermute | solution.py:60
  126.1 16.1 %collective-permute-done.15 = bf16[48,3584]{1,0:T(8,128)(2,1)S(1)} collective-permute-done((bf16[48,3584]{1,0:T(8,128)(2,1)S(1)}, bf16[48,3584]{1,0:T(8,128)(2,1)S(1)}, u32[]{:S(2)}, u32[]{:S(2)}) %collective-permute-start.15) | collective-permute-done | bytes 344096 | tf_op jit(solution)/shard_map/ppermute | solution.py:60
  142.2 6.4 %collective-permute-done.16 = bf16[48,3584]{1,0:T(8,128)(2,1)S(1)} collective-permute-done((bf16[48,3584]{1,0:T(8,128)(2,1)S(1)}, bf16[48,3584]{1,0:T(8,128)(2,1)S(1)}, u32[]{:S(2)}, u32[]{:S(2)}) %collective-permute-start.16) | collective-permute-done | bytes 344096 | tf_op jit(solution)/shard_map/ppermute | solution.py:60
  148.6 2.1 fusion.5
  150.6 0.6 convolution_convert_fusion
  151.4 2.5 collective-permute-start.18
  153.9 1.5 collective-permute-start.20
  155.5 21.6 %collective-permute-done.18 = bf16[48,3584]{1,0:T(8,128)(2,1)S(1)} collective-permute-done((bf16[48,3584]{1,0:T(8,128)(2,1)S(1)}, bf16[48,3584]{1,0:T(8,128)(2,1)S(1)}, u32[]{:S(2)}, u32[]{:S(2)}) %collective-permute-start.18) | collective-permute-done | bytes 344096 | tf_op jit(solution)/shard_map/ppermute | solution.py:60
  177.2 5.5 %collective-permute-done.19 = bf16[48,3584]{1,0:T(8,128)(2,1)S(1)} collective-permute-done((bf16[48,3584]{1,0:T(8,128)(2,1)S(1)}, bf16[48,3584]{1,0:T(8,128)(2,1)S(1)}, u32[]{:S(2)}, u32[]{:S(2)}) %collective-permute-start.19) | collective-permute-done | bytes 344096 | tf_op jit(solution)/shard_map/ppermute | solution.py:60
  182.7 1.3 convolution_convert_fusion.4
  184.0 1.6 collective-permute-start.22
  185.6 2.8 %fusion.4 = f32[192,512]{1,0:T(8,128)S(1)} fusion(bf16[256,3584]{1,0:T(8,128)(2,1)} %collective-permute-done.6, bf16[256,3584]{1,0:T(8,128)(2,1)S(1)} %bitcast.38, bf16[48,3584]{1,0:T(8,128)(2,1)S(1)} %collective-permute-done.20, bf16[48,3584]{1,0:T(8,128)(2,1)S(1)} %collective-permute-done.19, bf16[48,3584]{1,0:T(8,128)(2,1)S(1)} %collective-permute-done.18, ...), kind=kOutput, calls=%fused_computation.16 | convolution fusion | flops 717488128 | bytes 5439488 | tf_op jit(solution)/shard_map/dot_general | solution.py:134
  188.4 2.9 %fusion.58 = f32[192,3584]{1,0:T(8,128)S(1)} fusion(f32[192,512]{1,0:T(8,128)S(1)} %fusion.4, bf16[384,256]{1,0:T(8,128)(2,1)S(1)} %get-tuple-element.29, bf16[384,256]{1,0:T(8,128)(2,1)S(1)} %get-tuple-element.27, bf16[3584,256]{1,0:T(8,128)(2,1)} %collective-permute-done.5, bf16[3584,256]{1,0:T(8,128)(2,1)S(1)} %bitcast.42), kind=kOutput, calls=%fused_computation.95 | convolution fusion | flops 712966144 | bytes 7208960 | tf_op jit(solution)/shard_map/dot_general | solution.py:146
  191.3 3.0 %fusion.52 = f32[192,3584]{1,0:T(8,128)S(1)} fusion(bf16[192,512]{1,0:T(8,128)(2,1)S(1)} %collective-permute-done.22, bf16[384,256]{1,0:T(8,128)(2,1)S(1)} %get-tuple-element.27, bf16[384,256]{1,0:T(8,128)(2,1)S(1)} %get-tuple-element.29, bf16[3584,256]{1,0:T(8,128)(2,1)} %collective-permute-done.5, bf16[3584,256]{1,0:T(8,128)(2,1)S(1)} %bitcast.43), kind=kOutput, calls=%fused_computation.92 | convolution fusion | flops 713064448 | bytes 7012352 | tf_op jit(solution)/shard_map/dot_general | solution.py:146
  194.3 2.9 %fusion.1 = bf16[192,3584]{1,0:T(8,128)(2,1)S(1)} fusion(f32[192,3584]{1,0:T(8,128)S(1)} %fusion.52, bf16[192,512]{1,0:T(8,128)(2,1)S(1)} %collective-permute-done.22, bf16[384,256]{1,0:T(8,128)(2,1)S(1)} %get-tuple-element.26, bf16[384,256]{1,0:T(8,128)(2,1)S(1)} %get-tuple-element.28, bf16[384,256]{1,0:T(8,128)(2,1)S(1)} %get-tuple-element.27, ...), kind=kOutput, calls=%fused_computation.4 | convolution fusion | flops 715227136 | bytes 8781824 | tf_op jit(solution)/shard_map/dot_general | solution.py:145
  197.3 0.6 collective-permute-start.23
  197.9 1.5 collective-permute-start.24
  199.9 1.5 collective-permute-start.28
  201.4 2.8 %convolution_add_fusion.1 = f32[192,3584]{1,0:T(8,128)S(1)} fusion(f32[192,3584]{1,0:T(8,128)S(1)} %fusion.58, f32[192,512]{1,0:T(8,128)S(1)} %fusion.4, bf16[384,256]{1,0:T(8,128)(2,1)S(1)} %get-tuple-element.28, bf16[384,256]{1,0:T(8,128)(2,1)S(1)} %get-tuple-element.26, bf16[384,256]{1,0:T(8,128)(2,1)S(1)} %get-tuple-element.29, ...), kind=kOutput, calls=%fused_computation.1 | convolution fusion | flops 714440704 | bytes 10354688 | tf_op jit(solution)/shard_map/dot_general | solution.py:145
  204.3 4.1 %collective-permute-done.23 = bf16[48,3584]{1,0:T(8,128)(2,1)S(1)} collective-permute-done((bf16[48,3584]{1,0:T(8,128)(2,1)S(1)}, bf16[48,3584]{1,0:T(8,128)(2,1)S(1)}, u32[]{:S(2)}, u32[]{:S(2)}) %collective-permute-start.23) | collective-permute-done | bytes 344096 | tf_op jit(solution)/shard_map/ppermute | solution.py:64
  208.3 7.4 %collective-permute-done.24 = bf16[48,3584]{1,0:T(8,128)(2,1)S(1)} collective-permute-done((bf16[48,3584]{1,0:T(8,128)(2,1)S(1)}, bf16[48,3584]{1,0:T(8,128)(2,1)S(1)}, u32[]{:S(2)}, u32[]{:S(2)}) %collective-permute-start.24) | collective-permute-done | bytes 344096 | tf_op jit(solution)/shard_map/ppermute | solution.py:64
  215.7 7.4 %collective-permute-done.26 = bf16[48,3584]{1,0:T(8,128)(2,1)S(1)} collective-permute-done((bf16[48,3584]{1,0:T(8,128)(2,1)S(1)}, bf16[48,3584]{1,0:T(8,128)(2,1)S(1)}, u32[]{:S(2)}, u32[]{:S(2)}) %collective-permute-start.26) | collective-permute-done | bytes 344096 | tf_op jit(solution)/shard_map/ppermute | solution.py:64
  223.1 5.2 %collective-permute-done.28 = bf16[48,3584]{1,0:T(8,128)(2,1)S(1)} collective-permute-done((bf16[48,3584]{1,0:T(8,128)(2,1)S(1)}, bf16[48,3584]{1,0:T(8,128)(2,1)S(1)}, u32[]{:S(2)}, u32[]{:S(2)}) %collective-permute-start.28) | collective-permute-done | bytes 344096 | tf_op jit(solution)/shard_map/ppermute | solution.py:64
  228.6 2.5 collective-permute-start.27
  231.1 2.8 %collective-permute-start.29 = (bf16[48,3584]{1,0:T(8,128)(2,1)S(1)}, bf16[48,3584]{1,0:T(8,128)(2,1)S(1)}, u32[]{:S(2)}, u32[]{:S(2)}) collective-permute-start(bf16[48,3584]{1,0:T(8,128)(2,1)S(1)} %get-tuple-element.7), channel_id=1, source_target_pairs={{0,4},{1,5},{2,6},{3,7},{4,8},{5,9},{6,10},{7,11},{8,12},{9,13},{1... | collective-permute-start | bytes 1032200 | tf_op jit(solution)/shard_map/ppermute | solution.py:60
  234.0 1.4 fusion.22
  235.3 19.0 %collective-permute-done.25 = bf16[48,3584]{1,0:T(8,128)(2,1)S(1)} collective-permute-done((bf16[48,3584]{1,0:T(8,128)(2,1)S(1)}, bf16[48,3584]{1,0:T(8,128)(2,1)S(1)}, u32[]{:S(2)}, u32[]{:S(2)}) %collective-permute-start.25) | collective-permute-done | bytes 344096 | tf_op jit(solution)/shard_map/ppermute | solution.py:60
  254.4 3.5 %collective-permute-done.29 = bf16[48,3584]{1,0:T(8,128)(2,1)S(1)} collective-permute-done((bf16[48,3584]{1,0:T(8,128)(2,1)S(1)}, bf16[48,3584]{1,0:T(8,128)(2,1)S(1)}, u32[]{:S(2)}, u32[]{:S(2)}) %collective-permute-start.29) | collective-permute-done | bytes 344096 | tf_op jit(solution)/shard_map/ppermute | solution.py:60
  257.8 1.4 fusion.3
  (86 shorter events, 4.3 us)
Async XLA Ops:
  0.6 23.3 %collective-permute-start = (bf16[1,128,3584]{2,1,0:T(8,128)(2,1)}, bf16[1,128,3584]{2,1,0:T(8,128)(2,1)S(1)}, u32[]{:S(2)}, u32[]{:S(2)}) collective-permute-start(bf16[1,128,3584]{2,1,0:T(8,128)(2,1)} %param.15), channel_id=1, source_target_pairs={{0,16},{1,17},{2,18},{3,19},{4,20},{5,21},{6,22},{7,23},{8,24},{9,... | collective-permute-start | bytes 2752520 | tf_op jit(solution)/shard_map/ppermute | solution.py:17
  4.1 89.2 %collective-permute-start.4 = (bf16[3584,256]{1,0:T(8,128)(2,1)}, bf16[3584,256]{1,0:T(8,128)(2,1)}, u32[]{:S(2)}, u32[]{:S(2)}) collective-permute-start(bf16[3584,256]{1,0:T(8,128)(2,1)} %bitcast.44), channel_id=1, source_target_pairs={{0,1},{1,0},{2,3},{3,2},{4,5},{5,4},{6,7},{7,6},{8,9},{9,8},{10,11... | collective-permute-start | bytes 5505032 | tf_op jit(solution)/shard_map/ppermute | solution.py:67
  4.2 92.0 %collective-permute-start.5 = (bf16[3584,256]{1,0:T(8,128)(2,1)}, bf16[3584,256]{1,0:T(8,128)(2,1)}, u32[]{:S(2)}, u32[]{:S(2)}) collective-permute-start(bf16[3584,256]{1,0:T(8,128)(2,1)} %bitcast.39), channel_id=1, source_target_pairs={{0,1},{1,0},{2,3},{3,2},{4,5},{5,4},{6,7},{7,6},{8,9},{9,8},{10,11... | collective-permute-start | bytes 5505032 | tf_op jit(solution)/shard_map/ppermute | solution.py:67
  4.7 88.4 %collective-permute-start.12 = (bf16[256,3584]{1,0:T(8,128)(2,1)}, bf16[256,3584]{1,0:T(8,128)(2,1)S(1)}, u32[]{:S(2)}, u32[]{:S(2)}) collective-permute-start(bf16[256,3584]{1,0:T(8,128)(2,1)} %bitcast.35), channel_id=1, source_target_pairs={{0,2},{1,3},{2,0},{3,1},{4,6},{5,7},{6,4},{7,5},{8,10},{9,11},{10,... | collective-permute-start | bytes 5505032 | tf_op jit(solution)/shard_map/ppermute | solution.py:64
  25.7 4.1 %copy-start.12 = (bf16[1,768,256]{2,1,0:T(8,128)(2,1)S(1)}, bf16[1,768,256]{2,1,0:T(8,128)(2,1)}, u32[]{:S(2)}) copy-start(bf16[1,768,256]{2,1,0:T(8,128)(2,1)} %param.23) | copy-start | bytes 1179652
  25.7 4.1 %copy-start.14 = (bf16[1,768,256]{2,1,0:T(8,128)(2,1)S(1)}, bf16[1,768,256]{2,1,0:T(8,128)(2,1)}, u32[]{:S(2)}) copy-start(bf16[1,768,256]{2,1,0:T(8,128)(2,1)} %param.22) | copy-start | bytes 1179652
  26.7 4.3 %copy-start.3 = (f32[1,3584]{1,0:T(1,128)S(1)}, f32[1,3584]{1,0:T(1,128)}, u32[]{:S(2)}) copy-start(f32[1,3584]{1,0:T(1,128)} %param.27) | copy-start | bytes 43012
  26.7 27.6 %collective-permute-start.7 = (bf16[48,3584]{1,0:T(8,128)(2,1)S(1)}, bf16[48,3584]{1,0:T(8,128)(2,1)S(1)}, u32[]{:S(2)}, u32[]{:S(2)}) collective-permute-start(bf16[48,3584]{1,0:T(8,128)(2,1)S(1)} %get-tuple-element.25), channel_id=1, source_target_pairs={{0,2},{1,3},{2,0},{3,1},{4,6},{5,7},{6,4},{7,5},{8,10},{9,11},{10,... | collective-permute-start | bytes 1032200 | tf_op jit(solution)/shard_map/ppermute | solution.py:64
  28.2 28.7 %collective-permute-start.1 = (bf16[48,3584]{1,0:T(8,128)(2,1)}, bf16[48,3584]{1,0:T(8,128)(2,1)}, u32[]{:S(2)}, u32[]{:S(2)}) collective-permute-start(bf16[48,3584]{1,0:T(8,128)(2,1)} %get-tuple-element.24), channel_id=1, source_target_pairs={{0,4},{1,5},{2,6},{3,7},{4,8},{5,9},{6,10},{7,11},{8,12},{9,13},{1... | collective-permute-start | bytes 1032200 | tf_op jit(solution)/shard_map/ppermute | solution.py:60
  32.4 61.4 %copy-start.9 = (bf16[1,3584,256]{2,1,0:T(8,128)(2,1)S(1)}, bf16[1,3584,256]{2,1,0:T(8,128)(2,1)}, u32[]{:S(2)}) copy-start(bf16[1,3584,256]{2,1,0:T(8,128)(2,1)} %param.24) | copy-start | bytes 5505028
  54.3 16.9 %collective-permute-start.2 = (bf16[48,3584]{1,0:T(8,128)(2,1)}, bf16[48,3584]{1,0:T(8,128)(2,1)S(1)}, u32[]{:S(2)}, u32[]{:S(2)}) collective-permute-start(bf16[48,3584]{1,0:T(8,128)(2,1)} %get-tuple-element.23), channel_id=1, source_target_pairs={{0,8},{1,9},{2,10},{3,11},{4,12},{5,13},{6,14},{7,15},{8,0},{9,1},... | collective-permute-start | bytes 1032200 | tf_op jit(solution)/shard_map/ppermute | solution.py:60
  56.9 15.6 %collective-permute-start.8 = (bf16[48,3584]{1,0:T(8,128)(2,1)}, bf16[48,3584]{1,0:T(8,128)(2,1)S(1)}, u32[]{:S(2)}, u32[]{:S(2)}) collective-permute-start(bf16[48,3584]{1,0:T(8,128)(2,1)} %collective-permute-done.1), channel_id=1, source_target_pairs={{0,2},{1,3},{2,0},{3,1},{4,6},{5,7},{6,4},{7,5},{8,10},{9,11},{10,... | collective-permute-start | bytes 1032200 | tf_op jit(solution)/shard_map/ppermute | solution.py:64
  71.2 29.0 %copy-start.16 = (bf16[48,3584]{1,0:T(8,128)(2,1)}, bf16[48,3584]{1,0:T(8,128)(2,1)S(1)}, u32[]{:S(2)}) copy-start(bf16[48,3584]{1,0:T(8,128)(2,1)S(1)} %collective-permute-done.2) | copy-start | bytes 1032196
  71.2 10.2 %collective-permute-start.3 = (bf16[48,3584]{1,0:T(8,128)(2,1)}, bf16[48,3584]{1,0:T(8,128)(2,1)S(1)}, u32[]{:S(2)}, u32[]{:S(2)}) collective-permute-start(bf16[48,3584]{1,0:T(8,128)(2,1)} %get-tuple-element.22), channel_id=1, source_target_pairs={{0,12},{1,13},{2,14},{3,15},{4,0},{5,1},{6,2},{7,3},{8,4},{9,5},{1... | collective-permute-start | bytes 1032200 | tf_op jit(solution)/shard_map/ppermute | solution.py:60
  72.4 9.0 %collective-permute-start.9 = (bf16[48,3584]{1,0:T(8,128)(2,1)S(1)}, bf16[48,3584]{1,0:T(8,128)(2,1)S(1)}, u32[]{:S(2)}, u32[]{:S(2)}) collective-permute-start(bf16[48,3584]{1,0:T(8,128)(2,1)S(1)} %collective-permute-done.2), channel_id=1, source_target_pairs={{0,2},{1,3},{2,0},{3,1},{4,6},{5,7},{6,4},{7,5},{8,10},{9,11},{10,... | collective-permute-start | bytes 1032200 | tf_op jit(solution)/shard_map/ppermute | solution.py:64
  81.4 18.8 %copy-start.18 = (bf16[48,3584]{1,0:T(8,128)(2,1)}, bf16[48,3584]{1,0:T(8,128)(2,1)S(1)}, u32[]{:S(2)}) copy-start(bf16[48,3584]{1,0:T(8,128)(2,1)S(1)} %collective-permute-done.3) | copy-start | bytes 1032196
  81.4 26.8 %collective-permute-start.6 = (bf16[256,3584]{1,0:T(8,128)(2,1)}, bf16[256,3584]{1,0:T(8,128)(2,1)}, u32[]{:S(2)}, u32[]{:S(2)}) collective-permute-start(bf16[256,3584]{1,0:T(8,128)(2,1)} %bitcast.36), channel_id=1, source_target_pairs={{0,1},{1,0},{2,3},{3,2},{4,5},{5,4},{6,7},{7,6},{8,9},{9,8},{10,11... | collective-permute-start | bytes 5505032 | tf_op jit(solution)/shard_map/ppermute | solution.py:67
  81.4 10.5 %collective-permute-start.10 = (bf16[48,3584]{1,0:T(8,128)(2,1)S(1)}, bf16[48,3584]{1,0:T(8,128)(2,1)S(1)}, u32[]{:S(2)}, u32[]{:S(2)}) collective-permute-start(bf16[48,3584]{1,0:T(8,128)(2,1)S(1)} %collective-permute-done.3), channel_id=1, source_target_pairs={{0,2},{1,3},{2,0},{3,1},{4,6},{5,7},{6,4},{7,5},{8,10},{9,11},{10,... | collective-permute-start | bytes 1032200 | tf_op jit(solution)/shard_map/ppermute | solution.py:64
  91.9 31.1 %collective-permute-start.17 = (bf16[1,128,3584]{2,1,0:T(8,128)(2,1)}, bf16[1,128,3584]{2,1,0:T(8,128)(2,1)}, u32[]{:S(2)}, u32[]{:S(2)}) collective-permute-start(bf16[1,128,3584]{2,1,0:T(8,128)(2,1)} %param.19), channel_id=1, source_target_pairs={{16,0},{17,1},{18,2},{19,3},{20,4},{21,5},{22,6},{23,7},{24,8},{25... | collective-permute-start | bytes 2752520 | tf_op jit(solution)/shard_map/ppermute | solution.py:17
  93.2 10.4 %collective-permute-start.13 = (bf16[256,3584]{1,0:T(8,128)(2,1)S(1)}, bf16[256,3584]{1,0:T(8,128)(2,1)S(1)}, u32[]{:S(2)}, u32[]{:S(2)}) collective-permute-start(bf16[256,3584]{1,0:T(8,128)(2,1)S(1)} %collective-permute-done.12), channel_id=1, source_target_pairs={{0,1},{1,0},{2,3},{3,2},{4,5},{5,4},{6,7},{7,6},{8,9},{9,8},{10,11... | collective-permute-start | bytes 5505032 | tf_op jit(solution)/shard_map/ppermute | solution.py:67
  93.3 3.0 %copy-start.7 = (bf16[1,3584,256]{2,1,0:T(8,128)(2,1)S(1)}, bf16[1,3584,256]{2,1,0:T(8,128)(2,1)}, u32[]{:S(2)}) copy-start(bf16[1,3584,256]{2,1,0:T(8,128)(2,1)} %param.25) | copy-start | bytes 5505028
  93.3 62.2 %collective-permute-start.21 = (bf16[384,512]{1,0:T(8,128)(2,1)}, bf16[384,512]{1,0:T(8,128)(2,1)S(1)}, u32[]{:S(2)}, u32[]{:S(2)}) collective-permute-start(bf16[384,512]{1,0:T(8,128)(2,1)} %convolution_convert_fusion.2), channel_id=1, source_target_pairs={{0,1},{1,0},{2,3},{3,2},{4,5},{5,4},{6,7},{7,6},{8,9},{9,8},{10,11... | collective-permute-start | bytes 1179656 | tf_op jit(solution)/shard_map/ppermute | solution.py:67
  98.6 7.0 %collective-permute-start.11 = (bf16[192,512]{1,0:T(8,128)(2,1)S(1)}, bf16[192,512]{1,0:T(8,128)(2,1)S(1)}, u32[]{:S(2)}, u32[]{:S(2)}) collective-permute-start(bf16[192,512]{1,0:T(8,128)(2,1)S(1)} %multiply_convert_fusion), channel_id=1, source_target_pairs={{0,2},{1,3},{2,0},{3,1},{4,6},{5,7},{6,4},{7,5},{8,10},{9,11},{10,... | collective-permute-start | bytes 589832 | tf_op jit(solution)/shard_map/ppermute | solution.py:64
  103.7 4.4 %copy-start = (bf16[512,3584]{1,0:T(8,128)(2,1)}, bf16[512,3584]{1,0:T(8,128)(2,1)S(1)}, u32[]{:S(2)}) copy-start(bf16[512,3584]{1,0:T(8,128)(2,1)S(1)} %constant_dynamic-update-slice_fusion.4) | copy-start | bytes 11010052
  103.7 4.4 %copy-start.17 = (bf16[48,3584]{1,0:T(8,128)(2,1)S(1)}, bf16[48,3584]{1,0:T(8,128)(2,1)}, u32[]{:S(2)}) copy-start(bf16[48,3584]{1,0:T(8,128)(2,1)} %copy-done.16) | copy-start | bytes 1032196
  114.1 8.3 %copy-start.13 = (bf16[1,768,256]{2,1,0:T(8,128)(2,1)S(1)}, bf16[1,768,256]{2,1,0:T(8,128)(2,1)}, u32[]{:S(2)}) copy-start(bf16[1,768,256]{2,1,0:T(8,128)(2,1)} %param.23) | copy-start | bytes 1179652
  114.1 8.3 %copy-start.15 = (bf16[1,768,256]{2,1,0:T(8,128)(2,1)S(1)}, bf16[1,768,256]{2,1,0:T(8,128)(2,1)}, u32[]{:S(2)}) copy-start(bf16[1,768,256]{2,1,0:T(8,128)(2,1)} %param.22) | copy-start | bytes 1179652
  114.3 34.3 %copy-start.11 = (bf16[128,3584]{1,0:T(8,128)(2,1)S(1)}, bf16[128,3584]{1,0:T(8,128)(2,1)}, u32[]{:S(2)}) copy-start(bf16[128,3584]{1,0:T(8,128)(2,1)} %param.18) | copy-start | bytes 2752516
  114.3 34.3 %copy-start.19 = (f32[1,128]{1,0:T(1,128)S(1)}, f32[1,128]{1,0:T(1,128)}, u32[]{:S(2)}) copy-start(f32[1,128]{1,0:T(1,128)} %param.17) | copy-start | bytes 1540
  114.3 11.8 %collective-permute-start.14 = (bf16[48,3584]{1,0:T(8,128)(2,1)S(1)}, bf16[48,3584]{1,0:T(8,128)(2,1)S(1)}, u32[]{:S(2)}, u32[]{:S(2)}) collective-permute-start(bf16[48,3584]{1,0:T(8,128)(2,1)S(1)} %get-tuple-element.21), channel_id=1, source_target_pairs={{0,12},{1,13},{2,14},{3,15},{4,0},{5,1},{6,2},{7,3},{8,4},{9,5},{1... | collective-permute-start | bytes 1032200 | tf_op jit(solution)/shard_map/ppermute | solution.py:60
  116.9 25.2 %collective-permute-start.15 = (bf16[48,3584]{1,0:T(8,128)(2,1)S(1)}, bf16[48,3584]{1,0:T(8,128)(2,1)S(1)}, u32[]{:S(2)}, u32[]{:S(2)}) collective-permute-start(bf16[48,3584]{1,0:T(8,128)(2,1)S(1)} %get-tuple-element.20), channel_id=1, source_target_pairs={{0,8},{1,9},{2,10},{3,11},{4,12},{5,13},{6,14},{7,15},{8,0},{9,1},... | collective-permute-start | bytes 1032200 | tf_op jit(solution)/shard_map/ppermute | solution.py:60
  119.5 29.1 %collective-permute-start.16 = (bf16[48,3584]{1,0:T(8,128)(2,1)S(1)}, bf16[48,3584]{1,0:T(8,128)(2,1)S(1)}, u32[]{:S(2)}, u32[]{:S(2)}) collective-permute-start(bf16[48,3584]{1,0:T(8,128)(2,1)S(1)} %get-tuple-element.19), channel_id=1, source_target_pairs={{0,4},{1,5},{2,6},{3,7},{4,8},{5,9},{6,10},{7,11},{8,12},{9,13},{1... | collective-permute-start | bytes 1032200 | tf_op jit(solution)/shard_map/ppermute | solution.py:60
  148.6 2.1 copy-start.4
  150.6 83.4 %copy-start.5 = (f32[128]{0:T(128)}, f32[128]{0:T(128)S(1)}, u32[]{:S(2)}) copy-start(f32[128]{0:T(128)S(1)} %get-tuple-element.4) | copy-start | bytes 1540
  151.3 31.4 %copy-start.1 = (bf16[512,3584]{1,0:T(8,128)(2,1)S(1)}, bf16[512,3584]{1,0:T(8,128)(2,1)}, u32[]{:S(2)}) copy-start(bf16[512,3584]{1,0:T(8,128)(2,1)} %copy-done) | copy-start | bytes 11010052
  151.4 25.8 %collective-permute-start.18 = (bf16[48,3584]{1,0:T(8,128)(2,1)S(1)}, bf16[48,3584]{1,0:T(8,128)(2,1)S(1)}, u32[]{:S(2)}, u32[]{:S(2)}) collective-permute-start(bf16[48,3584]{1,0:T(8,128)(2,1)S(1)} %get-tuple-element.17), channel_id=1, source_target_pairs={{0,4},{1,5},{2,6},{3,7},{4,8},{5,9},{6,10},{7,11},{8,12},{9,13},{1... | collective-permute-start | bytes 1032200 | tf_op jit(solution)/shard_map/ppermute | solution.py:60
  153.9 28.7 %collective-permute-start.19 = (bf16[48,3584]{1,0:T(8,128)(2,1)S(1)}, bf16[48,3584]{1,0:T(8,128)(2,1)S(1)}, u32[]{:S(2)}, u32[]{:S(2)}) collective-permute-start(bf16[48,3584]{1,0:T(8,128)(2,1)S(1)} %get-tuple-element.16), channel_id=1, source_target_pairs={{0,8},{1,9},{2,10},{3,11},{4,12},{5,13},{6,14},{7,15},{8,0},{9,1},... | collective-permute-start | bytes 1032200 | tf_op jit(solution)/shard_map/ppermute | solution.py:60
  153.9 28.7 %collective-permute-start.20 = (bf16[48,3584]{1,0:T(8,128)(2,1)S(1)}, bf16[48,3584]{1,0:T(8,128)(2,1)S(1)}, u32[]{:S(2)}, u32[]{:S(2)}) collective-permute-start(bf16[48,3584]{1,0:T(8,128)(2,1)S(1)} %get-tuple-element.15), channel_id=1, source_target_pairs={{0,12},{1,13},{2,14},{3,15},{4,0},{5,1},{6,2},{7,3},{8,4},{9,5},{1... | collective-permute-start | bytes 1032200 | tf_op jit(solution)/shard_map/ppermute | solution.py:60
  182.7 2.9 %copy-start.6 = (bf16[1,256,3584]{2,1,0:T(8,128)(2,1)S(1)}, bf16[1,256,3584]{2,1,0:T(8,128)(2,1)}, u32[]{:S(2)}) copy-start(bf16[1,256,3584]{2,1,0:T(8,128)(2,1)} %param.26) | copy-start | bytes 5505028
  184.0 4.4 %copy-start.8 = (bf16[1,3584,256]{2,1,0:T(8,128)(2,1)S(1)}, bf16[1,3584,256]{2,1,0:T(8,128)(2,1)}, u32[]{:S(2)}) copy-start(bf16[1,3584,256]{2,1,0:T(8,128)(2,1)} %param.25) | copy-start | bytes 5505028
  184.0 7.3 %collective-permute-start.22 = (bf16[192,512]{1,0:T(8,128)(2,1)S(1)}, bf16[192,512]{1,0:T(8,128)(2,1)S(1)}, u32[]{:S(2)}, u32[]{:S(2)}) collective-permute-start(bf16[192,512]{1,0:T(8,128)(2,1)S(1)} %convolution_convert_fusion.4), channel_id=1, source_target_pairs={{0,2},{1,3},{2,0},{3,1},{4,6},{5,7},{6,4},{7,5},{8,10},{9,11},{10,... | collective-permute-start | bytes 589832 | tf_op jit(solution)/shard_map/ppermute | solution.py:64
  191.3 3.0 %copy-start.10 = (bf16[1,3584,256]{2,1,0:T(8,128)(2,1)S(1)}, bf16[1,3584,256]{2,1,0:T(8,128)(2,1)}, u32[]{:S(2)}) copy-start(bf16[1,3584,256]{2,1,0:T(8,128)(2,1)} %param.24) | copy-start | bytes 5505028
  197.3 11.1 %collective-permute-start.23 = (bf16[48,3584]{1,0:T(8,128)(2,1)S(1)}, bf16[48,3584]{1,0:T(8,128)(2,1)S(1)}, u32[]{:S(2)}, u32[]{:S(2)}) collective-permute-start(bf16[48,3584]{1,0:T(8,128)(2,1)S(1)} %get-tuple-element.10), channel_id=1, source_target_pairs={{0,2},{1,3},{2,0},{3,1},{4,6},{5,7},{6,4},{7,5},{8,10},{9,11},{10,... | collective-permute-start | bytes 1032200 | tf_op jit(solution)/shard_map/ppermute | solution.py:64
  197.9 17.9 %collective-permute-start.24 = (bf16[48,3584]{1,0:T(8,128)(2,1)S(1)}, bf16[48,3584]{1,0:T(8,128)(2,1)S(1)}, u32[]{:S(2)}, u32[]{:S(2)}) collective-permute-start(bf16[48,3584]{1,0:T(8,128)(2,1)S(1)} %get-tuple-element.13), channel_id=1, source_target_pairs={{0,2},{1,3},{2,0},{3,1},{4,6},{5,7},{6,4},{7,5},{8,10},{9,11},{10,... | collective-permute-start | bytes 1032200 | tf_op jit(solution)/shard_map/ppermute | solution.py:64
  199.4 23.7 %collective-permute-start.26 = (bf16[48,3584]{1,0:T(8,128)(2,1)S(1)}, bf16[48,3584]{1,0:T(8,128)(2,1)S(1)}, u32[]{:S(2)}, u32[]{:S(2)}) collective-permute-start(bf16[48,3584]{1,0:T(8,128)(2,1)S(1)} %get-tuple-element.12), channel_id=1, source_target_pairs={{0,2},{1,3},{2,0},{3,1},{4,6},{5,7},{6,4},{7,5},{8,10},{9,11},{10,... | collective-permute-start | bytes 1032200 | tf_op jit(solution)/shard_map/ppermute | solution.py:64
  199.9 28.4 %collective-permute-start.28 = (bf16[48,3584]{1,0:T(8,128)(2,1)S(1)}, bf16[48,3584]{1,0:T(8,128)(2,1)S(1)}, u32[]{:S(2)}, u32[]{:S(2)}) collective-permute-start(bf16[48,3584]{1,0:T(8,128)(2,1)S(1)} %get-tuple-element.11), channel_id=1, source_target_pairs={{0,2},{1,3},{2,0},{3,1},{4,6},{5,7},{6,4},{7,5},{8,10},{9,11},{10,... | collective-permute-start | bytes 1032200 | tf_op jit(solution)/shard_map/ppermute | solution.py:64
  204.2 29.7 %copy-start.2 = (bf16[128,3584]{1,0:T(8,128)(2,1)S(1)}, bf16[128,3584]{1,0:T(8,128)(2,1)}, u32[]{:S(2)}) copy-start(bf16[128,3584]{1,0:T(8,128)(2,1)} %param.14) | copy-start | bytes 2752516
  228.6 25.8 %collective-permute-start.25 = (bf16[48,3584]{1,0:T(8,128)(2,1)S(1)}, bf16[48,3584]{1,0:T(8,128)(2,1)S(1)}, u32[]{:S(2)}, u32[]{:S(2)}) collective-permute-start(bf16[48,3584]{1,0:T(8,128)(2,1)S(1)} %get-tuple-element.9), channel_id=1, source_target_pairs={{0,12},{1,13},{2,14},{3,15},{4,0},{5,1},{6,2},{7,3},{8,4},{9,5},{1... | collective-permute-start | bytes 1032200 | tf_op jit(solution)/shard_map/ppermute | solution.py:60
  228.6 25.7 %collective-permute-start.27 = (bf16[48,3584]{1,0:T(8,128)(2,1)S(1)}, bf16[48,3584]{1,0:T(8,128)(2,1)S(1)}, u32[]{:S(2)}, u32[]{:S(2)}) collective-permute-start(bf16[48,3584]{1,0:T(8,128)(2,1)S(1)} %get-tuple-element.8), channel_id=1, source_target_pairs={{0,8},{1,9},{2,10},{3,11},{4,12},{5,13},{6,14},{7,15},{8,0},{9,1},... | collective-permute-start | bytes 1032200 | tf_op jit(solution)/shard_map/ppermute | solution.py:60
  231.1 26.7 %collective-permute-start.29 = (bf16[48,3584]{1,0:T(8,128)(2,1)S(1)}, bf16[48,3584]{1,0:T(8,128)(2,1)S(1)}, u32[]{:S(2)}, u32[]{:S(2)}) collective-permute-start(bf16[48,3584]{1,0:T(8,128)(2,1)S(1)} %get-tuple-element.7), channel_id=1, source_target_pairs={{0,4},{1,5},{2,6},{3,7},{4,8},{5,9},{6,10},{7,11},{8,12},{9,13},{1... | collective-permute-start | bytes 1032200 | tf_op jit(solution)/shard_map/ppermute | solution.py:60

commit v2 on v1

v2 whole, which is shorter than its diff:
```python
import functools

import jax
import jax.numpy as jnp
from jax import lax
from jax.experimental import pallas as pl
from jax.experimental.pallas import tpu as pltpu
from jax.sharding import PartitionSpec as P

H = 1024
CORES = 2
EARLY = (2,)
PARTS = 1
OPT = {'split_rows': True, 'pack': False, 'z_depth': 2, 'x_depth': 2, 'm_core': True, 'rows_got': False, 'rows_d1': False, 'rows_core': True, 'x_wd': False, 'd3_after': 1, 'one_group': False, 'gh_after': 0, 'mine_first': False, 'theirs_after': 0, 'wd_first': False, 'rs_order': [2, 1, 3, 0], 'h2_after': 0, 'limit_add': 24, 'limit_mm': 16, 'limit_rows': 24, 'limit_first': 56, 'br_dep': False, 'cost': {'grad_rows': 10000000000, 'add_rows': 2000000000, 'forward_end': 50000000000}}
COST = 5000000000
BF16 = jnp.bfloat16
F32 = jnp.float32
COLS = 896
ROWS_BY_ROWS = (((1,), (1,)), ((), ()))
SMEM = pl.BlockSpec(memory_space=pltpu.SMEM)
VMEM = pl.BlockSpec(memory_space=pltpu.VMEM)


def after(value, *deps):
    return lax.optimization_barrier((value, *deps))[0] if deps else value


def dot(a, b):
    return jnp.dot(a, b, preferred_element_type=F32)


def dot_rows(a, b):
    return lax.dot_general(a, b, ROWS_BY_ROWS, preferred_element_type=F32)


def shape(rows, cols, dtype=BF16):
    return jax.ShapeDtypeStruct((rows, cols), dtype)


def shifted(value, axis, by):
    devices = lax.axis_size(axis)
    pairs = [(i, i + by) for i in range(devices) if 0 <= i + by < devices]
    return lax.ppermute(value, axis, pairs)


def call(kernel, name, outs, args, grid=None, in_specs=None, out_specs=None, scratch=(), limit=24):
    extra = {} if grid is None else {"grid": grid}
    return pl.pallas_call(
        kernel,
        out_shape=outs,
        in_specs=in_specs,
        out_specs=out_specs if out_specs is not None else [VMEM] * len(outs),
        scratch_shapes=list(scratch),
        name=name,
        cost_estimate=pl.CostEstimate(flops=OPT["cost"].get(name, COST), bytes_accessed=100000, transcendentals=0),
        compiler_params=pltpu.CompilerParams(vmem_limit_bytes=limit << 20),
        **extra,
    )(*args)


def stacked(values):
    if values[0].shape[0] % 16 == 0:
        return jnp.concatenate(values, axis=0)
    return jnp.concatenate([value.astype(F32) for value in values], axis=0).astype(BF16)


def slot_of(ids, plane, experts, capacity, axis):
    tokens = ids.shape[axis]
    wide = (tokens, 128) if axis == 0 else (max(8, experts), tokens)
    chosen = jnp.where(ids == lax.broadcasted_iota(jnp.int32, wide, 1 - axis), 1.0, 0.0)
    row = lax.broadcasted_iota(jnp.int32, (tokens, tokens), 0)
    col = lax.broadcasted_iota(jnp.int32, (tokens, tokens), 1)
    if axis == 0:
        earlier = dot(jnp.where(col < row, 1.0, 0.0).astype(BF16), chosen.astype(BF16))
    else:
        earlier = dot(chosen.astype(BF16), jnp.where(row < col, 1.0, 0.0).astype(BF16))
    position = jnp.sum(chosen * earlier, axis=1 - axis, keepdims=True).astype(jnp.int32)
    ahead = ids - plane
    return jnp.where(ahead < 0, ahead + experts, ahead) * capacity + position


def slots_by_tokens(ids_row, plane, experts, capacity):
    wide = (experts * capacity, ids_row.shape[1])
    slot = slot_of(ids_row, plane, experts, capacity, 1)
    return jnp.where(lax.broadcasted_iota(jnp.int32, wide, 0) == slot, 1.0, 0.0).astype(BF16)


def tokens_by_slots(ids_row, plane, experts, capacity):
    wide = (ids_row.shape[1], experts * capacity)
    slot = slot_of(column(ids_row), plane, experts, capacity, 0)
    return jnp.where(lax.broadcasted_iota(jnp.int32, wide, 1) == slot, 1.0, 0.0).astype(BF16)


def column(row):
    size = row.shape[1]
    diagonal = lax.broadcasted_iota(jnp.int32, (size, size), 0) == lax.broadcasted_iota(jnp.int32, (size, size), 1)
    return jnp.sum(jnp.where(diagonal, row, jnp.zeros_like(row)), axis=1, keepdims=True)


def unit_of(steer):
    return steer / jnp.sqrt(jnp.sum(steer * steer, axis=1, keepdims=True) + 1e-06)


def pieces(width):
    return [slice(at, at + COLS) for at in range(0, width, COLS)]


def gather_into(layout, tokens_at, blocks, capacity, width):
    for cols in pieces(width):
        rows = dot(layout, tokens_at(cols))
        for k, ref in blocks.items():
            ref[:, cols] = rows[k * capacity : (k + 1) * capacity].astype(BF16)


def sent_at(token_refs, weight_ref, steer_ref):
    unit = unit_of(steer_ref[...])

    def wide(cols):
        return jnp.concatenate([ref[:, cols].astype(F32) for ref in token_refs], axis=0)

    along = 0.0
    for cols in pieces(unit.shape[1]):
        along = along + jnp.sum(wide(cols) * unit[:, cols], axis=1, keepdims=True)
    weight = column(weight_ref[...])
    return lambda cols: (weight * (wide(cols) - along * unit[:, cols])).astype(BF16)


def pack_kernel(experts, capacity, at_ref, gate, up, saved_gate, saved_up, packed, kept):
    plane, chip, core = at_ref[0], at_ref[3], at_ref[4]
    size, width = gate.shape[1], gate.shape[0]
    count = CORES * experts * capacity
    packed[:width, :] = gate[...]
    packed[width : 2 * width, :] = up[...]
    wide = (capacity, saved_gate.shape[0])
    ahead = lax.broadcasted_iota(jnp.int32, wide, 1) - lax.broadcasted_iota(jnp.int32, wide, 0)

    def rows_of(core_index):
        chosen = []
        for chip_index in (chip, 1 - chip):
            for k in range(experts):
                source = jnp.where(plane < k, plane - k + experts, plane - k)
                start = ((source * 2 + chip_index) * CORES + core_index) * capacity
                chosen.append(jnp.where(ahead == start, 1.0, 0.0))
        return jnp.concatenate(chosen, axis=0).astype(BF16)

    chosen = rows_of(core)
    kept[:, :size] = dot(chosen, saved_gate[...]).astype(BF16)
    kept[:, size:] = dot(chosen, saved_up[...]).astype(BF16)
    chosen = rows_of(1 - core)
    start = packed.shape[0] - 2 * count
    packed[start : start + count, :] = dot(chosen, saved_gate[...]).astype(BF16)
    packed[start + count :, :] = dot(chosen, saved_up[...]).astype(BF16)


def saved_kernel(experts, capacity, at_ref, saved_gate, saved_up, kept, leaving):
    plane, chip, core = at_ref[0], at_ref[3], at_ref[4]
    size = saved_gate.shape[1]
    wide = (capacity, saved_gate.shape[0])
    ahead = lax.broadcasted_iota(jnp.int32, wide, 1) - lax.broadcasted_iota(jnp.int32, wide, 0)
    for ref, core_index in ((kept, core), (leaving, 1 - core)):
        chosen = []
        for chip_index in (chip, 1 - chip):
            for k in range(experts):
                source = jnp.where(plane < k, plane - k + experts, plane - k)
                start = ((source * 2 + chip_index) * CORES + core_index) * capacity
                chosen.append(jnp.where(ahead == start, 1.0, 0.0))
        chosen = jnp.concatenate(chosen, axis=0).astype(BF16)
        ref[:, :size] = dot(chosen, saved_gate[...]).astype(BF16)
        ref[:, size:] = dot(chosen, saved_up[...]).astype(BF16)


def first_kernel(ks, experts, capacity, at_ref, f_ids, b_ids, f_tok, b_tok, b_weight, steer, *out):
    blocks, width = dict(zip(ks, out)), f_tok.shape[1]

    @pl.when(at_ref[1] == 1)
    def _():
        layout = slots_by_tokens(b_ids[...], at_ref[0], experts, capacity)
        gather_into(layout, sent_at([b_tok], b_weight, steer), blocks, capacity, width)

    @pl.when(at_ref[1] == 0)
    def _():
        layout = slots_by_tokens(f_ids[...], at_ref[0], experts, capacity)
        gather_into(layout, lambda cols: f_tok[:, cols], blocks, capacity, width)


def rows_kernel(cuts, early, experts, capacity, at_ref, f_ids, b_ids, f_near, b_near, weight, steer, *refs):
    far, out = refs[: 2 * cuts], refs[2 * cuts :]
    width = f_near.shape[1]
    forward, backward = dict(enumerate(out[:experts])), dict(enumerate(out[experts:]))
    layout = slots_by_tokens(f_ids[...], at_ref[0], experts, capacity)

    @pl.when(at_ref[2] == 1)
    def _():
        gather_into(layout, lambda cols: f_near[:, cols], forward, capacity, width)

    @pl.when(at_ref[2] == 0)
    def _():
        gather_into(layout, lambda cols: jnp.concatenate([ref[:, cols] for ref in far[:cuts]], axis=0), forward, capacity, width)

    layout = slots_by_tokens(b_ids[...], at_ref[0], experts, capacity)

    @pl.when(at_ref[1] == 1)
    def _():
        others = {k: ref for k, ref in backward.items() if k not in early}
        gather_into(layout, sent_at([b_near], weight, steer), others, capacity, width)
        for k in early:
            backward[k][...] = forward[k][...]

    @pl.when(at_ref[1] == 0)
    def _():
        gather_into(layout, sent_at(far[cuts:], weight, steer), backward, capacity, width)


def forward_rows_kernel(experts, capacity, at_ref, ids, near, far, *out):
    blocks, width = dict(enumerate(out)), near.shape[1]
    layout = slots_by_tokens(ids[...], at_ref[0], experts, capacity)
    pl.when(at_ref[2] == 1)(lambda: gather_into(layout, lambda cols: near[:, cols], blocks, capacity, width))
    pl.when(at_ref[2] == 0)(lambda: gather_into(layout, lambda cols: far[:, cols], blocks, capacity, width))


def backward_rows_kernel(early, experts, capacity, at_ref, ids, near, weight, steer, far, *refs):
    swapped, out = refs[: len(early)], refs[len(early) :]
    blocks, width = dict(enumerate(out)), near.shape[1]
    layout = slots_by_tokens(ids[...], at_ref[0], experts, capacity)

    @pl.when(at_ref[1] == 1)
    def _():
        others = {k: ref for k, ref in blocks.items() if k not in early}
        gather_into(layout, sent_at([near], weight, steer), others, capacity, width)
        for k, ref in zip(early, swapped):
            blocks[k][...] = ref[...]

    @pl.when(at_ref[1] == 0)
    def _():
        gather_into(layout, sent_at([far], weight, steer), blocks, capacity, width)


def hidden_kernel(count, *refs):
    rows, weights = refs[: 2 * count], refs[2 * count : 2 * count + 4]
    own, other, x = refs[2 * count + 4 :]
    x[...] = stacked([ref[...] for ref in rows])
    half, size = own.shape[0], weights[0].shape[1]
    for j in range(CORES):
        value = jax.nn.silu(dot(x[...], weights[j][...])) * dot(x[...], weights[CORES + j][...])
        cols = slice(j * size, (j + 1) * size)
        own[:, cols], other[:, cols] = value[:half].astype(BF16), value[half:].astype(BF16)


def out_kernel(capacity, own, other, d0, d1, *refs):
    d2, d3, out = refs[:PARTS], refs[PARTS : 2 * PARTS], refs[2 * PARTS :]
    size = d0.shape[0]
    for cols in pieces(d0.shape[1]):
        rows = dot(own[:, :size], d0[:, cols]) + dot(own[:, size:], d1[:, cols])
        rows = rows + dot(other[:, :size], stacked([ref[:, cols] for ref in d2]))
        rows = rows + dot(other[:, size:], stacked([ref[:, cols] for ref in d3]))
        for i, ref in enumerate(out):
            ref[:, cols] = rows[i * capacity : (i + 1) * capacity].astype(BF16)


def grad_hidden_kernel(*refs):
    rows, downs, (own, other, x) = refs[: -5 - 2 * PARTS], refs[-5 - 2 * PARTS : -3], refs[-3:]
    x[...] = stacked([ref[...] for ref in rows])
    size = downs[0].shape[0]
    groups = (downs[2 : 2 + PARTS], downs[2 + PARTS :], downs[:1], downs[1:2])
    for j, group in enumerate(groups):
        grads = dot_rows(x[...], stacked([ref[...] for ref in group]))
        ref = other if j < 2 else own
        ref[:, (j % 2) * size : (j % 2 + 1) * size] = grads.astype(ref.dtype)


def grad_rows_kernel(capacity, got_count, side, grads, kept, *refs):
    got, (g0, g1, u0, u1) = refs[:got_count], refs[got_count : got_count + 4]
    out, (gate_grad, up_grad) = refs[got_count + 4 : -2], refs[-2:]
    size, height = g0.shape[1], grads.shape[0]
    here = slice(side * height, (side + 1) * height)
    theirs = (got[0][here, :size], got[0][here, size:]) if got_count == 1 else (got[0][...], got[1][...])
    saved = ((kept[here, :size], kept[here, size:]), theirs)
    for j, (g, u) in enumerate(saved):
        at = slice(j * size, (j + 1) * size)
        g, u = g.astype(F32), u.astype(F32)
        grad = grads[:, at].astype(F32)
        s = jax.nn.sigmoid(g)
        gate_grad[:, at] = (grad * u * s * (1.0 + g * (1.0 - s))).astype(BF16)
        up_grad[:, at] = (grad * g * s).astype(BF16)
    for cols in pieces(g0.shape[0]):
        rows = dot_rows(gate_grad[:, :size], g0[cols, :]) + dot_rows(gate_grad[:, size:], g1[cols, :])
        rows = rows + dot_rows(up_grad[:, :size], u0[cols, :]) + dot_rows(up_grad[:, size:], u1[cols, :])
        for i, ref in enumerate(out):
            ref[:, cols] = rows[i * capacity : (i + 1) * capacity].astype(ref.dtype)


def add_kernel(ours, theirs, out):
    out[...] = (ours[...] + theirs[...].astype(F32)).astype(BF16)


def forward_end_kernel(cuts, experts, capacity, at_ref, ids, near, weight, steer, *refs):
    far, back, (out, coefficient, mixed) = refs[:cuts], refs[cuts : cuts + experts], refs[cuts + experts :]
    layout = tokens_by_slots(ids[...], at_ref[0], experts, capacity)
    unit = unit_of(steer[...])
    along, scale = 0.0, column(weight[...])
    for cols in pieces(near.shape[1]):
        rows = scale * dot(layout, stacked([ref[:, cols] for ref in back]))
        mixed[:, cols] = rows
        along = along + jnp.sum(rows * unit[:, cols], axis=1, keepdims=True)
    size = along.shape[0]
    diagonal = lax.broadcasted_iota(jnp.int32, (size, size), 0) == lax.broadcasted_iota(jnp.int32, (size, size), 1)
    coefficient[...] = jnp.sum(jnp.where(diagonal, along, 0.0), axis=0, keepdims=True)

    def finish(*tokens):
        for cols in pieces(near.shape[1]):
            start = jnp.concatenate([ref[:, cols].astype(F32) for ref in tokens], axis=0)
            out[:, cols] = (start + mixed[:, cols] - along * unit[:, cols]).astype(BF16)

    pl.when(at_ref[2] == 1)(lambda: finish(near))
    pl.when(at_ref[2] == 0)(lambda: finish(*far))


def backward_end_kernel(cuts, experts, capacity, at_ref, ids, near, *refs):
    far, back, out = refs[:cuts], refs[cuts : cuts + experts], refs[cuts + experts]
    layout = tokens_by_slots(ids[...], at_ref[0], experts, capacity)

    def finish(*tokens):
        for cols in pieces(near.shape[1]):
            rows = dot(layout, stacked([ref[:, cols] for ref in back]))
            start = jnp.concatenate([ref[:, cols].astype(F32) for ref in tokens], axis=0)
            out[:, cols] = (start + rows).astype(BF16)

    pl.when(at_ref[1] == 1)(lambda: finish(near))
    pl.when(at_ref[1] == 0)(lambda: finish(*far))


def body(
    embedded,
    forward_held,
    forward_route,
    forward_weight,
    loss_cotangent,
    backward_held,
    backward_route,
    backward_weight,
    saved_gate,
    saved_up,
    gate_weight,
    up_weight,
    down_weight,
    steering,
):
    section_count = lax.axis_size("section")
    section_index = lax.axis_index("section")
    device_count = lax.axis_size("expert")
    device_index = lax.axis_index("expert")
    local_hidden = gate_weight.shape[2]
    holders = H // local_hidden
    experts = device_count // holders
    capacity = saved_gate.shape[1] // device_count
    rows = experts * capacity
    tokens, width = embedded.shape
    plane = device_index // holders
    chip = lax.rem(device_index, holders) // CORES
    core = lax.rem(device_index, CORES)
    first, last = section_index == 0, section_index == section_count - 1
    at = jnp.stack([plane, last.astype(jnp.int32), first.astype(jnp.int32), chip, core])
    early = [k for k in EARLY if k < experts]
    routed = [k for k in range(1, experts) if k not in early]

    def to_plane(value, by):
        pairs = [(i, (i + by * holders) % device_count) for i in range(device_count)]
        return lax.ppermute(value, "expert", pairs)

    def to_chip(value):
        pairs = [(i, i // holders * holders + (i + CORES) % holders) for i in range(device_count)]
        return lax.ppermute(value, "expert", pairs)

    def to_core(value):
        return lax.ppermute(value, "expert", [(i, i ^ 1) for i in range(device_count)])

    z_order, x_order = [], []

    def z_send(block, by, *deps):
        depth = OPT["z_depth"]
        out = to_plane(after(block, *z_order[-depth:][: len(z_order) >= depth], *deps), by)
        z_order.append(out)
        return out

    def x_send(block, *deps):
        depth = OPT["x_depth"]
        out = to_chip(after(block, *x_order[-depth:][: len(x_order) >= depth], *deps))
        x_order.append(out)
        return out

    def columns(height):
        return pl.BlockSpec((height, COLS), lambda i: (0, i))

    def whole(height, cols, index=0):
        return pl.BlockSpec((height, cols), lambda i: (index, 0))

    steps = width // COLS
    gate, up, down = gate_weight[0], up_weight[0], down_weight[0]
    f_ids, b_ids = forward_route[0].reshape(1, tokens), backward_route[0].reshape(1, tokens)
    f_weight, b_weight = forward_weight, backward_weight

    arriving = [shifted(forward_held, "section", 1)[0]]
    returning = [shifted(backward_held, "section", -1)[0]]
    d1 = to_core(down)
    part = local_hidden // PARTS
    d2 = []
    for p in range(PARTS):
        d2.append(to_chip(after(down, *d2[-1:])[p * part : (p + 1) * part]))
    if OPT["x_wd"]:
        x_order += d2
    core_first = () if OPT["pack"] else (to_core(gate), to_core(up))

    if section_count == 2:
        near_forward, near_backward = embedded, loss_cotangent
    else:
        near_forward = jnp.where(first, embedded, jnp.concatenate(arriving, axis=0))
        near_backward = jnp.where(last, loss_cotangent, jnp.concatenate(returning, axis=0))
    ones = call(
        functools.partial(first_kernel, early, experts, capacity),
        "first_rows",
        [shape(capacity, width)] * len(early),
        (at, f_ids, b_ids, near_forward, near_backward, b_weight, steering),
        in_specs=[SMEM] + [VMEM] * 6,
        limit=OPT["limit_first"],
    )
    got_one = {k: z_send(block, k, *(core_first if OPT["m_core"] else ())) for k, block in zip(early, ones)}

    def saved_rows(*deps):
        kept, leaving = call(
            functools.partial(saved_kernel, experts, capacity),
            "saved_rows",
            [shape(CORES * rows, 2 * local_hidden)] * 2,
            (at, after(saved_gate[0], *deps), saved_up[0]),
            in_specs=[SMEM] + [VMEM] * 2,
        )
        return kept, to_core(leaving)

    early_deps = list(got_one.values()) if OPT["rows_got"] else []
    if not OPT["pack"]:
        kept, got = saved_rows(*ones)
        if OPT["rows_core"]:
            early_deps += [got, *core_first]
    if OPT["rows_d1"]:
        early_deps.append(d1)
    if OPT["wd_first"]:
        early_deps.append(d2[0])
    ready = after(at, *early_deps)
    if OPT["split_rows"]:
        forward_rows = call(
            functools.partial(forward_rows_kernel, experts, capacity),
            "forward_rows",
            [shape(capacity, width)] * experts,
            (ready, f_ids, embedded, *arriving),
            in_specs=[SMEM] + [VMEM] * 3,
            limit=OPT["limit_rows"],
        )
        backward_rows = call(
            functools.partial(backward_rows_kernel, early, experts, capacity),
            "backward_rows",
            [shape(capacity, width)] * experts,
            (at, b_ids, loss_cotangent, b_weight, steering, *returning, *(forward_rows[k] for k in early)),
            in_specs=[SMEM] + [VMEM] * (5 + len(early)),
            limit=OPT["limit_rows"],
        )
    else:
        both = call(
            functools.partial(rows_kernel, 1, early, experts, capacity),
            "rows",
            [shape(capacity, width)] * (2 * experts),
            (ready, f_ids, b_ids, embedded, loss_cotangent, b_weight, steering, *arriving, *returning),
            in_specs=[SMEM] + [VMEM] * 8,
            limit=OPT["limit_rows"],
        )
        forward_rows, backward_rows = both[:experts], both[experts:]
    forward_got, backward_got = {0: forward_rows[0]}, {0: backward_rows[0]}
    for k in routed:
        forward_got[k] = z_send(forward_rows[k], k, *(backward_rows[:1] if OPT["br_dep"] else ()))
    across = {0: x_send(forward_got[0])}
    got_two = {k: z_send(backward_rows[k], k) for k in early}

    if OPT["pack"]:
        saved_block = pl.cdiv(2 * width, rows)
        packed, kept = call(
            functools.partial(pack_kernel, experts, capacity),
            "packed",
            [shape((saved_block + 2 * CORES) * rows, local_hidden), shape(CORES * rows, 2 * local_hidden)],
            (at, gate, up, saved_gate[0], after(saved_up[0], *forward_rows)),
            in_specs=[SMEM] + [VMEM] * 4,
            limit=40,
        )
        sibling = to_core(packed)
    anchors = [(), tuple(got_two.values()), tuple(forward_got[k] for k in routed), (across[0],)]
    d3 = [to_core(after(each, *anchors[OPT["d3_after"]])) for each in d2]

    for k in routed:
        across[k] = x_send(forward_got[k])
        backward_got[k] = z_send(backward_rows[k], k)
    for k in early:
        forward_got[k] = jnp.where(last, got_two[k], got_one[k])
        backward_got[k] = jnp.where(last, got_one[k], got_two[k])
        across[k] = x_send(forward_got[k])

    columns_of = (gate, core_first[0], up, core_first[1])
    saved_args = (kept, got)
    downs = (down, d1, *d2, *d3)

    def hidden_of(group, *deps):
        count = len(group)
        height = count * capacity
        return call(
            functools.partial(hidden_kernel, count),
            "hidden",
            [shape(height, 2 * local_hidden)] * 2,
            [after(forward_got[group[0]], *deps)]
            + [forward_got[k] for k in group[1:]]
            + [across[k] for k in group]
            + list(columns_of),
            limit=OPT["limit_mm"],
            in_specs=[VMEM] * (2 * count + 4),
            scratch=[pltpu.VMEM((2 * height, width), BF16)],
        )

    def out_of(group, own, other):
        height = len(group) * capacity
        return call(
            functools.partial(out_kernel, capacity),
            "expert_out",
            [shape(capacity, width)] * len(group),
            (own, other, *downs),
            limit=OPT["limit_mm"],
            in_specs=[VMEM] * (2 + len(downs)),
        )

    groups = [g for g in ([0] + routed, early) if g]
    if OPT["one_group"]:
        groups = [list(range(experts))]
    forward_back = {}
    marks = [()]
    for group in groups:
        own, other = hidden_of(group, *marks[min(OPT["h2_after"], len(marks) - 1)])
        marks.append((other,))
        blocks = out_of(group, own, x_send(other))
        marks.append((blocks[0],))
        for k, block in zip(group, blocks):
            forward_back[k] = block if k == 0 else z_send(block, -k)

    gh_after = marks[min(OPT["gh_after"], len(marks) - 1)]
    grads_own, grads_other = call(
        grad_hidden_kernel,
        "grad_hidden",
        [shape(rows, 2 * local_hidden, F32), shape(rows, 2 * local_hidden)],
        [after(backward_got[0], *gh_after)] + [backward_got[k] for k in range(1, experts)] + list(downs),
        limit=OPT["limit_mm"],
        in_specs=[VMEM] * (experts + len(downs)),
        scratch=[pltpu.VMEM((rows, width), BF16)],
    )
    grads_got = x_send(grads_other)

    def grad_rows(grads, side, outs):
        return call(
            functools.partial(grad_rows_kernel, capacity, len(saved_args) - 1, side),
            "grad_rows",
            outs,
            (grads, *saved_args, *columns_of),
            limit=OPT["limit_mm"],
            in_specs=[VMEM] * (6 + len(saved_args) - 1 + 0),
            scratch=[pltpu.VMEM((rows, 2 * local_hidden), BF16)] * 2,
        )

    mine = grad_rows(grads_own, 0, [shape(capacity, width, F32)] * experts)
    if OPT["mine_first"]:
        grads_got = after(grads_got, *mine)
    grads_got = after(grads_got, *marks[min(OPT["theirs_after"], len(marks) - 1)])
    theirs = grad_rows(grads_got, 1, [shape(capacity, width)] * experts)
    backward_back = {}
    ahead = [k for k in OPT["rs_order"] if k < experts]
    for k in ahead + [k for k in range(experts) if k not in ahead]:
        block = call(add_kernel, "add_rows", [shape(capacity, width)], (mine[k], x_send(theirs[k])), in_specs=[VMEM] * 2, limit=OPT["limit_add"])[0]
        backward_back[k] = block if k == 0 else z_send(block, -k)

    forward_out, coefficient = call(
        functools.partial(forward_end_kernel, len(arriving), experts, capacity),
        "forward_end",
        [shape(tokens, width), shape(1, tokens, F32)],
        (at, f_ids, embedded, f_weight, steering, *arriving, *(forward_back[k] for k in range(experts))),
        in_specs=[SMEM] + [VMEM] * (4 + len(arriving) + experts),
        scratch=[pltpu.VMEM((tokens, width), F32)],
    )
    backward_out = call(
        functools.partial(backward_end_kernel, len(arriving), experts, capacity),
        "backward_end",
        [shape(tokens, width)],
        (at, b_ids, loss_cotangent, *returning, *(backward_back[k] for k in range(experts))),
        in_specs=[SMEM] + [VMEM] * (2 + len(arriving) + experts),
    )[0]
    return (forward_out[None], coefficient, backward_out[None])


def solution(mesh):
    in_specs = (
        P("expert", None),
        P("section", "expert", None),
        P("section", "expert", None),
        P("section", "expert"),
        P("expert", None),
        P("section", "expert", None),
        P("section", "expert", None),
        P("section", "expert"),
        P("section", None, "expert"),
        P("section", None, "expert"),
        P("section", None, "expert"),
        P("section", None, "expert"),
        P("section", "expert", None),
        P("section", None),
    )
    out_specs = (P("section", "expert", None), P("section", "expert"), P("section", "expert", None))
    return jax.shard_map(body, mesh=mesh, in_specs=in_specs, out_specs=out_specs, check_vma=False)
```

time: 263 us -> 158 us (0.60)
  the two profiles are of different devices: /device:TPU:8 before, /device:TPU:0 now
where the time goes in v2:
time: 158 us
  waiting for transfers between devices  79.1 us (50%)
  starting transfers between devices  42.1 us (27%)
  Pallas kernels  35.3 us (22%)
    ppermute x12, waiting for transfers between devices, to_plane(): return lax.ppermute(value, 'expert', pairs)  41.9 us
    pallas_call x17, Pallas kernels, call(): pl.pallas_call(kernel, out_shape=outs, in_specs=in_specs, out_specs=out_s...  35.3 us
    ppermute x12, waiting for transfers between devices, to_chip(): return lax.ppermute(value, 'expert', pairs)  28.5 us
    ppermute x12, starting transfers between devices, to_plane(): return lax.ppermute(value, 'expert', pairs)  21.8 us
    ppermute x12, starting transfers between devices, to_chip(): return lax.ppermute(value, 'expert', pairs)  12.6 us
    ppermute x2, starting transfers between devices, shifted(): return lax.ppermute(value, axis, pairs)  7.06 us
    ppermute x2, waiting for transfers between devices, shifted(): return lax.ppermute(value, axis, pairs)  7.06 us
  transfers between devices with their start and end apart: 31, of which 11 were waited for; matrix products, arithmetic and copies ran while one was open for 0% of the time, Pallas kernels for 21%

profile of v2, /device:TPU:0, one launch (start us, length us, event | category | flops | bytes accessed | tf_op | source)
XLA Modules:
  0.0 158.2 jit_solution(16170969115649534272)
XLA Ops:
  0.6 0.5 collective-permute-start.2
  1.1 0.1 collective-permute-start.3
  1.2 5.8 %collective-permute-start = (bf16[1,128,3584]{2,1,0:T(8,128)(2,1)}, bf16[1,128,3584]{2,1,0:T(8,128)(2,1)}, u32[]{:S(2)}, u32[]{:S(2)}) collective-permute-start(bf16[1,128,3584]{2,1,0:T(8,128)(2,1)} %param.15), channel_id=1, source_target_pairs={{0,16},{1,17},{2,18},{3,19},{4,20},{5,21},{6,22},{7,23},{8,24},{9,... | collective-permute-start | bytes 2752520 | tf_op jit(solution)/shard_map/ppermute | solution.py:43
  7.0 1.3 collective-permute-start.13
  8.3 1.6 collective-permute-start.12
  9.9 0.6 stack.31.at_ref
  10.5 2.9 %first_rows.1 = bf16[48,3584]{1,0:T(8,128)(2,1)} custom-call(s32[5]{0:T(128)} %stack.31.at_ref, s32[1,128]{1,0:T(1,128)} %bitcast.35, s32[1,128]{1,0:T(1,128)} %bitcast.38, bf16[128,3584]{1,0:T(8,128)(2,1)} %near.6, bf16[128,3584]{1,0:T(8,128)(2,1)} %near.7, f32[1,128]{1,0:T(1,128)} %weight.2, f32[1,3584]{1,0:T(1,128)} %steer.5), custom_call_target="tpu_custom_call" | custom-call | flops 5000000000 | bytes 100000 | tf_op jit(solution)/shard_map/first_rows/pallas_call | solution.py:48
  13.4 0.0 copy-start.13
  13.4 0.0 copy-start.4
  13.4 0.0 copy-start.10
  13.5 1.3 saved_rows.1
  14.8 0.1 collective-permute-start.1
  14.9 1.7 %collective-permute-done.1.refs_0_ = bf16[384,512]{1,0:T(8,128)(2,1)S(1)} collective-permute-done((bf16[384,512]{1,0:T(8,128)(2,1)S(1)}, bf16[384,512]{1,0:T(8,128)(2,1)S(1)}, u32[]{:S(2)}, u32[]{:S(2)}) %collective-permute-start.1) | collective-permute-done | bytes 393248 | tf_op jit(solution)/shard_map/ppermute | solution.py:375
  16.6 2.6 %collective-permute-start.5 = (bf16[48,3584]{1,0:T(8,128)(2,1)S(1)}, bf16[48,3584]{1,0:T(8,128)(2,1)S(1)}, u32[]{:S(2)}, u32[]{:S(2)}) collective-permute-start(bf16[48,3584]{1,0:T(8,128)(2,1)S(1)} %copy-done.13), channel_id=1, source_target_pairs={{0,8},{1,9},{2,10},{3,11},{4,12},{5,13},{6,14},{7,15},{8,0},{9,1},... | collective-permute-start | bytes 1032200 | tf_op jit(solution)/shard_map/ppermute | solution.py:368
  19.2 7.1 %collective-permute-done = bf16[1,128,3584]{2,1,0:T(8,128)(2,1)} collective-permute-done((bf16[1,128,3584]{2,1,0:T(8,128)(2,1)}, bf16[1,128,3584]{2,1,0:T(8,128)(2,1)}, u32[]{:S(2)}, u32[]{:S(2)}) %collective-permute-start) | collective-permute-done | bytes 917536 | tf_op jit(solution)/shard_map/ppermute | solution.py:43
  26.2 0.0 copy-start.9
  26.3 0.0 copy-start.12
  26.3 1.9 %forward_rows.1 = (bf16[48,3584]{1,0:T(8,128)(2,1)S(1)}, bf16[48,3584]{1,0:T(8,128)(2,1)S(1)}, bf16[48,3584]{1,0:T(8,128)(2,1)S(1)}, bf16[48,3584]{1,0:T(8,128)(2,1)S(1)}) custom-call(s32[5]{0:T(128)S(1)} %copy-done, s32[1,128]{1,0:T(1,128)S(1)} %bitcast.36, bf16[128,3584]{1,0:T(8,128)(2,1)S(1)} %copy-done.4, bf16[128,3584]{1,0:T(8,128)(2,1)} %bitcast.6.far.refs_0_), custom_call_target="tpu_custom_call" | custom-call | flops 5000000000 | bytes 100000 | tf_op jit(solution)/shard_map/forward_rows/pallas_call | solution.py:48
  28.2 1.6 %collective-permute-start.4 = (bf16[48,3584]{1,0:T(8,128)(2,1)S(1)}, bf16[48,3584]{1,0:T(8,128)(2,1)S(1)}, u32[]{:S(2)}, u32[]{:S(2)}) collective-permute-start(bf16[48,3584]{1,0:T(8,128)(2,1)S(1)} %get-tuple-element.59), channel_id=1, source_target_pairs={{0,4},{1,5},{2,6},{3,7},{4,8},{5,9},{6,10},{7,11},{8,12},{9,13},{1... | collective-permute-start | bytes 1032200 | tf_op jit(solution)/shard_map/ppermute | solution.py:368
  29.8 1.5 collective-permute-start.7
  31.3 11.2 %collective-permute-done.5 = bf16[48,3584]{1,0:T(8,128)(2,1)S(1)} collective-permute-done((bf16[48,3584]{1,0:T(8,128)(2,1)S(1)}, bf16[48,3584]{1,0:T(8,128)(2,1)S(1)}, u32[]{:S(2)}, u32[]{:S(2)}) %collective-permute-start.5) | collective-permute-done | bytes 344096 | tf_op jit(solution)/shard_map/ppermute | solution.py:368
  42.6 0.0 copy-start.1
  42.6 0.0 copy-start.2
  42.6 1.6 %backward_rows.1 = (bf16[48,3584]{1,0:T(8,128)(2,1)S(1)}, bf16[48,3584]{1,0:T(8,128)(2,1)S(1)}, bf16[48,3584]{1,0:T(8,128)(2,1)S(1)}, bf16[48,3584]{1,0:T(8,128)(2,1)S(1)}) custom-call(s32[5]{0:T(128)S(1)} %copy-done, s32[1,128]{1,0:T(1,128)S(1)} %bitcast.39, bf16[128,3584]{1,0:T(8,128)(2,1)S(1)} %copy-done.5, f32[1,128]{1,0:T(1,128)S(1)} %copy-done.9, ...), custom_call_target="tpu_custom_call" | custom-call | flops 5000000000 | bytes 100000 | tf_op jit(solution)/shard_map/backward_rows/pallas_call | solution.py:48
  44.2 0.7 collective-permute-start.14
  45.0 12.7 %collective-permute-done.7.refs_3_ = bf16[48,3584]{1,0:T(8,128)(2,1)S(1)} collective-permute-done((bf16[48,3584]{1,0:T(8,128)(2,1)S(1)}, bf16[48,3584]{1,0:T(8,128)(2,1)S(1)}, u32[]{:S(2)}, u32[]{:S(2)}) %collective-permute-start.7) | collective-permute-done | bytes 344096 | tf_op jit(solution)/shard_map/ppermute | solution.py:372
  57.7 1.5 collective-permute-start.8
  59.2 0.5 collective-permute-start.9
  59.7 1.6 collective-permute-start.16
  61.3 10.6 %collective-permute-done.14 = bf16[48,3584]{1,0:T(8,128)(2,1)S(1)} collective-permute-done((bf16[48,3584]{1,0:T(8,128)(2,1)S(1)}, bf16[48,3584]{1,0:T(8,128)(2,1)S(1)}, u32[]{:S(2)}, u32[]{:S(2)}) %collective-permute-start.14) | collective-permute-done | bytes 344096 | tf_op jit(solution)/shard_map/ppermute | solution.py:368
  71.9 0.6 collective-permute-start.18
  72.5 1.4 collective-permute-done.9.refs_5_
  73.9 5.7 %collective-permute-start.21 = (bf16[48,3584]{1,0:T(8,128)(2,1)S(1)}, bf16[48,3584]{1,0:T(8,128)(2,1)S(1)}, u32[]{:S(2)}, u32[]{:S(2)}) collective-permute-start(bf16[48,3584]{1,0:T(8,128)(2,1)S(1)} %get-tuple-element.83), channel_id=1, source_target_pairs={{0,12},{1,13},{2,14},{3,15},{4,0},{5,1},{6,2},{7,3},{8,4},{9,5},{1... | collective-permute-start | bytes 1032200 | tf_op jit(solution)/shard_map/ppermute | solution.py:368
  79.6 4.4 %hidden.2 = (bf16[144,512]{1,0:T(8,128)(2,1)S(1)}, bf16[144,512]{1,0:T(8,128)(2,1)S(1)}) custom-call(bf16[48,3584]{1,0:T(8,128)(2,1)S(1)} %get-tuple-element.58.refs_0_, bf16[48,3584]{1,0:T(8,128)(2,1)S(1)} %collective-permute-done.4.refs_1_, bf16[48,3584]{1,0:T(8,128)(2,1)S(1)} %collective-permute-done.6.refs_2_, ...), custom_call_target="tpu_custom_call" | custom-call | flops 5000000000 | bytes 100000 | tf_op jit(solution)/shard_map/hidden/pallas_call | solution.py:48
  84.0 1.6 collective-permute-start.10
  85.6 3.3 %hidden.3 = (bf16[48,512]{1,0:T(8,128)(2,1)S(1)}, bf16[48,512]{1,0:T(8,128)(2,1)S(1)}) custom-call(bf16[48,3584]{1,0:T(8,128)(2,1)S(1)} %get-tuple-element.76.refs_0_, bf16[48,3584]{1,0:T(8,128)(2,1)S(1)} %collective-permute-done.18.refs_1_, bf16[3584,256]{1,0:T(8,128)(2,1)S(1)} %bitcast.18, ...), custom_call_target="tpu_custom_call" | custom-call | flops 5000000000 | bytes 100000 | tf_op jit(solution)/shard_map/hidden/pallas_call | solution.py:48
  88.9 0.6 collective-permute-start.19
  89.5 2.5 %grad_hidden.1 = (f32[192,512]{1,0:T(8,128)S(1)}, bf16[192,512]{1,0:T(8,128)(2,1)S(1)}) custom-call(bf16[48,3584]{1,0:T(8,128)(2,1)S(1)} %get-tuple-element.87.refs_0_, bf16[48,3584]{1,0:T(8,128)(2,1)S(1)} %collective-permute-done.16.refs_1_, bf16[48,3584]{1,0:T(8,128)(2,1)S(1)} %get-tuple-element.107.refs_2_, ...), custom_call_target="tpu_custom_call" | custom-call | flops 5000000000 | bytes 100000 | tf_op jit(solution)/shard_map/grad_hidden/pallas_call | solution.py:48
  92.1 1.6 collective-permute-start.23
  93.6 1.4 expert_out.2
  95.0 0.1 collective-permute-start.22
  95.1 3.8 %collective-permute-start.17 = (bf16[48,3584]{1,0:T(8,128)(2,1)S(1)}, bf16[48,3584]{1,0:T(8,128)(2,1)S(1)}, u32[]{:S(2)}, u32[]{:S(2)}) collective-permute-start(bf16[48,3584]{1,0:T(8,128)(2,1)S(1)} %get-tuple-element.75), channel_id=1, source_target_pairs={{0,12},{1,13},{2,14},{3,15},{4,0},{5,1},{6,2},{7,3},{8,4},{9,5},{1... | collective-permute-start | bytes 1032200 | tf_op jit(solution)/shard_map/ppermute | solution.py:368
  98.9 4.5 %grad_rows.2 = (f32[48,3584]{1,0:T(8,128)S(1)}, f32[48,3584]{1,0:T(8,128)S(1)}, f32[48,3584]{1,0:T(8,128)S(1)}, f32[48,3584]{1,0:T(8,128)S(1)}) custom-call(f32[192,512]{1,0:T(8,128)S(1)} %get-tuple-element.88.grads, bf16[384,512]{1,0:T(8,128)(2,1)S(1)} %get-tuple-element.89.kept, bf16[384,512]{1,0:T(8,128)(2,1)S(1)} %collective-permute-done.1.refs_0_, ...), custom_call_target="tpu_custom_call" | custom-call | flops 10000000000 | bytes 100000 | tf_op jit(solution)/shard_map/grad_rows/pallas_call | solution.py:48
  103.4 4.5 %grad_rows.3 = (bf16[48,3584]{1,0:T(8,128)(2,1)S(1)}, bf16[48,3584]{1,0:T(8,128)(2,1)S(1)}, bf16[48,3584]{1,0:T(8,128)(2,1)S(1)}, bf16[48,3584]{1,0:T(8,128)(2,1)S(1)}) custom-call(bf16[192,512]{1,0:T(8,128)(2,1)S(1)} %collective-permute-done.23.grads, bf16[384,512]{1,0:T(8,128)(2,1)S(1)} %get-tuple-element.89.kept, ...), custom_call_target="tpu_custom_call" | custom-call | flops 10000000000 | bytes 100000 | tf_op jit(solution)/shard_map/grad_rows/pallas_call | solution.py:48
  107.9 0.6 collective-permute-start.27
  108.5 1.5 collective-permute-start.24
  110.0 1.2 expert_out.3
  111.2 0.1 collective-permute-start.20
  111.3 7.6 %collective-permute-done.27.theirs = bf16[48,3584]{1,0:T(8,128)(2,1)S(1)} collective-permute-done((bf16[48,3584]{1,0:T(8,128)(2,1)S(1)}, bf16[48,3584]{1,0:T(8,128)(2,1)S(1)}, u32[]{:S(2)}, u32[]{:S(2)}) %collective-permute-start.27) | collective-permute-done | bytes 344096 | tf_op jit(solution)/shard_map/ppermute | solution.py:372
  119.0 0.5 collective-permute-start.29
  119.5 0.1 add_rows.6
  119.6 0.1 collective-permute-start.28
  119.6 6.7 %collective-permute-done.24.theirs = bf16[48,3584]{1,0:T(8,128)(2,1)S(1)} collective-permute-done((bf16[48,3584]{1,0:T(8,128)(2,1)S(1)}, bf16[48,3584]{1,0:T(8,128)(2,1)S(1)}, u32[]{:S(2)}, u32[]{:S(2)}) %collective-permute-start.24) | collective-permute-done | bytes 344096 | tf_op jit(solution)/shard_map/ppermute | solution.py:372
  126.3 0.5 collective-permute-start.25
  126.9 0.1 add_rows.5
  126.9 6.5 %collective-permute-done.20.refs_3_ = bf16[48,3584]{1,0:T(8,128)(2,1)S(1)} collective-permute-done((bf16[48,3584]{1,0:T(8,128)(2,1)S(1)}, bf16[48,3584]{1,0:T(8,128)(2,1)S(1)}, u32[]{:S(2)}, u32[]{:S(2)}) %collective-permute-start.20) | collective-permute-done | bytes 344096 | tf_op jit(solution)/shard_map/ppermute | solution.py:368
  133.5 0.8 collective-permute-start.26
  134.3 0.1 add_rows.7
  134.3 6.5 %collective-permute-done.28.refs_3_ = bf16[48,3584]{1,0:T(8,128)(2,1)S(1)} collective-permute-done((bf16[48,3584]{1,0:T(8,128)(2,1)S(1)}, bf16[48,3584]{1,0:T(8,128)(2,1)S(1)}, u32[]{:S(2)}, u32[]{:S(2)}) %collective-permute-start.28) | collective-permute-done | bytes 344096 | tf_op jit(solution)/shard_map/ppermute | solution.py:368
  140.9 4.7 %collective-permute-start.30 = (bf16[48,3584]{1,0:T(8,128)(2,1)S(1)}, bf16[48,3584]{1,0:T(8,128)(2,1)S(1)}, u32[]{:S(2)}, u32[]{:S(2)}) collective-permute-start(bf16[48,3584]{1,0:T(8,128)(2,1)S(1)} %add_rows.7), channel_id=1, source_target_pairs={{0,4},{1,5},{2,6},{3,7},{4,8},{5,9},{6,10},{7,11},{8,12},{9,13},{1... | collective-permute-start | bytes 1032200 | tf_op jit(solution)/shard_map/ppermute | solution.py:368
  145.6 3.2 %forward_end.1 = (bf16[128,3584]{1,0:T(8,128)(2,1)}, f32[1,128]{1,0:T(1,128)}) custom-call(s32[5]{0:T(128)S(1)} %copy-done, s32[1,128]{1,0:T(1,128)S(1)} %bitcast.37, bf16[128,3584]{1,0:T(8,128)(2,1)S(1)} %copy-done.4, f32[1,128]{1,0:T(1,128)S(1)} %copy-done.11, f32[1,3584]{1,0:T(1,128)S(1)} %copy-done.8, bf16[128,3584]{1,0:T(8,128)(2,1)} %bitcast.6.far.refs_0_, ...), custom_call_target="tpu_custom_call" | custom-call | flops 49999998976 | bytes 100000 | tf_op jit(solution)/shard_map/forward_end/pallas_call | solution.py:48
  148.9 0.1 add_rows.4.refs_1_
  149.0 7.0 %collective-permute-done.30.refs_4_ = bf16[48,3584]{1,0:T(8,128)(2,1)S(1)} collective-permute-done((bf16[48,3584]{1,0:T(8,128)(2,1)S(1)}, bf16[48,3584]{1,0:T(8,128)(2,1)S(1)}, u32[]{:S(2)}, u32[]{:S(2)}) %collective-permute-start.30) | collective-permute-done | bytes 344096 | tf_op jit(solution)/shard_map/ppermute | solution.py:368
  156.0 2.2 %backward_end.1 = bf16[128,3584]{1,0:T(8,128)(2,1)} custom-call(s32[5]{0:T(128)S(1)} %copy-done, s32[1,128]{1,0:T(1,128)S(1)} %bitcast.40, bf16[128,3584]{1,0:T(8,128)(2,1)S(1)} %copy-done.5, bf16[128,3584]{1,0:T(8,128)(2,1)S(1)} %bitcast.32, bf16[48,3584]{1,0:T(8,128)(2,1)S(1)} %add_rows.4.refs_1_, bf16[48,3584]{1,0:T(8,128)(2,1)S(1)} %collective-permute-done.26.refs_2_, ...), custom_call_target="tpu_custom_call" | custom-call | flops 5000000000 | bytes 100000 | tf_op jit(solution)/shard_map/backward_end/pallas_call | solution.py:48
  (45 shorter events, 0.2 us)
Async XLA Ops:
  0.6 14.2 %collective-permute-start.2 = (bf16[3584,256]{1,0:T(8,128)(2,1)}, bf16[3584,256]{1,0:T(8,128)(2,1)}, u32[]{:S(2)}, u32[]{:S(2)}) collective-permute-start(bf16[3584,256]{1,0:T(8,128)(2,1)} %bitcast.16), channel_id=1, source_target_pairs={{0,1},{1,0},{2,3},{3,2},{4,5},{5,4},{6,7},{7,6},{8,9},{9,8},{10,11... | collective-permute-start | bytes 5505032 | tf_op jit(solution)/shard_map/ppermute | solution.py:375
  1.1 13.7 %collective-permute-start.3 = (bf16[3584,256]{1,0:T(8,128)(2,1)}, bf16[3584,256]{1,0:T(8,128)(2,1)}, u32[]{:S(2)}, u32[]{:S(2)}) collective-permute-start(bf16[3584,256]{1,0:T(8,128)(2,1)} %bitcast.21), channel_id=1, source_target_pairs={{0,1},{1,0},{2,3},{3,2},{4,5},{5,4},{6,7},{7,6},{8,9},{9,8},{10,11... | collective-permute-start | bytes 5505032 | tf_op jit(solution)/shard_map/ppermute | solution.py:375
  1.2 25.0 %collective-permute-start = (bf16[1,128,3584]{2,1,0:T(8,128)(2,1)}, bf16[1,128,3584]{2,1,0:T(8,128)(2,1)}, u32[]{:S(2)}, u32[]{:S(2)}) collective-permute-start(bf16[1,128,3584]{2,1,0:T(8,128)(2,1)} %param.15), channel_id=1, source_target_pairs={{0,16},{1,17},{2,18},{3,19},{4,20},{5,21},{6,22},{7,23},{8,24},{9,... | collective-permute-start | bytes 2752520 | tf_op jit(solution)/shard_map/ppermute | solution.py:43
  7.0 35.6 %collective-permute-start.13 = (bf16[1,128,3584]{2,1,0:T(8,128)(2,1)}, bf16[1,128,3584]{2,1,0:T(8,128)(2,1)S(1)}, u32[]{:S(2)}, u32[]{:S(2)}) collective-permute-start(bf16[1,128,3584]{2,1,0:T(8,128)(2,1)} %param.19), channel_id=1, source_target_pairs={{16,0},{17,1},{18,2},{19,3},{20,4},{21,5},{22,6},{23,7},{24,8},{25... | collective-permute-start | bytes 2752520 | tf_op jit(solution)/shard_map/ppermute | solution.py:43
  8.3 51.4 %collective-permute-start.12 = (bf16[256,3584]{1,0:T(8,128)(2,1)}, bf16[256,3584]{1,0:T(8,128)(2,1)S(1)}, u32[]{:S(2)}, u32[]{:S(2)}) collective-permute-start(bf16[256,3584]{1,0:T(8,128)(2,1)} %bitcast.26), channel_id=1, source_target_pairs={{0,2},{1,3},{2,0},{3,1},{4,6},{5,7},{6,4},{7,5},{8,10},{9,11},{10,... | collective-permute-start | bytes 5505032 | tf_op jit(solution)/shard_map/ppermute | solution.py:372
  10.5 3.0 %copy-start = (s32[5]{0:T(128)S(1)}, s32[5]{0:T(128)}, u32[]{:S(2)}) copy-start(s32[5]{0:T(128)} %stack.31.at_ref) | copy-start | bytes 64
  10.5 3.0 %copy-start.6 = (bf16[1,768,256]{2,1,0:T(8,128)(2,1)S(1)}, bf16[1,768,256]{2,1,0:T(8,128)(2,1)}, u32[]{:S(2)}) copy-start(bf16[1,768,256]{2,1,0:T(8,128)(2,1)} %param.22) | copy-start | bytes 1179652
  10.5 3.0 %copy-start.7 = (bf16[1,768,256]{2,1,0:T(8,128)(2,1)S(1)}, bf16[1,768,256]{2,1,0:T(8,128)(2,1)}, u32[]{:S(2)}) copy-start(bf16[1,768,256]{2,1,0:T(8,128)(2,1)} %param.23) | copy-start | bytes 1179652
  13.4 3.2 %copy-start.13 = (bf16[48,3584]{1,0:T(8,128)(2,1)S(1)}, bf16[48,3584]{1,0:T(8,128)(2,1)}, u32[]{:S(2)}) copy-start(bf16[48,3584]{1,0:T(8,128)(2,1)} %first_rows.1) | copy-start | bytes 1032196
  13.4 12.8 %copy-start.4 = (bf16[128,3584]{1,0:T(8,128)(2,1)S(1)}, bf16[128,3584]{1,0:T(8,128)(2,1)}, u32[]{:S(2)}) copy-start(bf16[128,3584]{1,0:T(8,128)(2,1)} %near.6) | copy-start | bytes 2752516
  13.4 12.8 %copy-start.10 = (s32[1,128,1]{1,2,0:T(1,128)S(1)}, s32[1,128,1]{1,2,0:T(1,128)}, u32[]{:S(2)}) copy-start(s32[1,128,1]{1,2,0:T(1,128)} %param.16) | copy-start | bytes 1540
  14.8 1.8 %collective-permute-start.1 = (bf16[384,512]{1,0:T(8,128)(2,1)S(1)}, bf16[384,512]{1,0:T(8,128)(2,1)S(1)}, u32[]{:S(2)}, u32[]{:S(2)}) collective-permute-start(bf16[384,512]{1,0:T(8,128)(2,1)S(1)} %get-tuple-element.56), channel_id=1, source_target_pairs={{0,1},{1,0},{2,3},{3,2},{4,5},{5,4},{6,7},{7,6},{8,9},{9,8},{10,11... | collective-permute-start | bytes 1179656 | tf_op jit(solution)/shard_map/ppermute | solution.py:375
  16.6 26.0 %collective-permute-start.5 = (bf16[48,3584]{1,0:T(8,128)(2,1)S(1)}, bf16[48,3584]{1,0:T(8,128)(2,1)S(1)}, u32[]{:S(2)}, u32[]{:S(2)}) collective-permute-start(bf16[48,3584]{1,0:T(8,128)(2,1)S(1)} %copy-done.13), channel_id=1, source_target_pairs={{0,8},{1,9},{2,10},{3,11},{4,12},{5,13},{6,14},{7,15},{8,0},{9,1},... | collective-permute-start | bytes 1032200 | tf_op jit(solution)/shard_map/ppermute | solution.py:368
  26.2 16.3 %copy-start.5 = (bf16[128,3584]{1,0:T(8,128)(2,1)S(1)}, bf16[128,3584]{1,0:T(8,128)(2,1)}, u32[]{:S(2)}) copy-start(bf16[128,3584]{1,0:T(8,128)(2,1)} %near.7) | copy-start | bytes 2752516
  26.2 16.3 %copy-start.8 = (f32[1,3584]{1,0:T(1,128)S(1)}, f32[1,3584]{1,0:T(1,128)}, u32[]{:S(2)}) copy-start(f32[1,3584]{1,0:T(1,128)} %steer.5) | copy-start | bytes 43012
  26.2 16.3 %copy-start.9 = (f32[1,128]{1,0:T(1,128)S(1)}, f32[1,128]{1,0:T(1,128)}, u32[]{:S(2)}) copy-start(f32[1,128]{1,0:T(1,128)} %weight.2) | copy-start | bytes 1540
  26.3 16.3 %copy-start.12 = (s32[1,128,1]{1,2,0:T(1,128)S(1)}, s32[1,128,1]{1,2,0:T(1,128)}, u32[]{:S(2)}) copy-start(s32[1,128,1]{1,2,0:T(1,128)} %param.20) | copy-start | bytes 1540
  28.2 16.0 %collective-permute-start.4 = (bf16[48,3584]{1,0:T(8,128)(2,1)S(1)}, bf16[48,3584]{1,0:T(8,128)(2,1)S(1)}, u32[]{:S(2)}, u32[]{:S(2)}) collective-permute-start(bf16[48,3584]{1,0:T(8,128)(2,1)S(1)} %get-tuple-element.59), channel_id=1, source_target_pairs={{0,4},{1,5},{2,6},{3,7},{4,8},{5,9},{6,10},{7,11},{8,12},{9,13},{1... | collective-permute-start | bytes 1032200 | tf_op jit(solution)/shard_map/ppermute | solution.py:368
  29.8 27.8 %collective-permute-start.7 = (bf16[48,3584]{1,0:T(8,128)(2,1)S(1)}, bf16[48,3584]{1,0:T(8,128)(2,1)S(1)}, u32[]{:S(2)}, u32[]{:S(2)}) collective-permute-start(bf16[48,3584]{1,0:T(8,128)(2,1)S(1)} %get-tuple-element.58.refs_0_), channel_id=1, source_target_pairs={{0,2},{1,3},{2,0},{3,1},{4,6},{5,7},{6,4},{7,5},{8,10},{9,11},{10,... | collective-permute-start | bytes 1032200 | tf_op jit(solution)/shard_map/ppermute | solution.py:372
  42.6 16.6 %collective-permute-start.6 = (bf16[48,3584]{1,0:T(8,128)(2,1)S(1)}, bf16[48,3584]{1,0:T(8,128)(2,1)S(1)}, u32[]{:S(2)}, u32[]{:S(2)}) collective-permute-start(bf16[48,3584]{1,0:T(8,128)(2,1)S(1)} %get-tuple-element.62), channel_id=1, source_target_pairs={{0,12},{1,13},{2,14},{3,15},{4,0},{5,1},{6,2},{7,3},{8,4},{9,5},{1... | collective-permute-start | bytes 1032200 | tf_op jit(solution)/shard_map/ppermute | solution.py:368
  42.6 2.4 %copy-start.3 = (bf16[1,256,3584]{2,1,0:T(8,128)(2,1)S(1)}, bf16[1,256,3584]{2,1,0:T(8,128)(2,1)}, u32[]{:S(2)}) copy-start(bf16[1,256,3584]{2,1,0:T(8,128)(2,1)} %param.26) | copy-start | bytes 5505028
  42.6 37.0 %copy-start.1 = (bf16[1,3584,256]{2,1,0:T(8,128)(2,1)S(1)}, bf16[1,3584,256]{2,1,0:T(8,128)(2,1)}, u32[]{:S(2)}) copy-start(bf16[1,3584,256]{2,1,0:T(8,128)(2,1)} %param.24) | copy-start | bytes 5505028
  42.6 37.0 %copy-start.2 = (bf16[1,3584,256]{2,1,0:T(8,128)(2,1)S(1)}, bf16[1,3584,256]{2,1,0:T(8,128)(2,1)}, u32[]{:S(2)}) copy-start(bf16[1,3584,256]{2,1,0:T(8,128)(2,1)} %param.25) | copy-start | bytes 5505028
  44.2 27.6 %collective-permute-start.14 = (bf16[48,3584]{1,0:T(8,128)(2,1)S(1)}, bf16[48,3584]{1,0:T(8,128)(2,1)S(1)}, u32[]{:S(2)}, u32[]{:S(2)}) collective-permute-start(bf16[48,3584]{1,0:T(8,128)(2,1)S(1)} %get-tuple-element.69), channel_id=1, source_target_pairs={{0,8},{1,9},{2,10},{3,11},{4,12},{5,13},{6,14},{7,15},{8,0},{9,1},... | collective-permute-start | bytes 1032200 | tf_op jit(solution)/shard_map/ppermute | solution.py:368
  45.0 44.0 %collective-permute-start.11 = (bf16[256,3584]{1,0:T(8,128)(2,1)S(1)}, bf16[256,3584]{1,0:T(8,128)(2,1)S(1)}, u32[]{:S(2)}, u32[]{:S(2)}) collective-permute-start(bf16[256,3584]{1,0:T(8,128)(2,1)S(1)} %bitcast.27), channel_id=1, source_target_pairs={{0,1},{1,0},{2,3},{3,2},{4,5},{5,4},{6,7},{7,6},{8,9},{9,8},{10,11... | collective-permute-start | bytes 5505032 | tf_op jit(solution)/shard_map/ppermute | solution.py:375
  57.7 14.2 %collective-permute-start.8 = (bf16[48,3584]{1,0:T(8,128)(2,1)S(1)}, bf16[48,3584]{1,0:T(8,128)(2,1)S(1)}, u32[]{:S(2)}, u32[]{:S(2)}) collective-permute-start(bf16[48,3584]{1,0:T(8,128)(2,1)S(1)} %collective-permute-done.4.refs_1_), channel_id=1, source_target_pairs={{0,2},{1,3},{2,0},{3,1},{4,6},{5,7},{6,4},{7,5},{8,10},{9,11},{10,... | collective-permute-start | bytes 1032200 | tf_op jit(solution)/shard_map/ppermute | solution.py:372
  59.2 14.8 %collective-permute-start.9 = (bf16[48,3584]{1,0:T(8,128)(2,1)S(1)}, bf16[48,3584]{1,0:T(8,128)(2,1)S(1)}, u32[]{:S(2)}, u32[]{:S(2)}) collective-permute-start(bf16[48,3584]{1,0:T(8,128)(2,1)S(1)} %collective-permute-done.6.refs_2_), channel_id=1, source_target_pairs={{0,2},{1,3},{2,0},{3,1},{4,6},{5,7},{6,4},{7,5},{8,10},{9,11},{10,... | collective-permute-start | bytes 1032200 | tf_op jit(solution)/shard_map/ppermute | solution.py:372
  59.7 29.8 %collective-permute-start.16 = (bf16[48,3584]{1,0:T(8,128)(2,1)S(1)}, bf16[48,3584]{1,0:T(8,128)(2,1)S(1)}, u32[]{:S(2)}, u32[]{:S(2)}) collective-permute-start(bf16[48,3584]{1,0:T(8,128)(2,1)S(1)} %get-tuple-element.74), channel_id=1, source_target_pairs={{0,4},{1,5},{2,6},{3,7},{4,8},{5,9},{6,10},{7,11},{8,12},{9,13},{1... | collective-permute-start | bytes 1032200 | tf_op jit(solution)/shard_map/ppermute | solution.py:368
  71.8 17.7 %collective-permute-start.15 = (bf16[256,3584]{1,0:T(8,128)(2,1)S(1)}, bf16[256,3584]{1,0:T(8,128)(2,1)S(1)}, u32[]{:S(2)}, u32[]{:S(2)}) collective-permute-start(bf16[256,3584]{1,0:T(8,128)(2,1)S(1)} %collective-permute-done.12.refs_0_.refs_6_), channel_id=1, source_target_pairs={{0,1},{1,0},{2,3},{3,2},{4,5},{5,4},{6,7},{7,6},{8,9},{9,8},{10,11... | collective-permute-start | bytes 5505032 | tf_op jit(solution)/shard_map/ppermute | solution.py:375
  71.9 12.1 %collective-permute-start.18 = (bf16[48,3584]{1,0:T(8,128)(2,1)S(1)}, bf16[48,3584]{1,0:T(8,128)(2,1)S(1)}, u32[]{:S(2)}, u32[]{:S(2)}) collective-permute-start(bf16[48,3584]{1,0:T(8,128)(2,1)S(1)} %get-tuple-element.76.refs_0_), channel_id=1, source_target_pairs={{0,2},{1,3},{2,0},{3,1},{4,6},{5,7},{6,4},{7,5},{8,10},{9,11},{10,... | collective-permute-start | bytes 1032200 | tf_op jit(solution)/shard_map/ppermute | solution.py:372
  73.9 15.6 %collective-permute-start.21 = (bf16[48,3584]{1,0:T(8,128)(2,1)S(1)}, bf16[48,3584]{1,0:T(8,128)(2,1)S(1)}, u32[]{:S(2)}, u32[]{:S(2)}) collective-permute-start(bf16[48,3584]{1,0:T(8,128)(2,1)S(1)} %get-tuple-element.83), channel_id=1, source_target_pairs={{0,12},{1,13},{2,14},{3,15},{4,0},{5,1},{6,2},{7,3},{8,4},{9,5},{1... | collective-permute-start | bytes 1032200 | tf_op jit(solution)/shard_map/ppermute | solution.py:368
  84.0 8.1 %collective-permute-start.10 = (bf16[144,512]{1,0:T(8,128)(2,1)S(1)}, bf16[144,512]{1,0:T(8,128)(2,1)S(1)}, u32[]{:S(2)}, u32[]{:S(2)}) collective-permute-start(bf16[144,512]{1,0:T(8,128)(2,1)S(1)} %get-tuple-element.66), channel_id=1, source_target_pairs={{0,2},{1,3},{2,0},{3,1},{4,6},{5,7},{6,4},{7,5},{8,10},{9,11},{10,... | collective-permute-start | bytes 442376 | tf_op jit(solution)/shard_map/ppermute | solution.py:372
  88.9 19.0 %collective-permute-start.19 = (bf16[48,512]{1,0:T(8,128)(2,1)S(1)}, bf16[48,512]{1,0:T(8,128)(2,1)S(1)}, u32[]{:S(2)}, u32[]{:S(2)}) collective-permute-start(bf16[48,512]{1,0:T(8,128)(2,1)S(1)} %get-tuple-element.79), channel_id=1, source_target_pairs={{0,2},{1,3},{2,0},{3,1},{4,6},{5,7},{6,4},{7,5},{8,10},{9,11},{10,... | collective-permute-start | bytes 147464 | tf_op jit(solution)/shard_map/ppermute | solution.py:372
  92.1 11.3 %collective-permute-start.23 = (bf16[192,512]{1,0:T(8,128)(2,1)S(1)}, bf16[192,512]{1,0:T(8,128)(2,1)S(1)}, u32[]{:S(2)}, u32[]{:S(2)}) collective-permute-start(bf16[192,512]{1,0:T(8,128)(2,1)S(1)} %get-tuple-element.92), channel_id=1, source_target_pairs={{0,2},{1,3},{2,0},{3,1},{4,6},{5,7},{6,4},{7,5},{8,10},{9,11},{10,... | collective-permute-start | bytes 589832 | tf_op jit(solution)/shard_map/ppermute | solution.py:372
  95.0 24.5 %collective-permute-start.22 = (bf16[48,3584]{1,0:T(8,128)(2,1)S(1)}, bf16[48,3584]{1,0:T(8,128)(2,1)S(1)}, u32[]{:S(2)}, u32[]{:S(2)}) collective-permute-start(bf16[48,3584]{1,0:T(8,128)(2,1)S(1)} %get-tuple-element.84), channel_id=1, source_target_pairs={{0,4},{1,5},{2,6},{3,7},{4,8},{5,9},{6,10},{7,11},{8,12},{9,13},{1... | collective-permute-start | bytes 1032200 | tf_op jit(solution)/shard_map/ppermute | solution.py:368
  95.1 16.1 %collective-permute-start.17 = (bf16[48,3584]{1,0:T(8,128)(2,1)S(1)}, bf16[48,3584]{1,0:T(8,128)(2,1)S(1)}, u32[]{:S(2)}, u32[]{:S(2)}) collective-permute-start(bf16[48,3584]{1,0:T(8,128)(2,1)S(1)} %get-tuple-element.75), channel_id=1, source_target_pairs={{0,12},{1,13},{2,14},{3,15},{4,0},{5,1},{6,2},{7,3},{8,4},{9,5},{1... | collective-permute-start | bytes 1032200 | tf_op jit(solution)/shard_map/ppermute | solution.py:368
  107.9 11.1 %collective-permute-start.27 = (bf16[48,3584]{1,0:T(8,128)(2,1)S(1)}, bf16[48,3584]{1,0:T(8,128)(2,1)S(1)}, u32[]{:S(2)}, u32[]{:S(2)}) collective-permute-start(bf16[48,3584]{1,0:T(8,128)(2,1)S(1)} %get-tuple-element.101), channel_id=1, source_target_pairs={{0,2},{1,3},{2,0},{3,1},{4,6},{5,7},{6,4},{7,5},{8,10},{9,11},{10,... | collective-permute-start | bytes 1032200 | tf_op jit(solution)/shard_map/ppermute | solution.py:372
  108.5 17.8 %collective-permute-start.24 = (bf16[48,3584]{1,0:T(8,128)(2,1)S(1)}, bf16[48,3584]{1,0:T(8,128)(2,1)S(1)}, u32[]{:S(2)}, u32[]{:S(2)}) collective-permute-start(bf16[48,3584]{1,0:T(8,128)(2,1)S(1)} %get-tuple-element.95), channel_id=1, source_target_pairs={{0,2},{1,3},{2,0},{3,1},{4,6},{5,7},{6,4},{7,5},{8,10},{9,11},{10,... | collective-permute-start | bytes 1032200 | tf_op jit(solution)/shard_map/ppermute | solution.py:372
  111.2 22.2 %collective-permute-start.20 = (bf16[48,3584]{1,0:T(8,128)(2,1)S(1)}, bf16[48,3584]{1,0:T(8,128)(2,1)S(1)}, u32[]{:S(2)}, u32[]{:S(2)}) collective-permute-start(bf16[48,3584]{1,0:T(8,128)(2,1)S(1)} %expert_out.3), channel_id=1, source_target_pairs={{0,8},{1,9},{2,10},{3,11},{4,12},{5,13},{6,14},{7,15},{8,0},{9,1},... | collective-permute-start | bytes 1032200 | tf_op jit(solution)/shard_map/ppermute | solution.py:368
  119.0 15.3 %collective-permute-start.29 = (bf16[48,3584]{1,0:T(8,128)(2,1)S(1)}, bf16[48,3584]{1,0:T(8,128)(2,1)S(1)}, u32[]{:S(2)}, u32[]{:S(2)}) collective-permute-start(bf16[48,3584]{1,0:T(8,128)(2,1)S(1)} %get-tuple-element.105), channel_id=1, source_target_pairs={{0,2},{1,3},{2,0},{3,1},{4,6},{5,7},{6,4},{7,5},{8,10},{9,11},{10,... | collective-permute-start | bytes 1032200 | tf_op jit(solution)/shard_map/ppermute | solution.py:372
  119.6 21.3 %collective-permute-start.28 = (bf16[48,3584]{1,0:T(8,128)(2,1)S(1)}, bf16[48,3584]{1,0:T(8,128)(2,1)S(1)}, u32[]{:S(2)}, u32[]{:S(2)}) collective-permute-start(bf16[48,3584]{1,0:T(8,128)(2,1)S(1)} %add_rows.6), channel_id=1, source_target_pairs={{0,8},{1,9},{2,10},{3,11},{4,12},{5,13},{6,14},{7,15},{8,0},{9,1},... | collective-permute-start | bytes 1032200 | tf_op jit(solution)/shard_map/ppermute | solution.py:368
  126.3 22.5 %collective-permute-start.25 = (bf16[48,3584]{1,0:T(8,128)(2,1)S(1)}, bf16[48,3584]{1,0:T(8,128)(2,1)S(1)}, u32[]{:S(2)}, u32[]{:S(2)}) collective-permute-start(bf16[48,3584]{1,0:T(8,128)(2,1)S(1)} %get-tuple-element.96), channel_id=1, source_target_pairs={{0,2},{1,3},{2,0},{3,1},{4,6},{5,7},{6,4},{7,5},{8,10},{9,11},{10,... | collective-permute-start | bytes 1032200 | tf_op jit(solution)/shard_map/ppermute | solution.py:372
  133.5 15.5 %collective-permute-start.26 = (bf16[48,3584]{1,0:T(8,128)(2,1)S(1)}, bf16[48,3584]{1,0:T(8,128)(2,1)S(1)}, u32[]{:S(2)}, u32[]{:S(2)}) collective-permute-start(bf16[48,3584]{1,0:T(8,128)(2,1)S(1)} %add_rows.5), channel_id=1, source_target_pairs={{0,12},{1,13},{2,14},{3,15},{4,0},{5,1},{6,2},{7,3},{8,4},{9,5},{1... | collective-permute-start | bytes 1032200 | tf_op jit(solution)/shard_map/ppermute | solution.py:368
  134.3 11.4 %copy-start.11 = (f32[1,128]{1,0:T(1,128)S(1)}, f32[1,128]{1,0:T(1,128)}, u32[]{:S(2)}) copy-start(f32[1,128]{1,0:T(1,128)} %weight.3) | copy-start | bytes 1540
  140.9 15.1 %collective-permute-start.30 = (bf16[48,3584]{1,0:T(8,128)(2,1)S(1)}, bf16[48,3584]{1,0:T(8,128)(2,1)S(1)}, u32[]{:S(2)}, u32[]{:S(2)}) collective-permute-start(bf16[48,3584]{1,0:T(8,128)(2,1)S(1)} %add_rows.7), channel_id=1, source_target_pairs={{0,4},{1,5},{2,6},{3,7},{4,8},{5,9},{6,10},{7,11},{8,12},{9,13},{1... | collective-permute-start | bytes 1032200 | tf_op jit(solution)/shard_map/ppermute | solution.py:368

commit v3 on v2

v3 whole, which is shorter than its diff:
```python
import functools

import jax
import jax.numpy as jnp
from jax import lax
from jax.experimental import pallas as pl
from jax.experimental.pallas import tpu as pltpu
from jax.sharding import PartitionSpec as P

H = 1024
CORES = 2
EARLY = (2,)
DOWN_PARTS = 2
RETURN_ORDER = (2, 1, 3, 0)
FLOPS = {"grad_rows": 10000000000, "add_rows": 2000000000, "forward_end": 50000000000}
BF16 = jnp.bfloat16
F32 = jnp.float32
COLS = 896
ROWS_BY_ROWS = (((1,), (1,)), ((), ()))
SMEM = pl.BlockSpec(memory_space=pltpu.SMEM)
VMEM = pl.BlockSpec(memory_space=pltpu.VMEM)


def after(value, *deps):
    return lax.optimization_barrier((value, *deps))[0] if deps else value


def dot(a, b):
    return jnp.dot(a, b, preferred_element_type=F32)


def dot_rows(a, b):
    return lax.dot_general(a, b, ROWS_BY_ROWS, preferred_element_type=F32)


def shape(rows, cols, dtype=BF16):
    return jax.ShapeDtypeStruct((rows, cols), dtype)


def shifted(value, axis, by):
    devices = lax.axis_size(axis)
    pairs = [(i, i + by) for i in range(devices) if 0 <= i + by < devices]
    return lax.ppermute(value, axis, pairs)


def call(kernel, name, outs, args, grid=None, in_specs=None, out_specs=None, scratch=(), limit=24):
    extra = {} if grid is None else {"grid": grid}
    return pl.pallas_call(
        kernel,
        out_shape=outs,
        in_specs=in_specs,
        out_specs=out_specs if out_specs is not None else [VMEM] * len(outs),
        scratch_shapes=list(scratch),
        name=name,
        cost_estimate=pl.CostEstimate(flops=FLOPS.get(name, 5000000000), bytes_accessed=100000, transcendentals=0),
        compiler_params=pltpu.CompilerParams(vmem_limit_bytes=limit << 20),
        **extra,
    )(*args)


def stacked(values):
    if values[0].shape[0] % 16 == 0:
        return jnp.concatenate(values, axis=0)
    return jnp.concatenate([value.astype(F32) for value in values], axis=0).astype(BF16)


def slot_of(ids, plane, experts, capacity, axis):
    tokens = ids.shape[axis]
    wide = (tokens, 128) if axis == 0 else (max(8, experts), tokens)
    chosen = jnp.where(ids == lax.broadcasted_iota(jnp.int32, wide, 1 - axis), 1.0, 0.0)
    row = lax.broadcasted_iota(jnp.int32, (tokens, tokens), 0)
    col = lax.broadcasted_iota(jnp.int32, (tokens, tokens), 1)
    if axis == 0:
        earlier = dot(jnp.where(col < row, 1.0, 0.0).astype(BF16), chosen.astype(BF16))
    else:
        earlier = dot(chosen.astype(BF16), jnp.where(row < col, 1.0, 0.0).astype(BF16))
    position = jnp.sum(chosen * earlier, axis=1 - axis, keepdims=True).astype(jnp.int32)
    ahead = ids - plane
    return jnp.where(ahead < 0, ahead + experts, ahead) * capacity + position


def slots_by_tokens(ids_row, plane, experts, capacity):
    wide = (experts * capacity, ids_row.shape[1])
    slot = slot_of(ids_row, plane, experts, capacity, 1)
    return jnp.where(lax.broadcasted_iota(jnp.int32, wide, 0) == slot, 1.0, 0.0).astype(BF16)


def tokens_by_slots(ids_row, plane, experts, capacity):
    wide = (ids_row.shape[1], experts * capacity)
    slot = slot_of(column(ids_row), plane, experts, capacity, 0)
    return jnp.where(lax.broadcasted_iota(jnp.int32, wide, 1) == slot, 1.0, 0.0).astype(BF16)


def column(row):
    size = row.shape[1]
    diagonal = lax.broadcasted_iota(jnp.int32, (size, size), 0) == lax.broadcasted_iota(jnp.int32, (size, size), 1)
    return jnp.sum(jnp.where(diagonal, row, jnp.zeros_like(row)), axis=1, keepdims=True)


def unit_of(steer):
    return steer / jnp.sqrt(jnp.sum(steer * steer, axis=1, keepdims=True) + 1e-06)


def pieces(width):
    return [slice(at, at + COLS) for at in range(0, width, COLS)]


def gather_into(layout, tokens_at, blocks, capacity, width):
    for cols in pieces(width):
        rows = dot(layout, tokens_at(cols))
        for k, ref in blocks.items():
            ref[:, cols] = rows[k * capacity : (k + 1) * capacity].astype(BF16)


def sent_at(token_ref, weight_ref, steer_ref):
    unit = unit_of(steer_ref[...])

    def wide(cols):
        return token_ref[:, cols].astype(F32)

    along = 0.0
    for cols in pieces(unit.shape[1]):
        along = along + jnp.sum(wide(cols) * unit[:, cols], axis=1, keepdims=True)
    weight = column(weight_ref[...])
    return lambda cols: (weight * (wide(cols) - along * unit[:, cols])).astype(BF16)


def saved_kernel(experts, capacity, at_ref, saved_gate, saved_up, kept, leaving):
    plane, chip, core = at_ref[0], at_ref[3], at_ref[4]
    size = saved_gate.shape[1]
    wide = (capacity, saved_gate.shape[0])
    ahead = lax.broadcasted_iota(jnp.int32, wide, 1) - lax.broadcasted_iota(jnp.int32, wide, 0)
    for ref, core_index in ((kept, core), (leaving, 1 - core)):
        chosen = []
        for chip_index in (chip, 1 - chip):
            for k in range(experts):
                source = jnp.where(plane < k, plane - k + experts, plane - k)
                start = ((source * 2 + chip_index) * CORES + core_index) * capacity
                chosen.append(jnp.where(ahead == start, 1.0, 0.0))
        chosen = jnp.concatenate(chosen, axis=0).astype(BF16)
        ref[:, :size] = dot(chosen, saved_gate[...]).astype(BF16)
        ref[:, size:] = dot(chosen, saved_up[...]).astype(BF16)


def first_kernel(ks, experts, capacity, at_ref, f_ids, b_ids, f_tok, b_tok, b_weight, steer, *out):
    blocks, width = dict(zip(ks, out)), f_tok.shape[1]

    @pl.when(at_ref[1] == 1)
    def _():
        layout = slots_by_tokens(b_ids[...], at_ref[0], experts, capacity)
        gather_into(layout, sent_at(b_tok, b_weight, steer), blocks, capacity, width)

    @pl.when(at_ref[1] == 0)
    def _():
        layout = slots_by_tokens(f_ids[...], at_ref[0], experts, capacity)
        gather_into(layout, lambda cols: f_tok[:, cols], blocks, capacity, width)


def forward_rows_kernel(experts, capacity, at_ref, ids, near, far, *out):
    blocks, width = dict(enumerate(out)), near.shape[1]
    layout = slots_by_tokens(ids[...], at_ref[0], experts, capacity)
    pl.when(at_ref[2] == 1)(lambda: gather_into(layout, lambda cols: near[:, cols], blocks, capacity, width))
    pl.when(at_ref[2] == 0)(lambda: gather_into(layout, lambda cols: far[:, cols], blocks, capacity, width))


def backward_rows_kernel(early, experts, capacity, at_ref, ids, near, weight, steer, far, *refs):
    swapped, out = refs[: len(early)], refs[len(early) :]
    blocks, width = dict(enumerate(out)), near.shape[1]
    layout = slots_by_tokens(ids[...], at_ref[0], experts, capacity)

    @pl.when(at_ref[1] == 1)
    def _():
        others = {k: ref for k, ref in blocks.items() if k not in early}
        gather_into(layout, sent_at(near, weight, steer), others, capacity, width)
        for k, ref in zip(early, swapped):
            blocks[k][...] = ref[...]

    @pl.when(at_ref[1] == 0)
    def _():
        gather_into(layout, sent_at(far, weight, steer), blocks, capacity, width)


def hidden_kernel(count, *refs):
    rows, weights = refs[:count], refs[count : count + 4]
    own, other, x = refs[count + 4 :]
    x[...] = stacked([ref[...] for ref in rows])
    half, size = own.shape[0], weights[0].shape[1]
    for j in range(CORES):
        value = jax.nn.silu(dot(x[...], weights[j][...])) * dot(x[...], weights[CORES + j][...])
        cols = slice(j * size, (j + 1) * size)
        own[:, cols], other[:, cols] = value[:half].astype(BF16), value[half:].astype(BF16)


def out_kernel(capacity, own, other, d0, d1, *refs):
    d2, d3, out = refs[0], refs[1 : 1 + DOWN_PARTS], refs[1 + DOWN_PARTS :]
    size = d0.shape[0]
    for cols in pieces(d0.shape[1]):
        rows = dot(own[:, :size], d0[:, cols]) + dot(own[:, size:], d1[:, cols])
        rows = rows + dot(other[:, :size], d2[:, cols])
        rows = rows + dot(other[:, size:], stacked([ref[:, cols] for ref in d3]))
        for i, ref in enumerate(out):
            ref[:, cols] = rows[i * capacity : (i + 1) * capacity].astype(BF16)


def grad_hidden_kernel(*refs):
    rows, downs, (own, other, x) = refs[: -6 - DOWN_PARTS], refs[-6 - DOWN_PARTS : -3], refs[-3:]
    x[...] = stacked([ref[...] for ref in rows])
    size = downs[0].shape[0]
    groups = (downs[2:3], downs[3:], downs[:1], downs[1:2])
    for j, group in enumerate(groups):
        grads = dot_rows(x[...], stacked([ref[...] for ref in group]))
        ref = other if j < 2 else own
        ref[:, (j % 2) * size : (j % 2 + 1) * size] = grads.astype(ref.dtype)


def grad_rows_kernel(capacity, order, side, grads, kept, got, g0, g1, u0, u1, *refs):
    out, (gate_grad, up_grad) = refs[:-2], refs[-2:]
    size, height = g0.shape[1], grads.shape[0]
    here = slice(side * height, (side + 1) * height)
    for j, saved in enumerate((kept, got)):
        at = slice(j * size, (j + 1) * size)
        g, u = saved[here, :size].astype(F32), saved[here, size:].astype(F32)
        grad = grads[:, at].astype(F32)
        s = jax.nn.sigmoid(g)
        gate_grad[:, at] = (grad * u * s * (1.0 + g * (1.0 - s))).astype(BF16)
        up_grad[:, at] = (grad * g * s).astype(BF16)
    for cols in pieces(g0.shape[0]):
        rows = dot_rows(gate_grad[:, :size], g0[cols, :]) + dot_rows(gate_grad[:, size:], g1[cols, :])
        rows = rows + dot_rows(up_grad[:, :size], u0[cols, :]) + dot_rows(up_grad[:, size:], u1[cols, :])
        for ref, k in zip(out, order):
            ref[:, cols] = rows[k * capacity : (k + 1) * capacity].astype(ref.dtype)


def add_kernel(ours, theirs, out):
    out[...] = (ours[...] + theirs[...].astype(F32)).astype(BF16)


def forward_end_kernel(experts, capacity, at_ref, ids, near, far, weight, steer, *refs):
    back, (out, coefficient, mixed) = refs[:experts], refs[experts:]
    layout = tokens_by_slots(ids[...], at_ref[0], experts, capacity)
    unit = unit_of(steer[...])
    along, scale = 0.0, column(weight[...])
    for cols in pieces(near.shape[1]):
        rows = scale * dot(layout, stacked([ref[:, cols] for ref in back]))
        mixed[:, cols] = rows
        along = along + jnp.sum(rows * unit[:, cols], axis=1, keepdims=True)
    size = along.shape[0]
    diagonal = lax.broadcasted_iota(jnp.int32, (size, size), 0) == lax.broadcasted_iota(jnp.int32, (size, size), 1)
    coefficient[...] = jnp.sum(jnp.where(diagonal, along, 0.0), axis=0, keepdims=True)

    def finish(tokens):
        for cols in pieces(near.shape[1]):
            start = tokens[:, cols].astype(F32)
            out[:, cols] = (start + mixed[:, cols] - along * unit[:, cols]).astype(BF16)

    pl.when(at_ref[2] == 1)(lambda: finish(near))
    pl.when(at_ref[2] == 0)(lambda: finish(far))


def backward_end_kernel(experts, capacity, at_ref, ids, near, far, *refs):
    back, out = refs[:experts], refs[experts]
    layout = tokens_by_slots(ids[...], at_ref[0], experts, capacity)

    def finish(tokens):
        for cols in pieces(near.shape[1]):
            rows = dot(layout, stacked([ref[:, cols] for ref in back]))
            start = tokens[:, cols].astype(F32)
            out[:, cols] = (start + rows).astype(BF16)

    pl.when(at_ref[1] == 1)(lambda: finish(near))
    pl.when(at_ref[1] == 0)(lambda: finish(far))


def body(
    embedded,
    forward_held,
    forward_route,
    forward_weight,
    loss_cotangent,
    backward_held,
    backward_route,
    backward_weight,
    saved_gate,
    saved_up,
    gate_weight,
    up_weight,
    down_weight,
    steering,
):
    section_count = lax.axis_size("section")
    section_index = lax.axis_index("section")
    device_count = lax.axis_size("expert")
    device_index = lax.axis_index("expert")
    local_hidden = gate_weight.shape[2]
    holders = H // local_hidden
    experts = device_count // holders
    capacity = saved_gate.shape[1] // device_count
    rows = experts * capacity
    tokens, width = embedded.shape
    plane = device_index // holders
    chip = lax.rem(device_index, holders) // CORES
    core = lax.rem(device_index, CORES)
    first, last = section_index == 0, section_index == section_count - 1
    at = jnp.stack([plane, last.astype(jnp.int32), first.astype(jnp.int32), chip, core])
    early = [k for k in EARLY if k < experts]
    routed = [k for k in range(1, experts) if k not in early]

    def to_plane(value, by):
        pairs = [(i, (i + by * holders) % device_count) for i in range(device_count)]
        return lax.ppermute(value, "expert", pairs)

    def to_chip(value):
        pairs = [(i, i // holders * holders + (i + CORES) % holders) for i in range(device_count)]
        return lax.ppermute(value, "expert", pairs)

    def to_core(value):
        return lax.ppermute(value, "expert", [(i, i ^ 1) for i in range(device_count)])

    z_order, x_order = [], []

    def z_send(block, by, *deps, ahead=3):
        out = to_plane(after(block, *z_order[-ahead:][: len(z_order) >= ahead], *deps), by)
        z_order.append(out)
        return out

    def x_send(block):
        out = to_chip(after(block, *x_order[-2:][: len(x_order) >= 2]))
        x_order.append(out)
        return out

    gate, up, down = gate_weight[0], up_weight[0], down_weight[0]
    f_ids, b_ids = forward_route[0].reshape(1, tokens), backward_route[0].reshape(1, tokens)

    arriving = shifted(forward_held, "section", 1)[0]
    returning = shifted(backward_held, "section", -1)[0]
    d2 = to_chip(down)
    gate_sib, up_sib = to_core(gate), to_core(up)

    if section_count == 2:
        near_forward, near_backward = embedded, loss_cotangent
    else:
        near_forward = jnp.where(first, embedded, arriving)
        near_backward = jnp.where(last, loss_cotangent, returning)
    ones = call(
        functools.partial(first_kernel, early, experts, capacity),
        "first_rows",
        [shape(capacity, width)] * len(early),
        (at, f_ids, b_ids, near_forward, near_backward, backward_weight, steering),
        in_specs=[SMEM] + [VMEM] * 6,
        limit=56,
    )
    got_one = {k: z_send(block, k, gate_sib, up_sib) for k, block in zip(early, ones)}
    d1 = to_core(down)
    forward_rows = call(
        functools.partial(forward_rows_kernel, experts, capacity),
        "forward_rows",
        [shape(capacity, width)] * experts,
        (after(at, gate_sib, up_sib, d1), f_ids, embedded, arriving),
        in_specs=[SMEM] + [VMEM] * 3,
    )
    backward_rows = call(
        functools.partial(backward_rows_kernel, early, experts, capacity),
        "backward_rows",
        [shape(capacity, width)] * experts,
        (at, b_ids, loss_cotangent, backward_weight, steering, returning, *(forward_rows[k] for k in early)),
        in_specs=[SMEM] + [VMEM] * (5 + len(early)),
    )
    forward_got, backward_got = {0: forward_rows[0]}, {0: backward_rows[0]}
    for k in routed:
        forward_got[k] = z_send(forward_rows[k], k)
    got_two = {k: z_send(backward_rows[k], k) for k in early}

    kept, leaving = call(
        functools.partial(saved_kernel, experts, capacity),
        "saved_rows",
        [shape(CORES * rows, 2 * local_hidden)] * 2,
        (at, after(saved_gate[0], backward_rows[0]), saved_up[0]),
        in_specs=[SMEM] + [VMEM] * 2,
    )
    got = to_core(leaving)
    held = after(d2, *(forward_got[k] for k in routed))
    height = local_hidden // DOWN_PARTS
    d3 = [to_core(held[p * height : (p + 1) * height]) for p in range(DOWN_PARTS)]

    across = {}
    for k in routed:
        across[k] = x_send(forward_got[k])
        backward_got[k] = z_send(backward_rows[k], k, ahead=1)
    for k in early:
        forward_got[k] = jnp.where(last, got_two[k], got_one[k])
        backward_got[k] = jnp.where(last, got_one[k], got_two[k])
        across[k] = x_send(forward_got[k])
    across[0] = x_send(forward_got[0])
    columns_of = (gate, gate_sib, up, up_sib)
    downs = (down, d1, d2, *d3)

    forward_back, outs = {}, []
    for group in [each for each in (routed, early + [0]) if each]:
        height = len(group) * capacity
        own, other = call(
            functools.partial(hidden_kernel, 2 * len(group)),
            "hidden",
            [shape(height, 2 * local_hidden)] * 2,
            [after(forward_got[group[0]], got)]
            + [forward_got[k] for k in group[1:]]
            + [across[k] for k in group]
            + list(columns_of),
            in_specs=[VMEM] * (2 * len(group) + 4),
            scratch=[pltpu.VMEM((2 * height, width), BF16)],
            limit=16,
        )
        blocks = call(
            functools.partial(out_kernel, capacity),
            "expert_out",
            [shape(capacity, width)] * len(group),
            (own, x_send(other), *downs),
            in_specs=[VMEM] * (2 + len(downs)),
            limit=16,
        )
        outs.append(blocks[0])
        for k, block in zip(group, blocks):
            forward_back[k] = block if k == 0 else z_send(block, -k)

    grads_own, grads_other = call(
        grad_hidden_kernel,
        "grad_hidden",
        [shape(rows, 2 * local_hidden, F32), shape(rows, 2 * local_hidden)],
        [after(backward_got[0], outs[0])] + [backward_got[k] for k in range(1, experts)] + list(downs),
        in_specs=[VMEM] * (experts + len(downs)),
        scratch=[pltpu.VMEM((rows, width), BF16)],
        limit=16,
    )
    grads_got = x_send(grads_other)

    def grad_rows(grads, side, order, dtype):
        return call(
            functools.partial(grad_rows_kernel, capacity, order, side),
            "grad_rows",
            [shape(capacity, width, dtype)] * experts,
            (grads, kept, got, *columns_of),
            in_specs=[VMEM] * 7,
            scratch=[pltpu.VMEM((rows, 2 * local_hidden), BF16)] * 2,
            limit=16,
        )

    mine = grad_rows(grads_own, 0, list(range(experts)), F32)
    order = [k for k in RETURN_ORDER if k < experts]
    order += [k for k in range(experts) if k not in order]
    theirs = grad_rows(grads_got, 1, order, BF16)
    backward_back = {}
    for k, part in zip(order, theirs):
        block = call(add_kernel, "add_rows", [shape(capacity, width)], (mine[k], x_send(part)), in_specs=[VMEM] * 2)[0]
        backward_back[k] = block if k == 0 else z_send(block, -k)

    forward_out, coefficient = call(
        functools.partial(forward_end_kernel, experts, capacity),
        "forward_end",
        [shape(tokens, width), shape(1, tokens, F32)],
        (at, f_ids, embedded, arriving, forward_weight, steering, *(forward_back[k] for k in range(experts))),
        in_specs=[SMEM] + [VMEM] * (5 + experts),
        scratch=[pltpu.VMEM((tokens, width), F32)],
    )
    backward_out = call(
        functools.partial(backward_end_kernel, experts, capacity),
        "backward_end",
        [shape(tokens, width)],
        (at, b_ids, loss_cotangent, returning, *(backward_back[k] for k in range(experts))),
        in_specs=[SMEM] + [VMEM] * (3 + experts),
    )[0]
    return (forward_out[None], coefficient, backward_out[None])


def solution(mesh):
    in_specs = (
        P("expert", None),
        P("section", "expert", None),
        P("section", "expert", None),
        P("section", "expert"),
        P("expert", None),
        P("section", "expert", None),
        P("section", "expert", None),
        P("section", "expert"),
        P("section", None, "expert"),
        P("section", None, "expert"),
        P("section", None, "expert"),
        P("section", None, "expert"),
        P("section", "expert", None),
        P("section", None),
    )
    out_specs = (P("section", "expert", None), P("section", "expert"), P("section", "expert", None))
    return jax.shard_map(body, mesh=mesh, in_specs=in_specs, out_specs=out_specs, check_vma=False)
```

time: 158 us -> 151 us (0.956)
  the two profiles are of different devices: /device:TPU:0 before, /device:TPU:8 now
where the time goes in v3:
time: 151 us
  waiting for transfers between devices  74 us (49%)
  Pallas kernels  37.9 us (25%)
  starting transfers between devices  36.9 us (24%)
    ppermute x12, waiting for transfers between devices, to_chip(): return lax.ppermute(value, 'expert', pairs)  41.2 us
    pallas_call x17, Pallas kernels, call(): pl.pallas_call(kernel, out_shape=outs, in_specs=in_specs, out_specs=out_s...  37.9 us
    ppermute x12, waiting for transfers between devices, to_plane(): return lax.ppermute(value, 'expert', pairs)  18.7 us
    ppermute x12, starting transfers between devices, to_plane(): return lax.ppermute(value, 'expert', pairs)  17.2 us
    ppermute x2, waiting for transfers between devices, shifted(): return lax.ppermute(value, axis, pairs)  14 us
    ppermute x12, starting transfers between devices, to_chip(): return lax.ppermute(value, 'expert', pairs)  13.6 us
    ppermute x2, starting transfers between devices, shifted(): return lax.ppermute(value, axis, pairs)  4.75 us
  transfers between devices with their start and end apart: 32, of which 14 were waited for; matrix products, arithmetic and copies ran while one was open for 1% of the time, Pallas kernels for 24%

profile of v3, /device:TPU:8, one launch (start us, length us, event | category | flops | bytes accessed | tf_op | source)
XLA Modules:
  0.0 151.2 jit_solution(10546446887922766691)
XLA Ops:
  0.6 0.1 collective-permute-start.2
  0.7 0.5 collective-permute-start.3
  1.2 0.1 collective-permute-start.4
  1.3 3.5 %collective-permute-start = (bf16[1,128,3584]{2,1,0:T(8,128)(2,1)}, bf16[1,128,3584]{2,1,0:T(8,128)(2,1)S(1)}, u32[]{:S(2)}, u32[]{:S(2)}) collective-permute-start(bf16[1,128,3584]{2,1,0:T(8,128)(2,1)} %param.15), channel_id=1, source_target_pairs={{0,16},{1,17},{2,18},{3,19},{4,20},{5,21},{6,22},{7,23},{8,24},{9,... | collective-permute-start | bytes 2752520 | tf_op jit(solution)/shard_map/ppermute | solution.py:43
  4.8 1.6 %collective-permute-start.15 = (bf16[256,3584]{1,0:T(8,128)(2,1)}, bf16[256,3584]{1,0:T(8,128)(2,1)S(1)}, u32[]{:S(2)}, u32[]{:S(2)}) collective-permute-start(bf16[256,3584]{1,0:T(8,128)(2,1)} %bitcast.17), channel_id=1, source_target_pairs={{0,2},{1,3},{2,0},{3,1},{4,6},{5,7},{6,4},{7,5},{8,10},{9,11},{10,... | collective-permute-start | bytes 5505032 | tf_op jit(solution)/shard_map/ppermute | solution.py:314
  6.3 0.7 stack.31.at_ref
  7.0 1.3 collective-permute-start.1
  8.3 3.0 %first_rows.1 = bf16[48,3584]{1,0:T(8,128)(2,1)} custom-call(s32[5]{0:T(128)} %stack.31.at_ref, s32[1,128]{1,0:T(1,128)} %bitcast.37, s32[1,128]{1,0:T(1,128)} %bitcast.40, bf16[128,3584]{1,0:T(8,128)(2,1)} %near.6, bf16[128,3584]{1,0:T(8,128)(2,1)} %near.7, f32[1,128]{1,0:T(1,128)} %b_weight.1, f32[1,3584]{1,0:T(1,128)} %steer.5), custom_call_target="tpu_custom_call" | custom-call | flops 5000000000 | bytes 100000 | tf_op jit(solution)/shard_map/first_rows/pallas_call | solution.py:48
  11.3 2.6 %collective-permute-start.5 = (bf16[48,3584]{1,0:T(8,128)(2,1)}, bf16[48,3584]{1,0:T(8,128)(2,1)S(1)}, u32[]{:S(2)}, u32[]{:S(2)}) collective-permute-start(bf16[48,3584]{1,0:T(8,128)(2,1)} %first_rows.1), channel_id=1, source_target_pairs={{0,8},{1,9},{2,10},{3,11},{4,12},{5,13},{6,14},{7,15},{8,0},{9,1},... | collective-permute-start | bytes 1032200 | tf_op jit(solution)/shard_map/ppermute | solution.py:310
  13.9 11.3 %collective-permute-done = bf16[1,128,3584]{2,1,0:T(8,128)(2,1)S(1)} collective-permute-done((bf16[1,128,3584]{2,1,0:T(8,128)(2,1)}, bf16[1,128,3584]{2,1,0:T(8,128)(2,1)S(1)}, u32[]{:S(2)}, u32[]{:S(2)}) %collective-permute-start) | collective-permute-done | bytes 917536 | tf_op jit(solution)/shard_map/ppermute | solution.py:43
  25.3 1.2 forward_rows.1
  26.5 1.6 %collective-permute-start.8 = (bf16[48,3584]{1,0:T(8,128)(2,1)S(1)}, bf16[48,3584]{1,0:T(8,128)(2,1)S(1)}, u32[]{:S(2)}, u32[]{:S(2)}) collective-permute-start(bf16[48,3584]{1,0:T(8,128)(2,1)S(1)} %get-tuple-element.68), channel_id=1, source_target_pairs={{0,4},{1,5},{2,6},{3,7},{4,8},{5,9},{6,10},{7,11},{8,12},{9,13},{1... | collective-permute-start | bytes 1032200 | tf_op jit(solution)/shard_map/ppermute | solution.py:310
  28.1 0.4 collective-permute-start.11
  28.6 2.7 %collective-permute-done.1 = bf16[1,128,3584]{2,1,0:T(8,128)(2,1)S(1)} collective-permute-done((bf16[1,128,3584]{2,1,0:T(8,128)(2,1)}, bf16[1,128,3584]{2,1,0:T(8,128)(2,1)S(1)}, u32[]{:S(2)}, u32[]{:S(2)}) %collective-permute-start.1) | collective-permute-done | bytes 917536 | tf_op jit(solution)/shard_map/ppermute | solution.py:43
  31.3 1.6 %backward_rows.1 = (bf16[48,3584]{1,0:T(8,128)(2,1)S(1)}, bf16[48,3584]{1,0:T(8,128)(2,1)S(1)}, bf16[48,3584]{1,0:T(8,128)(2,1)S(1)}, bf16[48,3584]{1,0:T(8,128)(2,1)S(1)}) custom-call(s32[5]{0:T(128)S(1)} %copy-done, s32[1,128]{1,0:T(1,128)S(1)} %bitcast.41, bf16[128,3584]{1,0:T(8,128)(2,1)S(1)} %copy-done.5, f32[1,128]{1,0:T(1,128)S(1)} %copy-done.11, ...), custom_call_target="tpu_custom_call" | custom-call | flops 5000000000 | bytes 100000 | tf_op jit(solution)/shard_map/backward_rows/pallas_call | solution.py:48
  32.9 1.3 saved_rows.1
  34.2 0.1 collective-permute-start.7
  34.3 12.8 %collective-permute-done.15.refs_0_.refs_6_ = bf16[256,3584]{1,0:T(8,128)(2,1)S(1)} collective-permute-done((bf16[256,3584]{1,0:T(8,128)(2,1)}, bf16[256,3584]{1,0:T(8,128)(2,1)S(1)}, u32[]{:S(2)}, u32[]{:S(2)}) %collective-permute-start.15) | collective-permute-done | bytes 1835040 | tf_op jit(solution)/shard_map/ppermute | solution.py:314
  47.2 2.7 %collective-permute-start.6 = (bf16[48,3584]{1,0:T(8,128)(2,1)S(1)}, bf16[48,3584]{1,0:T(8,128)(2,1)S(1)}, u32[]{:S(2)}, u32[]{:S(2)}) collective-permute-start(bf16[48,3584]{1,0:T(8,128)(2,1)S(1)} %get-tuple-element.62), channel_id=1, source_target_pairs={{0,8},{1,9},{2,10},{3,11},{4,12},{5,13},{6,14},{7,15},{8,0},{9,1},... | collective-permute-start | bytes 1032200 | tf_op jit(solution)/shard_map/ppermute | solution.py:310
  49.8 1.5 collective-permute-start.12
  51.3 0.1 fusion
  51.4 0.1 collective-permute-start.17
  51.5 0.5 collective-permute-start.16
  52.0 0.5 collective-permute-start.9
  52.5 8.3 %collective-permute-done.12.refs_3_ = bf16[48,3584]{1,0:T(8,128)(2,1)S(1)} collective-permute-done((bf16[48,3584]{1,0:T(8,128)(2,1)S(1)}, bf16[48,3584]{1,0:T(8,128)(2,1)S(1)}, u32[]{:S(2)}, u32[]{:S(2)}) %collective-permute-start.12) | collective-permute-done | bytes 344096 | tf_op jit(solution)/shard_map/ppermute | solution.py:314
  60.8 1.5 collective-permute-start.13
  62.3 1.6 %collective-permute-done.6 = bf16[48,3584]{1,0:T(8,128)(2,1)S(1)} collective-permute-done((bf16[48,3584]{1,0:T(8,128)(2,1)S(1)}, bf16[48,3584]{1,0:T(8,128)(2,1)S(1)}, u32[]{:S(2)}, u32[]{:S(2)}) %collective-permute-start.6) | collective-permute-done | bytes 344096 | tf_op jit(solution)/shard_map/ppermute | solution.py:310
  63.9 4.2 %collective-permute-done.9.refs_2_ = bf16[48,3584]{1,0:T(8,128)(2,1)S(1)} collective-permute-done((bf16[48,3584]{1,0:T(8,128)(2,1)S(1)}, bf16[48,3584]{1,0:T(8,128)(2,1)S(1)}, u32[]{:S(2)}, u32[]{:S(2)}) %collective-permute-start.9) | collective-permute-done | bytes 344096 | tf_op jit(solution)/shard_map/ppermute | solution.py:314
  68.2 1.5 collective-permute-start.10
  69.7 3.7 %hidden.3 = (bf16[96,512]{1,0:T(8,128)(2,1)S(1)}, bf16[96,512]{1,0:T(8,128)(2,1)S(1)}) custom-call(bf16[48,3584]{1,0:T(8,128)(2,1)S(1)} %collective-permute-done.8.refs_0_, bf16[48,3584]{1,0:T(8,128)(2,1)S(1)} %collective-permute-done.11.refs_1_, bf16[48,3584]{1,0:T(8,128)(2,1)S(1)} %collective-permute-done.9.refs_2_, ...), custom_call_target="tpu_custom_call" | custom-call | flops 5000000000 | bytes 100000 | tf_op jit(solution)/shard_map/hidden/pallas_call | solution.py:48
  73.3 3.6 %collective-permute-done.20.refs_1_ = bf16[48,3584]{1,0:T(8,128)(2,1)S(1)} collective-permute-done((bf16[48,3584]{1,0:T(8,128)(2,1)S(1)}, bf16[48,3584]{1,0:T(8,128)(2,1)S(1)}, u32[]{:S(2)}, u32[]{:S(2)}) %collective-permute-start.20) | collective-permute-done | bytes 344096 | tf_op jit(solution)/shard_map/ppermute | solution.py:310
  76.9 2.8 %collective-permute-start.21 = (bf16[48,3584]{1,0:T(8,128)(2,1)S(1)}, bf16[48,3584]{1,0:T(8,128)(2,1)S(1)}, u32[]{:S(2)}, u32[]{:S(2)}) collective-permute-start(bf16[48,3584]{1,0:T(8,128)(2,1)S(1)} %get-tuple-element.87), channel_id=1, source_target_pairs={{0,12},{1,13},{2,14},{3,15},{4,0},{5,1},{6,2},{7,3},{8,4},{9,5},{1... | collective-permute-start | bytes 1032200 | tf_op jit(solution)/shard_map/ppermute | solution.py:310
  79.8 1.2 collective-permute-done.10.refs_2_
  81.0 1.5 collective-permute-start.18
  82.4 3.7 %hidden.2 = (bf16[96,512]{1,0:T(8,128)(2,1)S(1)}, bf16[96,512]{1,0:T(8,128)(2,1)S(1)}) custom-call(bf16[48,3584]{1,0:T(8,128)(2,1)S(1)} %get-tuple-element.69.refs_0_, bf16[48,3584]{1,0:T(8,128)(2,1)S(1)} %get-tuple-element.71.refs_1_, bf16[48,3584]{1,0:T(8,128)(2,1)S(1)} %collective-permute-done.10.refs_2_, ...), custom_call_target="tpu_custom_call" | custom-call | flops 5000000000 | bytes 100000 | tf_op jit(solution)/shard_map/hidden/pallas_call | solution.py:48
  86.1 0.6 collective-permute-start.14
  86.8 2.8 %expert_out.3 = (bf16[48,3584]{1,0:T(8,128)(2,1)S(1)}, bf16[48,3584]{1,0:T(8,128)(2,1)S(1)}) custom-call(bf16[96,512]{1,0:T(8,128)(2,1)S(1)} %get-tuple-element.78.own, bf16[96,512]{1,0:T(8,128)(2,1)S(1)} %collective-permute-done.18.other, bf16[256,3584]{1,0:T(8,128)(2,1)S(1)} %bitcast.18, bf16[256,3584]{1,0:T(8,128)(2,1)} %collective-permute-done.4.d1.refs_5_, ...), custom_call_target="tpu_custom_call" | custom-call | flops 5000000000 | bytes 100000 | tf_op jit(solution)/shard_map/expert_out/pallas_call | solution.py:48
  89.6 0.5 collective-permute-start.19
  90.1 1.6 %collective-permute-start.23 = (bf16[48,3584]{1,0:T(8,128)(2,1)S(1)}, bf16[48,3584]{1,0:T(8,128)(2,1)S(1)}, u32[]{:S(2)}, u32[]{:S(2)}) collective-permute-start(bf16[48,3584]{1,0:T(8,128)(2,1)S(1)} %get-tuple-element.90), channel_id=1, source_target_pairs={{0,4},{1,5},{2,6},{3,7},{4,8},{5,9},{6,10},{7,11},{8,12},{9,13},{1... | collective-permute-start | bytes 1032200 | tf_op jit(solution)/shard_map/ppermute | solution.py:310
  91.6 4.0 %grad_hidden.1 = (f32[192,512]{1,0:T(8,128)S(1)}, bf16[192,512]{1,0:T(8,128)(2,1)S(1)}) custom-call(bf16[48,3584]{1,0:T(8,128)(2,1)S(1)} %get-tuple-element.93.refs_0_, bf16[48,3584]{1,0:T(8,128)(2,1)S(1)} %collective-permute-done.20.refs_1_, bf16[48,3584]{1,0:T(8,128)(2,1)S(1)} %get-tuple-element.115.refs_2_, ...), custom_call_target="tpu_custom_call" | custom-call | flops 5000000000 | bytes 100000 | tf_op jit(solution)/shard_map/grad_hidden/pallas_call | solution.py:48
  95.7 1.5 %collective-permute-start.24 = (bf16[192,512]{1,0:T(8,128)(2,1)S(1)}, bf16[192,512]{1,0:T(8,128)(2,1)S(1)}, u32[]{:S(2)}, u32[]{:S(2)}) collective-permute-start(bf16[192,512]{1,0:T(8,128)(2,1)S(1)} %get-tuple-element.98), channel_id=1, source_target_pairs={{0,2},{1,3},{2,0},{3,1},{4,6},{5,7},{6,4},{7,5},{8,10},{9,11},{10,... | collective-permute-start | bytes 589832 | tf_op jit(solution)/shard_map/ppermute | solution.py:314
  97.2 2.8 %expert_out.2 = (bf16[48,3584]{1,0:T(8,128)(2,1)S(1)}, bf16[48,3584]{1,0:T(8,128)(2,1)S(1)}) custom-call(bf16[96,512]{1,0:T(8,128)(2,1)S(1)} %get-tuple-element.72.own, bf16[96,512]{1,0:T(8,128)(2,1)S(1)} %collective-permute-done.14.other, bf16[256,3584]{1,0:T(8,128)(2,1)S(1)} %bitcast.20, bf16[256,3584]{1,0:T(8,128)(2,1)} %collective-permute-done.4.d1.refs_5_, ...), custom_call_target="tpu_custom_call" | custom-call | flops 5000000000 | bytes 100000 | tf_op jit(solution)/shard_map/expert_out/pallas_call | solution.py:48
  100.0 2.2 %collective-permute-start.22 = (bf16[48,3584]{1,0:T(8,128)(2,1)S(1)}, bf16[48,3584]{1,0:T(8,128)(2,1)S(1)}, u32[]{:S(2)}, u32[]{:S(2)}) collective-permute-start(bf16[48,3584]{1,0:T(8,128)(2,1)S(1)} %get-tuple-element.88), channel_id=1, source_target_pairs={{0,8},{1,9},{2,10},{3,11},{4,12},{5,13},{6,14},{7,15},{8,0},{9,1},... | collective-permute-start | bytes 1032200 | tf_op jit(solution)/shard_map/ppermute | solution.py:310
  102.2 4.5 %grad_rows.3 = (bf16[48,3584]{1,0:T(8,128)(2,1)S(1)}, bf16[48,3584]{1,0:T(8,128)(2,1)S(1)}, bf16[48,3584]{1,0:T(8,128)(2,1)S(1)}, bf16[48,3584]{1,0:T(8,128)(2,1)S(1)}) custom-call(bf16[192,512]{1,0:T(8,128)(2,1)S(1)} %collective-permute-done.24.grads, bf16[384,512]{1,0:T(8,128)(2,1)S(1)} %get-tuple-element.95.kept, ...), custom_call_target="tpu_custom_call" | custom-call | flops 10000000000 | bytes 100000 | tf_op jit(solution)/shard_map/grad_rows/pallas_call | solution.py:48
  106.7 0.7 collective-permute-start.28
  107.4 1.4 collective-permute-start.25
  108.8 4.5 %grad_rows.2 = (f32[48,3584]{1,0:T(8,128)S(1)}, f32[48,3584]{1,0:T(8,128)S(1)}, f32[48,3584]{1,0:T(8,128)S(1)}, f32[48,3584]{1,0:T(8,128)S(1)}) custom-call(f32[192,512]{1,0:T(8,128)S(1)} %get-tuple-element.94.grads, bf16[384,512]{1,0:T(8,128)(2,1)S(1)} %get-tuple-element.95.kept, bf16[384,512]{1,0:T(8,128)(2,1)S(1)} %collective-permute-done.7.got, ...), custom_call_target="tpu_custom_call" | custom-call | flops 10000000000 | bytes 100000 | tf_op jit(solution)/shard_map/grad_rows/pallas_call | solution.py:48
  113.3 4.5 %collective-permute-done.28.theirs = bf16[48,3584]{1,0:T(8,128)(2,1)S(1)} collective-permute-done((bf16[48,3584]{1,0:T(8,128)(2,1)S(1)}, bf16[48,3584]{1,0:T(8,128)(2,1)S(1)}, u32[]{:S(2)}, u32[]{:S(2)}) %collective-permute-start.28) | collective-permute-done | bytes 344096 | tf_op jit(solution)/shard_map/ppermute | solution.py:314
  117.8 0.6 collective-permute-start.30
  118.4 0.1 add_rows.6
  118.5 2.2 %collective-permute-start.29 = (bf16[48,3584]{1,0:T(8,128)(2,1)S(1)}, bf16[48,3584]{1,0:T(8,128)(2,1)S(1)}, u32[]{:S(2)}, u32[]{:S(2)}) collective-permute-start(bf16[48,3584]{1,0:T(8,128)(2,1)S(1)} %add_rows.6), channel_id=1, source_target_pairs={{0,8},{1,9},{2,10},{3,11},{4,12},{5,13},{6,14},{7,15},{8,0},{9,1},... | collective-permute-start | bytes 1032200 | tf_op jit(solution)/shard_map/ppermute | solution.py:310
  120.7 4.5 %collective-permute-done.25.theirs = bf16[48,3584]{1,0:T(8,128)(2,1)S(1)} collective-permute-done((bf16[48,3584]{1,0:T(8,128)(2,1)S(1)}, bf16[48,3584]{1,0:T(8,128)(2,1)S(1)}, u32[]{:S(2)}, u32[]{:S(2)}) %collective-permute-start.25) | collective-permute-done | bytes 344096 | tf_op jit(solution)/shard_map/ppermute | solution.py:314
  125.1 0.1 add_rows.5
  125.2 0.7 collective-permute-start.26
  125.9 0.5 collective-permute-start.27
  126.3 5.3 %collective-permute-done.30.theirs = bf16[48,3584]{1,0:T(8,128)(2,1)S(1)} collective-permute-done((bf16[48,3584]{1,0:T(8,128)(2,1)S(1)}, bf16[48,3584]{1,0:T(8,128)(2,1)S(1)}, u32[]{:S(2)}, u32[]{:S(2)}) %collective-permute-start.30) | collective-permute-done | bytes 344096 | tf_op jit(solution)/shard_map/ppermute | solution.py:314
  131.6 0.1 add_rows.7
  131.8 0.5 copy-done.13
  132.3 2.6 %forward_end.1 = (bf16[128,3584]{1,0:T(8,128)(2,1)}, f32[1,128]{1,0:T(1,128)}) custom-call(s32[5]{0:T(128)S(1)} %copy-done, s32[1,128]{1,0:T(1,128)S(1)} %bitcast.39, bf16[128,3584]{1,0:T(8,128)(2,1)S(1)} %copy-done.4, bf16[128,3584]{1,0:T(8,128)(2,1)S(1)} %bitcast.32, f32[1,128]{1,0:T(1,128)S(1)} %copy-done.13, f32[1,3584]{1,0:T(1,128)S(1)} %copy-done.10, ...), custom_call_target="tpu_custom_call" | custom-call | flops 49999998976 | bytes 100000 | tf_op jit(solution)/shard_map/forward_end/pallas_call | solution.py:48
  134.9 0.5 collective-permute-done.26.theirs
  135.3 0.1 add_rows.4.refs_0_
  135.4 5.0 %collective-permute-done.29.refs_2_ = bf16[48,3584]{1,0:T(8,128)(2,1)S(1)} collective-permute-done((bf16[48,3584]{1,0:T(8,128)(2,1)S(1)}, bf16[48,3584]{1,0:T(8,128)(2,1)S(1)}, u32[]{:S(2)}, u32[]{:S(2)}) %collective-permute-start.29) | collective-permute-done | bytes 344096 | tf_op jit(solution)/shard_map/ppermute | solution.py:310
  140.4 8.5 %collective-permute-done.27.refs_1_ = bf16[48,3584]{1,0:T(8,128)(2,1)S(1)} collective-permute-done((bf16[48,3584]{1,0:T(8,128)(2,1)S(1)}, bf16[48,3584]{1,0:T(8,128)(2,1)S(1)}, u32[]{:S(2)}, u32[]{:S(2)}) %collective-permute-start.27) | collective-permute-done | bytes 344096 | tf_op jit(solution)/shard_map/ppermute | solution.py:310
  149.0 2.2 %backward_end.1 = bf16[128,3584]{1,0:T(8,128)(2,1)} custom-call(s32[5]{0:T(128)S(1)} %copy-done, s32[1,128]{1,0:T(1,128)S(1)} %bitcast.42, bf16[128,3584]{1,0:T(8,128)(2,1)S(1)} %copy-done.5, bf16[128,3584]{1,0:T(8,128)(2,1)S(1)} %bitcast.34, bf16[48,3584]{1,0:T(8,128)(2,1)S(1)} %add_rows.4.refs_0_, bf16[48,3584]{1,0:T(8,128)(2,1)S(1)} %collective-permute-done.27.refs_1_, ...), custom_call_target="tpu_custom_call" | custom-call | flops 5000000000 | bytes 100000 | tf_op jit(solution)/shard_map/backward_end/pallas_call | solution.py:48
  (50 shorter events, 0.2 us)
Async XLA Ops:
  0.6 6.4 %collective-permute-start.2 = (bf16[3584,256]{1,0:T(8,128)(2,1)}, bf16[3584,256]{1,0:T(8,128)(2,1)}, u32[]{:S(2)}, u32[]{:S(2)}) collective-permute-start(bf16[3584,256]{1,0:T(8,128)(2,1)} %bitcast.21), channel_id=1, source_target_pairs={{0,1},{1,0},{2,3},{3,2},{4,5},{5,4},{6,7},{7,6},{8,9},{9,8},{10,11... | collective-permute-start | bytes 5505032 | tf_op jit(solution)/shard_map/ppermute | solution.py:317
  0.7 10.6 %collective-permute-start.3 = (bf16[3584,256]{1,0:T(8,128)(2,1)}, bf16[3584,256]{1,0:T(8,128)(2,1)}, u32[]{:S(2)}, u32[]{:S(2)}) collective-permute-start(bf16[3584,256]{1,0:T(8,128)(2,1)} %bitcast.26), channel_id=1, source_target_pairs={{0,1},{1,0},{2,3},{3,2},{4,5},{5,4},{6,7},{7,6},{8,9},{9,8},{10,11... | collective-permute-start | bytes 5505032 | tf_op jit(solution)/shard_map/ppermute | solution.py:317
  1.2 12.7 %collective-permute-start.4 = (bf16[256,3584]{1,0:T(8,128)(2,1)}, bf16[256,3584]{1,0:T(8,128)(2,1)}, u32[]{:S(2)}, u32[]{:S(2)}) collective-permute-start(bf16[256,3584]{1,0:T(8,128)(2,1)} %bitcast.16), channel_id=1, source_target_pairs={{0,1},{1,0},{2,3},{3,2},{4,5},{5,4},{6,7},{7,6},{8,9},{9,8},{10,11... | collective-permute-start | bytes 5505032 | tf_op jit(solution)/shard_map/ppermute | solution.py:317
  1.3 23.9 %collective-permute-start = (bf16[1,128,3584]{2,1,0:T(8,128)(2,1)}, bf16[1,128,3584]{2,1,0:T(8,128)(2,1)S(1)}, u32[]{:S(2)}, u32[]{:S(2)}) collective-permute-start(bf16[1,128,3584]{2,1,0:T(8,128)(2,1)} %param.15), channel_id=1, source_target_pairs={{0,16},{1,17},{2,18},{3,19},{4,20},{5,21},{6,22},{7,23},{8,24},{9,... | collective-permute-start | bytes 2752520 | tf_op jit(solution)/shard_map/ppermute | solution.py:43
  4.8 42.4 %collective-permute-start.15 = (bf16[256,3584]{1,0:T(8,128)(2,1)}, bf16[256,3584]{1,0:T(8,128)(2,1)S(1)}, u32[]{:S(2)}, u32[]{:S(2)}) collective-permute-start(bf16[256,3584]{1,0:T(8,128)(2,1)} %bitcast.17), channel_id=1, source_target_pairs={{0,2},{1,3},{2,0},{3,1},{4,6},{5,7},{6,4},{7,5},{8,10},{9,11},{10,... | collective-permute-start | bytes 5505032 | tf_op jit(solution)/shard_map/ppermute | solution.py:314
  7.0 24.2 %collective-permute-start.1 = (bf16[1,128,3584]{2,1,0:T(8,128)(2,1)}, bf16[1,128,3584]{2,1,0:T(8,128)(2,1)S(1)}, u32[]{:S(2)}, u32[]{:S(2)}) collective-permute-start(bf16[1,128,3584]{2,1,0:T(8,128)(2,1)} %param.19), channel_id=1, source_target_pairs={{16,0},{17,1},{18,2},{19,3},{20,4},{21,5},{22,6},{23,7},{24,8},{25... | collective-permute-start | bytes 2752520 | tf_op jit(solution)/shard_map/ppermute | solution.py:43
  8.3 16.9 %copy-start = (s32[5]{0:T(128)S(1)}, s32[5]{0:T(128)}, u32[]{:S(2)}) copy-start(s32[5]{0:T(128)} %stack.31.at_ref) | copy-start | bytes 64
  8.3 16.9 %copy-start.4 = (bf16[128,3584]{1,0:T(8,128)(2,1)S(1)}, bf16[128,3584]{1,0:T(8,128)(2,1)}, u32[]{:S(2)}) copy-start(bf16[128,3584]{1,0:T(8,128)(2,1)} %near.6) | copy-start | bytes 2752516
  8.3 16.9 %copy-start.12 = (s32[1,128,1]{1,2,0:T(1,128)S(1)}, s32[1,128,1]{1,2,0:T(1,128)}, u32[]{:S(2)}) copy-start(s32[1,128,1]{1,2,0:T(1,128)} %param.16) | copy-start | bytes 1540
  11.3 35.9 %collective-permute-start.5 = (bf16[48,3584]{1,0:T(8,128)(2,1)}, bf16[48,3584]{1,0:T(8,128)(2,1)S(1)}, u32[]{:S(2)}, u32[]{:S(2)}) collective-permute-start(bf16[48,3584]{1,0:T(8,128)(2,1)} %first_rows.1), channel_id=1, source_target_pairs={{0,8},{1,9},{2,10},{3,11},{4,12},{5,13},{6,14},{7,15},{8,0},{9,1},... | collective-permute-start | bytes 1032200 | tf_op jit(solution)/shard_map/ppermute | solution.py:310
  25.2 6.0 %copy-start.5 = (bf16[128,3584]{1,0:T(8,128)(2,1)S(1)}, bf16[128,3584]{1,0:T(8,128)(2,1)}, u32[]{:S(2)}) copy-start(bf16[128,3584]{1,0:T(8,128)(2,1)} %near.7) | copy-start | bytes 2752516
  25.2 6.0 %copy-start.10 = (f32[1,3584]{1,0:T(1,128)S(1)}, f32[1,3584]{1,0:T(1,128)}, u32[]{:S(2)}) copy-start(f32[1,3584]{1,0:T(1,128)} %steer.5) | copy-start | bytes 43012
  25.2 6.0 %copy-start.11 = (f32[1,128]{1,0:T(1,128)S(1)}, f32[1,128]{1,0:T(1,128)}, u32[]{:S(2)}) copy-start(f32[1,128]{1,0:T(1,128)} %b_weight.1) | copy-start | bytes 1540
  25.3 6.0 %copy-start.14 = (s32[1,128,1]{1,2,0:T(1,128)S(1)}, s32[1,128,1]{1,2,0:T(1,128)}, u32[]{:S(2)}) copy-start(s32[1,128,1]{1,2,0:T(1,128)} %param.20) | copy-start | bytes 1540
  26.5 20.6 %collective-permute-start.8 = (bf16[48,3584]{1,0:T(8,128)(2,1)S(1)}, bf16[48,3584]{1,0:T(8,128)(2,1)S(1)}, u32[]{:S(2)}, u32[]{:S(2)}) collective-permute-start(bf16[48,3584]{1,0:T(8,128)(2,1)S(1)} %get-tuple-element.68), channel_id=1, source_target_pairs={{0,4},{1,5},{2,6},{3,7},{4,8},{5,9},{6,10},{7,11},{8,12},{9,13},{1... | collective-permute-start | bytes 1032200 | tf_op jit(solution)/shard_map/ppermute | solution.py:310
  28.1 19.0 %collective-permute-start.11 = (bf16[48,3584]{1,0:T(8,128)(2,1)S(1)}, bf16[48,3584]{1,0:T(8,128)(2,1)S(1)}, u32[]{:S(2)}, u32[]{:S(2)}) collective-permute-start(bf16[48,3584]{1,0:T(8,128)(2,1)S(1)} %get-tuple-element.70), channel_id=1, source_target_pairs={{0,12},{1,13},{2,14},{3,15},{4,0},{5,1},{6,2},{7,3},{8,4},{9,5},{1... | collective-permute-start | bytes 1032200 | tf_op jit(solution)/shard_map/ppermute | solution.py:310
  31.2 1.7 %copy-start.6 = (bf16[1,128,3584]{2,1,0:T(8,128)(2,1)}, bf16[1,128,3584]{2,1,0:T(8,128)(2,1)S(1)}, u32[]{:S(2)}) copy-start(bf16[1,128,3584]{2,1,0:T(8,128)(2,1)S(1)} %collective-permute-done.1) | copy-start | bytes 2752516
  31.3 1.6 %copy-start.8 = (bf16[1,768,256]{2,1,0:T(8,128)(2,1)S(1)}, bf16[1,768,256]{2,1,0:T(8,128)(2,1)}, u32[]{:S(2)}) copy-start(bf16[1,768,256]{2,1,0:T(8,128)(2,1)} %param.22) | copy-start | bytes 1179652
  31.3 1.6 %copy-start.9 = (bf16[1,768,256]{2,1,0:T(8,128)(2,1)S(1)}, bf16[1,768,256]{2,1,0:T(8,128)(2,1)}, u32[]{:S(2)}) copy-start(bf16[1,768,256]{2,1,0:T(8,128)(2,1)} %param.23) | copy-start | bytes 1179652
  34.2 17.8 %collective-permute-start.7 = (bf16[384,512]{1,0:T(8,128)(2,1)S(1)}, bf16[384,512]{1,0:T(8,128)(2,1)S(1)}, u32[]{:S(2)}, u32[]{:S(2)}) collective-permute-start(bf16[384,512]{1,0:T(8,128)(2,1)S(1)} %get-tuple-element.65), channel_id=1, source_target_pairs={{0,1},{1,0},{2,3},{3,2},{4,5},{5,4},{6,7},{7,6},{8,9},{9,8},{10,11... | collective-permute-start | bytes 1179656 | tf_op jit(solution)/shard_map/ppermute | solution.py:317
  47.1 22.5 %copy-start.2 = (bf16[1,3584,256]{2,1,0:T(8,128)(2,1)S(1)}, bf16[1,3584,256]{2,1,0:T(8,128)(2,1)}, u32[]{:S(2)}) copy-start(bf16[1,3584,256]{2,1,0:T(8,128)(2,1)} %param.24) | copy-start | bytes 5505028
  47.1 22.5 %copy-start.3 = (bf16[1,3584,256]{2,1,0:T(8,128)(2,1)S(1)}, bf16[1,3584,256]{2,1,0:T(8,128)(2,1)}, u32[]{:S(2)}) copy-start(bf16[1,3584,256]{2,1,0:T(8,128)(2,1)} %param.25) | copy-start | bytes 5505028
  47.2 16.7 %collective-permute-start.6 = (bf16[48,3584]{1,0:T(8,128)(2,1)S(1)}, bf16[48,3584]{1,0:T(8,128)(2,1)S(1)}, u32[]{:S(2)}, u32[]{:S(2)}) collective-permute-start(bf16[48,3584]{1,0:T(8,128)(2,1)S(1)} %get-tuple-element.62), channel_id=1, source_target_pairs={{0,8},{1,9},{2,10},{3,11},{4,12},{5,13},{6,14},{7,15},{8,0},{9,1},... | collective-permute-start | bytes 1032200 | tf_op jit(solution)/shard_map/ppermute | solution.py:310
  49.8 11.0 %collective-permute-start.12 = (bf16[48,3584]{1,0:T(8,128)(2,1)S(1)}, bf16[48,3584]{1,0:T(8,128)(2,1)S(1)}, u32[]{:S(2)}, u32[]{:S(2)}) collective-permute-start(bf16[48,3584]{1,0:T(8,128)(2,1)S(1)} %collective-permute-done.11.refs_1_), channel_id=1, source_target_pairs={{0,2},{1,3},{2,0},{3,1},{4,6},{5,7},{6,4},{7,5},{8,10},{9,11},{10,... | collective-permute-start | bytes 1032200 | tf_op jit(solution)/shard_map/ppermute | solution.py:314
  51.4 35.3 %collective-permute-start.17 = (bf16[128,3584]{1,0:T(8,128)(2,1)S(1)}, bf16[128,3584]{1,0:T(8,128)(2,1)S(1)}, u32[]{:S(2)}, u32[]{:S(2)}) collective-permute-start(bf16[128,3584]{1,0:T(8,128)(2,1)S(1)} %get-tuple-element.113), channel_id=1, source_target_pairs={{0,1},{1,0},{2,3},{3,2},{4,5},{5,4},{6,7},{7,6},{8,9},{9,8},{10,11... | collective-permute-start | bytes 2752520 | tf_op jit(solution)/shard_map/ppermute | solution.py:317
  51.5 35.2 %collective-permute-start.16 = (bf16[128,3584]{1,0:T(8,128)(2,1)S(1)}, bf16[128,3584]{1,0:T(8,128)(2,1)S(1)}, u32[]{:S(2)}, u32[]{:S(2)}) collective-permute-start(bf16[128,3584]{1,0:T(8,128)(2,1)S(1)} %get-tuple-element.114), channel_id=1, source_target_pairs={{0,1},{1,0},{2,3},{3,2},{4,5},{5,4},{6,7},{7,6},{8,9},{9,8},{10,11... | collective-permute-start | bytes 2752520 | tf_op jit(solution)/shard_map/ppermute | solution.py:317
  52.0 16.2 %collective-permute-start.9 = (bf16[48,3584]{1,0:T(8,128)(2,1)S(1)}, bf16[48,3584]{1,0:T(8,128)(2,1)S(1)}, u32[]{:S(2)}, u32[]{:S(2)}) collective-permute-start(bf16[48,3584]{1,0:T(8,128)(2,1)S(1)} %collective-permute-done.8.refs_0_), channel_id=1, source_target_pairs={{0,2},{1,3},{2,0},{3,1},{4,6},{5,7},{6,4},{7,5},{8,10},{9,11},{10,... | collective-permute-start | bytes 1032200 | tf_op jit(solution)/shard_map/ppermute | solution.py:314
  60.8 21.6 %collective-permute-start.13 = (bf16[48,3584]{1,0:T(8,128)(2,1)S(1)}, bf16[48,3584]{1,0:T(8,128)(2,1)S(1)}, u32[]{:S(2)}, u32[]{:S(2)}) collective-permute-start(bf16[48,3584]{1,0:T(8,128)(2,1)S(1)} %get-tuple-element.71.refs_1_), channel_id=1, source_target_pairs={{0,2},{1,3},{2,0},{3,1},{4,6},{5,7},{6,4},{7,5},{8,10},{9,11},{10,... | collective-permute-start | bytes 1032200 | tf_op jit(solution)/shard_map/ppermute | solution.py:314
  68.2 12.8 %collective-permute-start.10 = (bf16[48,3584]{1,0:T(8,128)(2,1)S(1)}, bf16[48,3584]{1,0:T(8,128)(2,1)S(1)}, u32[]{:S(2)}, u32[]{:S(2)}) collective-permute-start(bf16[48,3584]{1,0:T(8,128)(2,1)S(1)} %get-tuple-element.69.refs_0_), channel_id=1, source_target_pairs={{0,2},{1,3},{2,0},{3,1},{4,6},{5,7},{6,4},{7,5},{8,10},{9,11},{10,... | collective-permute-start | bytes 1032200 | tf_op jit(solution)/shard_map/ppermute | solution.py:314
  69.7 7.2 %collective-permute-start.20 = (bf16[48,3584]{1,0:T(8,128)(2,1)S(1)}, bf16[48,3584]{1,0:T(8,128)(2,1)S(1)}, u32[]{:S(2)}, u32[]{:S(2)}) collective-permute-start(bf16[48,3584]{1,0:T(8,128)(2,1)S(1)} %get-tuple-element.86), channel_id=1, source_target_pairs={{0,4},{1,5},{2,6},{3,7},{4,8},{5,9},{6,10},{7,11},{8,12},{9,13},{1... | collective-permute-start | bytes 1032200 | tf_op jit(solution)/shard_map/ppermute | solution.py:310
  76.9 14.7 %collective-permute-start.21 = (bf16[48,3584]{1,0:T(8,128)(2,1)S(1)}, bf16[48,3584]{1,0:T(8,128)(2,1)S(1)}, u32[]{:S(2)}, u32[]{:S(2)}) collective-permute-start(bf16[48,3584]{1,0:T(8,128)(2,1)S(1)} %get-tuple-element.87), channel_id=1, source_target_pairs={{0,12},{1,13},{2,14},{3,15},{4,0},{5,1},{6,2},{7,3},{8,4},{9,5},{1... | collective-permute-start | bytes 1032200 | tf_op jit(solution)/shard_map/ppermute | solution.py:310
  81.0 5.8 %copy-start.1 = (bf16[1,256,3584]{2,1,0:T(8,128)(2,1)S(1)}, bf16[1,256,3584]{2,1,0:T(8,128)(2,1)}, u32[]{:S(2)}) copy-start(bf16[1,256,3584]{2,1,0:T(8,128)(2,1)} %param.26) | copy-start | bytes 5505028
  81.0 5.8 %collective-permute-start.18 = (bf16[96,512]{1,0:T(8,128)(2,1)S(1)}, bf16[96,512]{1,0:T(8,128)(2,1)S(1)}, u32[]{:S(2)}, u32[]{:S(2)}) collective-permute-start(bf16[96,512]{1,0:T(8,128)(2,1)S(1)} %get-tuple-element.80), channel_id=1, source_target_pairs={{0,2},{1,3},{2,0},{3,1},{4,6},{5,7},{6,4},{7,5},{8,10},{9,11},{10,... | collective-permute-start | bytes 294920 | tf_op jit(solution)/shard_map/ppermute | solution.py:314
  86.1 11.1 %collective-permute-start.14 = (bf16[96,512]{1,0:T(8,128)(2,1)S(1)}, bf16[96,512]{1,0:T(8,128)(2,1)S(1)}, u32[]{:S(2)}, u32[]{:S(2)}) collective-permute-start(bf16[96,512]{1,0:T(8,128)(2,1)S(1)} %get-tuple-element.74), channel_id=1, source_target_pairs={{0,2},{1,3},{2,0},{3,1},{4,6},{5,7},{6,4},{7,5},{8,10},{9,11},{10,... | collective-permute-start | bytes 294920 | tf_op jit(solution)/shard_map/ppermute | solution.py:314
  89.6 28.9 %collective-permute-start.19 = (bf16[48,3584]{1,0:T(8,128)(2,1)S(1)}, bf16[48,3584]{1,0:T(8,128)(2,1)S(1)}, u32[]{:S(2)}, u32[]{:S(2)}) collective-permute-start(bf16[48,3584]{1,0:T(8,128)(2,1)S(1)} %get-tuple-element.82), channel_id=1, source_target_pairs={{0,12},{1,13},{2,14},{3,15},{4,0},{5,1},{6,2},{7,3},{8,4},{9,5},{1... | collective-permute-start | bytes 1032200 | tf_op jit(solution)/shard_map/ppermute | solution.py:310
  90.1 35.1 %collective-permute-start.23 = (bf16[48,3584]{1,0:T(8,128)(2,1)S(1)}, bf16[48,3584]{1,0:T(8,128)(2,1)S(1)}, u32[]{:S(2)}, u32[]{:S(2)}) collective-permute-start(bf16[48,3584]{1,0:T(8,128)(2,1)S(1)} %get-tuple-element.90), channel_id=1, source_target_pairs={{0,4},{1,5},{2,6},{3,7},{4,8},{5,9},{6,10},{7,11},{8,12},{9,13},{1... | collective-permute-start | bytes 1032200 | tf_op jit(solution)/shard_map/ppermute | solution.py:310
  95.7 6.6 %collective-permute-start.24 = (bf16[192,512]{1,0:T(8,128)(2,1)S(1)}, bf16[192,512]{1,0:T(8,128)(2,1)S(1)}, u32[]{:S(2)}, u32[]{:S(2)}) collective-permute-start(bf16[192,512]{1,0:T(8,128)(2,1)S(1)} %get-tuple-element.98), channel_id=1, source_target_pairs={{0,2},{1,3},{2,0},{3,1},{4,6},{5,7},{6,4},{7,5},{8,10},{9,11},{10,... | collective-permute-start | bytes 589832 | tf_op jit(solution)/shard_map/ppermute | solution.py:314
  100.0 31.7 %collective-permute-start.22 = (bf16[48,3584]{1,0:T(8,128)(2,1)S(1)}, bf16[48,3584]{1,0:T(8,128)(2,1)S(1)}, u32[]{:S(2)}, u32[]{:S(2)}) collective-permute-start(bf16[48,3584]{1,0:T(8,128)(2,1)S(1)} %get-tuple-element.88), channel_id=1, source_target_pairs={{0,8},{1,9},{2,10},{3,11},{4,12},{5,13},{6,14},{7,15},{8,0},{9,1},... | collective-permute-start | bytes 1032200 | tf_op jit(solution)/shard_map/ppermute | solution.py:310
  106.7 11.1 %collective-permute-start.28 = (bf16[48,3584]{1,0:T(8,128)(2,1)S(1)}, bf16[48,3584]{1,0:T(8,128)(2,1)S(1)}, u32[]{:S(2)}, u32[]{:S(2)}) collective-permute-start(bf16[48,3584]{1,0:T(8,128)(2,1)S(1)} %get-tuple-element.107), channel_id=1, source_target_pairs={{0,2},{1,3},{2,0},{3,1},{4,6},{5,7},{6,4},{7,5},{8,10},{9,11},{10,... | collective-permute-start | bytes 1032200 | tf_op jit(solution)/shard_map/ppermute | solution.py:314
  107.4 17.8 %collective-permute-start.25 = (bf16[48,3584]{1,0:T(8,128)(2,1)S(1)}, bf16[48,3584]{1,0:T(8,128)(2,1)S(1)}, u32[]{:S(2)}, u32[]{:S(2)}) collective-permute-start(bf16[48,3584]{1,0:T(8,128)(2,1)S(1)} %get-tuple-element.101), channel_id=1, source_target_pairs={{0,2},{1,3},{2,0},{3,1},{4,6},{5,7},{6,4},{7,5},{8,10},{9,11},{10,... | collective-permute-start | bytes 1032200 | tf_op jit(solution)/shard_map/ppermute | solution.py:314
  117.8 13.9 %collective-permute-start.30 = (bf16[48,3584]{1,0:T(8,128)(2,1)S(1)}, bf16[48,3584]{1,0:T(8,128)(2,1)S(1)}, u32[]{:S(2)}, u32[]{:S(2)}) collective-permute-start(bf16[48,3584]{1,0:T(8,128)(2,1)S(1)} %get-tuple-element.111), channel_id=1, source_target_pairs={{0,2},{1,3},{2,0},{3,1},{4,6},{5,7},{6,4},{7,5},{8,10},{9,11},{10,... | collective-permute-start | bytes 1032200 | tf_op jit(solution)/shard_map/ppermute | solution.py:314
  118.5 22.0 %collective-permute-start.29 = (bf16[48,3584]{1,0:T(8,128)(2,1)S(1)}, bf16[48,3584]{1,0:T(8,128)(2,1)S(1)}, u32[]{:S(2)}, u32[]{:S(2)}) collective-permute-start(bf16[48,3584]{1,0:T(8,128)(2,1)S(1)} %add_rows.6), channel_id=1, source_target_pairs={{0,8},{1,9},{2,10},{3,11},{4,12},{5,13},{6,14},{7,15},{8,0},{9,1},... | collective-permute-start | bytes 1032200 | tf_op jit(solution)/shard_map/ppermute | solution.py:310
  125.2 10.1 %collective-permute-start.26 = (bf16[48,3584]{1,0:T(8,128)(2,1)S(1)}, bf16[48,3584]{1,0:T(8,128)(2,1)S(1)}, u32[]{:S(2)}, u32[]{:S(2)}) collective-permute-start(bf16[48,3584]{1,0:T(8,128)(2,1)S(1)} %get-tuple-element.102), channel_id=1, source_target_pairs={{0,2},{1,3},{2,0},{3,1},{4,6},{5,7},{6,4},{7,5},{8,10},{9,11},{10,... | collective-permute-start | bytes 1032200 | tf_op jit(solution)/shard_map/ppermute | solution.py:314
  125.9 23.1 %collective-permute-start.27 = (bf16[48,3584]{1,0:T(8,128)(2,1)S(1)}, bf16[48,3584]{1,0:T(8,128)(2,1)S(1)}, u32[]{:S(2)}, u32[]{:S(2)}) collective-permute-start(bf16[48,3584]{1,0:T(8,128)(2,1)S(1)} %add_rows.5), channel_id=1, source_target_pairs={{0,12},{1,13},{2,14},{3,15},{4,0},{5,1},{6,2},{7,3},{8,4},{9,5},{1... | collective-permute-start | bytes 1032200 | tf_op jit(solution)/shard_map/ppermute | solution.py:310
  131.6 0.7 copy-start.13
  131.7 17.2 %collective-permute-start.31 = (bf16[48,3584]{1,0:T(8,128)(2,1)S(1)}, bf16[48,3584]{1,0:T(8,128)(2,1)S(1)}, u32[]{:S(2)}, u32[]{:S(2)}) collective-permute-start(bf16[48,3584]{1,0:T(8,128)(2,1)S(1)} %add_rows.7), channel_id=1, source_target_pairs={{0,4},{1,5},{2,6},{3,7},{4,8},{5,9},{6,10},{7,11},{8,12},{9,13},{1... | collective-permute-start | bytes 1032200 | tf_op jit(solution)/shard_map/ppermute | solution.py:310
  135.3 13.6 %copy-start.7 = (bf16[1,128,3584]{2,1,0:T(8,128)(2,1)S(1)}, bf16[1,128,3584]{2,1,0:T(8,128)(2,1)}, u32[]{:S(2)}) copy-start(bf16[1,128,3584]{2,1,0:T(8,128)(2,1)} %copy-done.6) | copy-start | bytes 2752516

commit v4 on v3

--- a/solution.py
+++ b/solution.py
@@ -257,18 +257,26 @@
     pl.when(at_ref[2] == 0)(lambda: finish(far))
 
 
-def backward_end_kernel(experts, capacity, at_ref, ids, near, far, *refs):
-    back, out = refs[:experts], refs[experts]
+def backward_most_kernel(ks, experts, capacity, at_ref, ids, near, far, *refs):
+    back, out = dict(zip(ks, refs)), refs[-1]
     layout = tokens_by_slots(ids[...], at_ref[0], experts, capacity)
 
     def finish(tokens):
         for cols in pieces(near.shape[1]):
-            rows = dot(layout, stacked([ref[:, cols] for ref in back]))
-            start = tokens[:, cols].astype(F32)
-            out[:, cols] = (start + rows).astype(BF16)
+            empty = jnp.zeros((capacity, COLS), BF16)
+            rows = dot(layout, stacked([back[k][:, cols] if k in back else empty for k in range(experts)]))
+            out[:, cols] = (tokens[:, cols].astype(F32) + rows).astype(BF16)
 
     pl.when(at_ref[1] == 1)(lambda: finish(near))
     pl.when(at_ref[1] == 0)(lambda: finish(far))
+
+
+def backward_end_kernel(k, experts, capacity, at_ref, ids, most, back, out):
+    slot = slot_of(column(ids[...]), at_ref[0], experts, capacity, 0) - k * capacity
+    wide = (slot.shape[0], capacity)
+    layout = jnp.where(lax.broadcasted_iota(jnp.int32, wide, 1) == slot, 1.0, 0.0).astype(BF16)
+    for cols in pieces(most.shape[1]):
+        out[:, cols] = (most[:, cols].astype(F32) + dot(layout, back[:, cols])).astype(BF16)
 
 
 def body(
@@ -460,12 +468,21 @@
         in_specs=[SMEM] + [VMEM] * (5 + experts),
         scratch=[pltpu.VMEM((tokens, width), F32)],
     )
+    final = [k for k in order if k][-1]
+    ks = [k for k in range(experts) if k != final]
+    backward_most = call(
+        functools.partial(backward_most_kernel, ks, experts, capacity),
+        "backward_most",
+        [shape(tokens, width)],
+        (at, b_ids, loss_cotangent, returning, *(backward_back[k] for k in ks)),
+        in_specs=[SMEM] + [VMEM] * (3 + len(ks)),
+    )[0]
     backward_out = call(
-        functools.partial(backward_end_kernel, experts, capacity),
+        functools.partial(backward_end_kernel, final, experts, capacity),
         "backward_end",
         [shape(tokens, width)],
-        (at, b_ids, loss_cotangent, returning, *(backward_back[k] for k in range(experts))),
-        in_specs=[SMEM] + [VMEM] * (3 + experts),
+        (at, b_ids, backward_most, backward_back[final]),
+        in_specs=[SMEM] + [VMEM] * 3,
     )[0]
     return (forward_out[None], coefficient, backward_out[None])
 

time: 151 us -> 158 us (1.046)
  waiting for transfers between devices: 74 us -> 79.9 us
    ppermute x12, waiting for transfers between devices: 18.7 us -> 25 us  [to_plane(): return lax.ppermute(value, 'expert', pairs)]
    pallas_call x17 -> x18, Pallas kernels: 37.9 us -> 39.2 us  [call(): pl.pallas_call(kernel, out_shape=outs, in_specs=in_specs, out_specs=out_s...]
  transfers between devices with their start and end apart: 32 -> 32, of which waited for: 14 -> 15; matrix products, arithmetic and copies ran while one was open for 1% -> 1% of each run, Pallas kernels for 24% -> 23%
where the time goes in v4:
time: 158 us
  waiting for transfers between devices  79.9 us (51%)
  Pallas kernels  39.2 us (25%)
  starting transfers between devices  37.1 us (23%)
    ppermute x12, waiting for transfers between devices, to_chip(): return lax.ppermute(value, 'expert', pairs)  40.9 us
    pallas_call x18, Pallas kernels, call(): pl.pallas_call(kernel, out_shape=outs, in_specs=in_specs, out_specs=out_s...  39.2 us
    ppermute x12, waiting for transfers between devices, to_plane(): return lax.ppermute(value, 'expert', pairs)  25 us
    ppermute x12, starting transfers between devices, to_plane(): return lax.ppermute(value, 'expert', pairs)  18 us
    ppermute x2, waiting for transfers between devices, shifted(): return lax.ppermute(value, axis, pairs)  14 us
    ppermute x12, starting transfers between devices, to_chip(): return lax.ppermute(value, 'expert', pairs)  13.1 us
    ppermute x2, starting transfers between devices, shifted(): return lax.ppermute(value, axis, pairs)  4.75 us
  transfers between devices with their start and end apart: 32, of which 15 were waited for; matrix products, arithmetic and copies ran while one was open for 1% of the time, Pallas kernels for 23%

profile of v4, /device:TPU:8, one launch (start us, length us, event | category | flops | bytes accessed | tf_op | source)
XLA Modules:
  0.0 158.2 jit_solution(4932936862152093486)
XLA Ops:
  0.6 0.1 collective-permute-start.2
  0.7 0.5 collective-permute-start.3
  1.2 0.1 collective-permute-start.4
  1.3 3.5 %collective-permute-start = (bf16[1,128,3584]{2,1,0:T(8,128)(2,1)}, bf16[1,128,3584]{2,1,0:T(8,128)(2,1)S(1)}, u32[]{:S(2)}, u32[]{:S(2)}) collective-permute-start(bf16[1,128,3584]{2,1,0:T(8,128)(2,1)} %param.15), channel_id=1, source_target_pairs={{0,16},{1,17},{2,18},{3,19},{4,20},{5,21},{6,22},{7,23},{8,24},{9,... | collective-permute-start | bytes 2752520 | tf_op jit(solution)/shard_map/ppermute | solution.py:43
  4.8 1.6 collective-permute-start.15
  6.3 0.7 stack.31.at_ref
  7.0 1.3 collective-permute-start.1
  8.3 3.0 %first_rows.1 = bf16[48,3584]{1,0:T(8,128)(2,1)} custom-call(s32[5]{0:T(128)} %stack.31.at_ref, s32[1,128]{1,0:T(1,128)} %bitcast.37, s32[1,128]{1,0:T(1,128)} %bitcast.40, bf16[128,3584]{1,0:T(8,128)(2,1)} %near.6, bf16[128,3584]{1,0:T(8,128)(2,1)} %near.7, f32[1,128]{1,0:T(1,128)} %b_weight.1, f32[1,3584]{1,0:T(1,128)} %steer.5), custom_call_target="tpu_custom_call" | custom-call | flops 5000000000 | bytes 100000 | tf_op jit(solution)/shard_map/first_rows/pallas_call | solution.py:48
  11.3 2.6 %collective-permute-start.5 = (bf16[48,3584]{1,0:T(8,128)(2,1)}, bf16[48,3584]{1,0:T(8,128)(2,1)S(1)}, u32[]{:S(2)}, u32[]{:S(2)}) collective-permute-start(bf16[48,3584]{1,0:T(8,128)(2,1)} %first_rows.1), channel_id=1, source_target_pairs={{0,8},{1,9},{2,10},{3,11},{4,12},{5,13},{6,14},{7,15},{8,0},{9,1},... | collective-permute-start | bytes 1032200 | tf_op jit(solution)/shard_map/ppermute | solution.py:318
  13.9 11.3 %collective-permute-done = bf16[1,128,3584]{2,1,0:T(8,128)(2,1)S(1)} collective-permute-done((bf16[1,128,3584]{2,1,0:T(8,128)(2,1)}, bf16[1,128,3584]{2,1,0:T(8,128)(2,1)S(1)}, u32[]{:S(2)}, u32[]{:S(2)}) %collective-permute-start) | collective-permute-done | bytes 917536 | tf_op jit(solution)/shard_map/ppermute | solution.py:43
  25.3 1.2 forward_rows.1
  26.5 1.6 %collective-permute-start.8 = (bf16[48,3584]{1,0:T(8,128)(2,1)S(1)}, bf16[48,3584]{1,0:T(8,128)(2,1)S(1)}, u32[]{:S(2)}, u32[]{:S(2)}) collective-permute-start(bf16[48,3584]{1,0:T(8,128)(2,1)S(1)} %get-tuple-element.68), channel_id=1, source_target_pairs={{0,4},{1,5},{2,6},{3,7},{4,8},{5,9},{6,10},{7,11},{8,12},{9,13},{1... | collective-permute-start | bytes 1032200 | tf_op jit(solution)/shard_map/ppermute | solution.py:318
  28.1 0.4 collective-permute-start.11
  28.6 2.7 %collective-permute-done.1 = bf16[1,128,3584]{2,1,0:T(8,128)(2,1)S(1)} collective-permute-done((bf16[1,128,3584]{2,1,0:T(8,128)(2,1)}, bf16[1,128,3584]{2,1,0:T(8,128)(2,1)S(1)}, u32[]{:S(2)}, u32[]{:S(2)}) %collective-permute-start.1) | collective-permute-done | bytes 917536 | tf_op jit(solution)/shard_map/ppermute | solution.py:43
  31.3 1.6 %backward_rows.1 = (bf16[48,3584]{1,0:T(8,128)(2,1)S(1)}, bf16[48,3584]{1,0:T(8,128)(2,1)S(1)}, bf16[48,3584]{1,0:T(8,128)(2,1)S(1)}, bf16[48,3584]{1,0:T(8,128)(2,1)S(1)}) custom-call(s32[5]{0:T(128)S(1)} %copy-done, s32[1,128]{1,0:T(1,128)S(1)} %bitcast.41, bf16[128,3584]{1,0:T(8,128)(2,1)S(1)} %copy-done.5, f32[1,128]{1,0:T(1,128)S(1)} %copy-done.11, ...), custom_call_target="tpu_custom_call" | custom-call | flops 5000000000 | bytes 100000 | tf_op jit(solution)/shard_map/backward_rows/pallas_call | solution.py:48
  32.9 1.3 saved_rows.1
  34.3 0.1 collective-permute-start.7
  34.3 12.8 %collective-permute-done.15.refs_0_.refs_6_ = bf16[256,3584]{1,0:T(8,128)(2,1)S(1)} collective-permute-done((bf16[256,3584]{1,0:T(8,128)(2,1)}, bf16[256,3584]{1,0:T(8,128)(2,1)S(1)}, u32[]{:S(2)}, u32[]{:S(2)}) %collective-permute-start.15) | collective-permute-done | bytes 1835040 | tf_op jit(solution)/shard_map/ppermute | solution.py:322
  47.2 2.7 %collective-permute-start.6 = (bf16[48,3584]{1,0:T(8,128)(2,1)S(1)}, bf16[48,3584]{1,0:T(8,128)(2,1)S(1)}, u32[]{:S(2)}, u32[]{:S(2)}) collective-permute-start(bf16[48,3584]{1,0:T(8,128)(2,1)S(1)} %get-tuple-element.62), channel_id=1, source_target_pairs={{0,8},{1,9},{2,10},{3,11},{4,12},{5,13},{6,14},{7,15},{8,0},{9,1},... | collective-permute-start | bytes 1032200 | tf_op jit(solution)/shard_map/ppermute | solution.py:318
  49.8 1.5 collective-permute-start.12
  51.3 0.1 fusion
  51.4 0.1 collective-permute-start.17
  51.5 0.5 collective-permute-start.16
  52.0 0.5 collective-permute-start.9
  52.5 8.3 %collective-permute-done.12.refs_3_ = bf16[48,3584]{1,0:T(8,128)(2,1)S(1)} collective-permute-done((bf16[48,3584]{1,0:T(8,128)(2,1)S(1)}, bf16[48,3584]{1,0:T(8,128)(2,1)S(1)}, u32[]{:S(2)}, u32[]{:S(2)}) %collective-permute-start.12) | collective-permute-done | bytes 344096 | tf_op jit(solution)/shard_map/ppermute | solution.py:322
  60.8 1.5 collective-permute-start.13
  62.3 1.6 %collective-permute-done.6 = bf16[48,3584]{1,0:T(8,128)(2,1)S(1)} collective-permute-done((bf16[48,3584]{1,0:T(8,128)(2,1)S(1)}, bf16[48,3584]{1,0:T(8,128)(2,1)S(1)}, u32[]{:S(2)}, u32[]{:S(2)}) %collective-permute-start.6) | collective-permute-done | bytes 344096 | tf_op jit(solution)/shard_map/ppermute | solution.py:318
  63.9 4.2 %collective-permute-done.9.refs_2_ = bf16[48,3584]{1,0:T(8,128)(2,1)S(1)} collective-permute-done((bf16[48,3584]{1,0:T(8,128)(2,1)S(1)}, bf16[48,3584]{1,0:T(8,128)(2,1)S(1)}, u32[]{:S(2)}, u32[]{:S(2)}) %collective-permute-start.9) | collective-permute-done | bytes 344096 | tf_op jit(solution)/shard_map/ppermute | solution.py:322
  68.2 1.5 collective-permute-start.10
  69.7 3.7 %hidden.3 = (bf16[96,512]{1,0:T(8,128)(2,1)S(1)}, bf16[96,512]{1,0:T(8,128)(2,1)S(1)}) custom-call(bf16[48,3584]{1,0:T(8,128)(2,1)S(1)} %collective-permute-done.8.refs_0_, bf16[48,3584]{1,0:T(8,128)(2,1)S(1)} %collective-permute-done.11.refs_1_, bf16[48,3584]{1,0:T(8,128)(2,1)S(1)} %collective-permute-done.9.refs_2_, ...), custom_call_target="tpu_custom_call" | custom-call | flops 5000000000 | bytes 100000 | tf_op jit(solution)/shard_map/hidden/pallas_call | solution.py:48
  73.3 3.6 %collective-permute-done.20.refs_1_ = bf16[48,3584]{1,0:T(8,128)(2,1)S(1)} collective-permute-done((bf16[48,3584]{1,0:T(8,128)(2,1)S(1)}, bf16[48,3584]{1,0:T(8,128)(2,1)S(1)}, u32[]{:S(2)}, u32[]{:S(2)}) %collective-permute-start.20) | collective-permute-done | bytes 344096 | tf_op jit(solution)/shard_map/ppermute | solution.py:318
  76.9 2.8 %collective-permute-start.21 = (bf16[48,3584]{1,0:T(8,128)(2,1)S(1)}, bf16[48,3584]{1,0:T(8,128)(2,1)S(1)}, u32[]{:S(2)}, u32[]{:S(2)}) collective-permute-start(bf16[48,3584]{1,0:T(8,128)(2,1)S(1)} %get-tuple-element.87), channel_id=1, source_target_pairs={{0,12},{1,13},{2,14},{3,15},{4,0},{5,1},{6,2},{7,3},{8,4},{9,5},{1... | collective-permute-start | bytes 1032200 | tf_op jit(solution)/shard_map/ppermute | solution.py:318
  79.8 1.2 collective-permute-done.10.refs_2_
  81.0 1.5 collective-permute-start.18
  82.4 3.7 %hidden.2 = (bf16[96,512]{1,0:T(8,128)(2,1)S(1)}, bf16[96,512]{1,0:T(8,128)(2,1)S(1)}) custom-call(bf16[48,3584]{1,0:T(8,128)(2,1)S(1)} %get-tuple-element.69.refs_0_, bf16[48,3584]{1,0:T(8,128)(2,1)S(1)} %get-tuple-element.71.refs_1_, bf16[48,3584]{1,0:T(8,128)(2,1)S(1)} %collective-permute-done.10.refs_2_, ...), custom_call_target="tpu_custom_call" | custom-call | flops 5000000000 | bytes 100000 | tf_op jit(solution)/shard_map/hidden/pallas_call | solution.py:48
  86.1 0.6 collective-permute-start.14
  86.8 2.8 %expert_out.3 = (bf16[48,3584]{1,0:T(8,128)(2,1)S(1)}, bf16[48,3584]{1,0:T(8,128)(2,1)S(1)}) custom-call(bf16[96,512]{1,0:T(8,128)(2,1)S(1)} %get-tuple-element.78.own, bf16[96,512]{1,0:T(8,128)(2,1)S(1)} %collective-permute-done.18.other, bf16[256,3584]{1,0:T(8,128)(2,1)S(1)} %bitcast.18, bf16[256,3584]{1,0:T(8,128)(2,1)} %collective-permute-done.4.d1.refs_5_, ...), custom_call_target="tpu_custom_call" | custom-call | flops 5000000000 | bytes 100000 | tf_op jit(solution)/shard_map/expert_out/pallas_call | solution.py:48
  89.5 0.5 collective-permute-start.19
  90.0 1.6 collective-permute-start.23
  91.6 2.8 %expert_out.2 = (bf16[48,3584]{1,0:T(8,128)(2,1)S(1)}, bf16[48,3584]{1,0:T(8,128)(2,1)S(1)}) custom-call(bf16[96,512]{1,0:T(8,128)(2,1)S(1)} %get-tuple-element.72.own, bf16[96,512]{1,0:T(8,128)(2,1)S(1)} %collective-permute-done.14.other, bf16[256,3584]{1,0:T(8,128)(2,1)S(1)} %bitcast.19, bf16[256,3584]{1,0:T(8,128)(2,1)} %collective-permute-done.4.d1.refs_5_, ...), custom_call_target="tpu_custom_call" | custom-call | flops 5000000000 | bytes 100000 | tf_op jit(solution)/shard_map/expert_out/pallas_call | solution.py:48
  94.4 4.0 %grad_hidden.1 = (f32[192,512]{1,0:T(8,128)S(1)}, bf16[192,512]{1,0:T(8,128)(2,1)S(1)}) custom-call(bf16[48,3584]{1,0:T(8,128)(2,1)S(1)} %get-tuple-element.93.refs_0_, bf16[48,3584]{1,0:T(8,128)(2,1)S(1)} %collective-permute-done.20.refs_1_, bf16[48,3584]{1,0:T(8,128)(2,1)S(1)} %get-tuple-element.115.refs_2_, ...), custom_call_target="tpu_custom_call" | custom-call | flops 5000000000 | bytes 100000 | tf_op jit(solution)/shard_map/grad_hidden/pallas_call | solution.py:48
  98.5 1.5 collective-permute-start.24
  100.0 2.2 %collective-permute-start.22 = (bf16[48,3584]{1,0:T(8,128)(2,1)S(1)}, bf16[48,3584]{1,0:T(8,128)(2,1)S(1)}, u32[]{:S(2)}, u32[]{:S(2)}) collective-permute-start(bf16[48,3584]{1,0:T(8,128)(2,1)S(1)} %get-tuple-element.88), channel_id=1, source_target_pairs={{0,8},{1,9},{2,10},{3,11},{4,12},{5,13},{6,14},{7,15},{8,0},{9,1},... | collective-permute-start | bytes 1032200 | tf_op jit(solution)/shard_map/ppermute | solution.py:318
  102.2 4.5 %grad_rows.2 = (f32[48,3584]{1,0:T(8,128)S(1)}, f32[48,3584]{1,0:T(8,128)S(1)}, f32[48,3584]{1,0:T(8,128)S(1)}, f32[48,3584]{1,0:T(8,128)S(1)}) custom-call(f32[192,512]{1,0:T(8,128)S(1)} %get-tuple-element.94.grads, bf16[384,512]{1,0:T(8,128)(2,1)S(1)} %get-tuple-element.95.kept, bf16[384,512]{1,0:T(8,128)(2,1)S(1)} %collective-permute-done.7.got, ...), custom_call_target="tpu_custom_call" | custom-call | flops 10000000000 | bytes 100000 | tf_op jit(solution)/shard_map/grad_rows/pallas_call | solution.py:48
  106.6 4.5 %grad_rows.3 = (bf16[48,3584]{1,0:T(8,128)(2,1)S(1)}, bf16[48,3584]{1,0:T(8,128)(2,1)S(1)}, bf16[48,3584]{1,0:T(8,128)(2,1)S(1)}, bf16[48,3584]{1,0:T(8,128)(2,1)S(1)}) custom-call(bf16[192,512]{1,0:T(8,128)(2,1)S(1)} %collective-permute-done.24.grads, bf16[384,512]{1,0:T(8,128)(2,1)S(1)} %get-tuple-element.95.kept, ...), custom_call_target="tpu_custom_call" | custom-call | flops 10000000000 | bytes 100000 | tf_op jit(solution)/shard_map/grad_rows/pallas_call | solution.py:48
  111.1 0.6 collective-permute-start.28
  111.7 1.5 collective-permute-start.25
  113.2 4.9 %collective-permute-done.22.refs_2_ = bf16[48,3584]{1,0:T(8,128)(2,1)S(1)} collective-permute-done((bf16[48,3584]{1,0:T(8,128)(2,1)S(1)}, bf16[48,3584]{1,0:T(8,128)(2,1)S(1)}, u32[]{:S(2)}, u32[]{:S(2)}) %collective-permute-start.22) | collective-permute-done | bytes 344096 | tf_op jit(solution)/shard_map/ppermute | solution.py:318
  118.2 2.6 %forward_end.1 = (bf16[128,3584]{1,0:T(8,128)(2,1)}, f32[1,128]{1,0:T(1,128)}) custom-call(s32[5]{0:T(128)S(1)} %copy-done, s32[1,128]{1,0:T(1,128)S(1)} %bitcast.39, bf16[128,3584]{1,0:T(8,128)(2,1)S(1)} %copy-done.4, bf16[128,3584]{1,0:T(8,128)(2,1)S(1)} %bitcast.32, f32[1,128]{1,0:T(1,128)S(1)} %copy-done.13, f32[1,3584]{1,0:T(1,128)S(1)} %copy-done.10, ...), custom_call_target="tpu_custom_call" | custom-call | flops 49999998976 | bytes 100000 | tf_op jit(solution)/shard_map/forward_end/pallas_call | solution.py:48
  120.7 0.6 collective-permute-done.28.theirs
  121.3 0.8 collective-permute-start.30
  122.1 0.1 add_rows.6
  122.2 3.5 %collective-permute-start.29 = (bf16[48,3584]{1,0:T(8,128)(2,1)S(1)}, bf16[48,3584]{1,0:T(8,128)(2,1)S(1)}, u32[]{:S(2)}, u32[]{:S(2)}) collective-permute-start(bf16[48,3584]{1,0:T(8,128)(2,1)S(1)} %add_rows.6), channel_id=1, source_target_pairs={{0,8},{1,9},{2,10},{3,11},{4,12},{5,13},{6,14},{7,15},{8,0},{9,1},... | collective-permute-start | bytes 1032200 | tf_op jit(solution)/shard_map/ppermute | solution.py:318
  125.6 0.9 collective-permute-done.25.theirs
  126.6 0.1 add_rows.5
  126.7 0.1 collective-permute-start.27
  126.7 7.2 %collective-permute-done.30.theirs = bf16[48,3584]{1,0:T(8,128)(2,1)S(1)} collective-permute-done((bf16[48,3584]{1,0:T(8,128)(2,1)S(1)}, bf16[48,3584]{1,0:T(8,128)(2,1)S(1)}, u32[]{:S(2)}, u32[]{:S(2)}) %collective-permute-start.30) | collective-permute-done | bytes 344096 | tf_op jit(solution)/shard_map/ppermute | solution.py:322
  134.0 0.1 add_rows.7
  134.1 5.6 %collective-permute-done.26.theirs = bf16[48,3584]{1,0:T(8,128)(2,1)S(1)} collective-permute-done((bf16[48,3584]{1,0:T(8,128)(2,1)S(1)}, bf16[48,3584]{1,0:T(8,128)(2,1)S(1)}, u32[]{:S(2)}, u32[]{:S(2)}) %collective-permute-start.26) | collective-permute-done | bytes 344096 | tf_op jit(solution)/shard_map/ppermute | solution.py:322
  139.7 0.1 add_rows.4.refs_0_
  139.8 5.4 %collective-permute-done.29.refs_2_ = bf16[48,3584]{1,0:T(8,128)(2,1)S(1)} collective-permute-done((bf16[48,3584]{1,0:T(8,128)(2,1)S(1)}, bf16[48,3584]{1,0:T(8,128)(2,1)S(1)}, u32[]{:S(2)}, u32[]{:S(2)}) %collective-permute-start.29) | collective-permute-done | bytes 344096 | tf_op jit(solution)/shard_map/ppermute | solution.py:318
  145.2 9.5 %collective-permute-done.27.refs_1_ = bf16[48,3584]{1,0:T(8,128)(2,1)S(1)} collective-permute-done((bf16[48,3584]{1,0:T(8,128)(2,1)S(1)}, bf16[48,3584]{1,0:T(8,128)(2,1)S(1)}, u32[]{:S(2)}, u32[]{:S(2)}) %collective-permute-start.27) | collective-permute-done | bytes 344096 | tf_op jit(solution)/shard_map/ppermute | solution.py:318
  154.7 1.3 backward_most.1.most
  156.0 2.2 %backward_end.1 = bf16[128,3584]{1,0:T(8,128)(2,1)} custom-call(s32[5]{0:T(128)S(1)} %copy-done, s32[1,128]{1,0:T(1,128)S(1)} %bitcast.43, bf16[128,3584]{1,0:T(8,128)(2,1)S(1)} %backward_most.1.most, bf16[48,3584]{1,0:T(8,128)(2,1)S(1)} %collective-permute-done.31.back), custom_call_target="tpu_custom_call" | custom-call | flops 5000000000 | bytes 100000 | tf_op jit(solution)/shard_map/backward_end/pallas_call | solution.py:48
  (51 shorter events, 0.2 us)
Async XLA Ops:
  0.6 6.4 %collective-permute-start.2 = (bf16[3584,256]{1,0:T(8,128)(2,1)}, bf16[3584,256]{1,0:T(8,128)(2,1)}, u32[]{:S(2)}, u32[]{:S(2)}) collective-permute-start(bf16[3584,256]{1,0:T(8,128)(2,1)} %bitcast.21), channel_id=1, source_target_pairs={{0,1},{1,0},{2,3},{3,2},{4,5},{5,4},{6,7},{7,6},{8,9},{9,8},{10,11... | collective-permute-start | bytes 5505032 | tf_op jit(solution)/shard_map/ppermute | solution.py:325
  0.7 10.6 %collective-permute-start.3 = (bf16[3584,256]{1,0:T(8,128)(2,1)}, bf16[3584,256]{1,0:T(8,128)(2,1)}, u32[]{:S(2)}, u32[]{:S(2)}) collective-permute-start(bf16[3584,256]{1,0:T(8,128)(2,1)} %bitcast.26), channel_id=1, source_target_pairs={{0,1},{1,0},{2,3},{3,2},{4,5},{5,4},{6,7},{7,6},{8,9},{9,8},{10,11... | collective-permute-start | bytes 5505032 | tf_op jit(solution)/shard_map/ppermute | solution.py:325
  1.2 12.7 %collective-permute-start.4 = (bf16[256,3584]{1,0:T(8,128)(2,1)}, bf16[256,3584]{1,0:T(8,128)(2,1)}, u32[]{:S(2)}, u32[]{:S(2)}) collective-permute-start(bf16[256,3584]{1,0:T(8,128)(2,1)} %bitcast.16), channel_id=1, source_target_pairs={{0,1},{1,0},{2,3},{3,2},{4,5},{5,4},{6,7},{7,6},{8,9},{9,8},{10,11... | collective-permute-start | bytes 5505032 | tf_op jit(solution)/shard_map/ppermute | solution.py:325
  1.3 23.9 %collective-permute-start = (bf16[1,128,3584]{2,1,0:T(8,128)(2,1)}, bf16[1,128,3584]{2,1,0:T(8,128)(2,1)S(1)}, u32[]{:S(2)}, u32[]{:S(2)}) collective-permute-start(bf16[1,128,3584]{2,1,0:T(8,128)(2,1)} %param.15), channel_id=1, source_target_pairs={{0,16},{1,17},{2,18},{3,19},{4,20},{5,21},{6,22},{7,23},{8,24},{9,... | collective-permute-start | bytes 2752520 | tf_op jit(solution)/shard_map/ppermute | solution.py:43
  4.8 42.4 %collective-permute-start.15 = (bf16[256,3584]{1,0:T(8,128)(2,1)}, bf16[256,3584]{1,0:T(8,128)(2,1)S(1)}, u32[]{:S(2)}, u32[]{:S(2)}) collective-permute-start(bf16[256,3584]{1,0:T(8,128)(2,1)} %bitcast.17), channel_id=1, source_target_pairs={{0,2},{1,3},{2,0},{3,1},{4,6},{5,7},{6,4},{7,5},{8,10},{9,11},{10,... | collective-permute-start | bytes 5505032 | tf_op jit(solution)/shard_map/ppermute | solution.py:322
  7.0 24.2 %collective-permute-start.1 = (bf16[1,128,3584]{2,1,0:T(8,128)(2,1)}, bf16[1,128,3584]{2,1,0:T(8,128)(2,1)S(1)}, u32[]{:S(2)}, u32[]{:S(2)}) collective-permute-start(bf16[1,128,3584]{2,1,0:T(8,128)(2,1)} %param.19), channel_id=1, source_target_pairs={{16,0},{17,1},{18,2},{19,3},{20,4},{21,5},{22,6},{23,7},{24,8},{25... | collective-permute-start | bytes 2752520 | tf_op jit(solution)/shard_map/ppermute | solution.py:43
  8.3 16.9 %copy-start = (s32[5]{0:T(128)S(1)}, s32[5]{0:T(128)}, u32[]{:S(2)}) copy-start(s32[5]{0:T(128)} %stack.31.at_ref) | copy-start | bytes 64
  8.3 16.9 %copy-start.4 = (bf16[128,3584]{1,0:T(8,128)(2,1)S(1)}, bf16[128,3584]{1,0:T(8,128)(2,1)}, u32[]{:S(2)}) copy-start(bf16[128,3584]{1,0:T(8,128)(2,1)} %near.6) | copy-start | bytes 2752516
  8.3 16.9 %copy-start.12 = (s32[1,128,1]{1,2,0:T(1,128)S(1)}, s32[1,128,1]{1,2,0:T(1,128)}, u32[]{:S(2)}) copy-start(s32[1,128,1]{1,2,0:T(1,128)} %param.16) | copy-start | bytes 1540
  11.3 35.9 %collective-permute-start.5 = (bf16[48,3584]{1,0:T(8,128)(2,1)}, bf16[48,3584]{1,0:T(8,128)(2,1)S(1)}, u32[]{:S(2)}, u32[]{:S(2)}) collective-permute-start(bf16[48,3584]{1,0:T(8,128)(2,1)} %first_rows.1), channel_id=1, source_target_pairs={{0,8},{1,9},{2,10},{3,11},{4,12},{5,13},{6,14},{7,15},{8,0},{9,1},... | collective-permute-start | bytes 1032200 | tf_op jit(solution)/shard_map/ppermute | solution.py:318
  25.2 6.0 %copy-start.5 = (bf16[128,3584]{1,0:T(8,128)(2,1)S(1)}, bf16[128,3584]{1,0:T(8,128)(2,1)}, u32[]{:S(2)}) copy-start(bf16[128,3584]{1,0:T(8,128)(2,1)} %near.7) | copy-start | bytes 2752516
  25.2 6.0 %copy-start.10 = (f32[1,3584]{1,0:T(1,128)S(1)}, f32[1,3584]{1,0:T(1,128)}, u32[]{:S(2)}) copy-start(f32[1,3584]{1,0:T(1,128)} %steer.5) | copy-start | bytes 43012
  25.2 6.0 %copy-start.11 = (f32[1,128]{1,0:T(1,128)S(1)}, f32[1,128]{1,0:T(1,128)}, u32[]{:S(2)}) copy-start(f32[1,128]{1,0:T(1,128)} %b_weight.1) | copy-start | bytes 1540
  25.3 6.0 %copy-start.14 = (s32[1,128,1]{1,2,0:T(1,128)S(1)}, s32[1,128,1]{1,2,0:T(1,128)}, u32[]{:S(2)}) copy-start(s32[1,128,1]{1,2,0:T(1,128)} %param.20) | copy-start | bytes 1540
  26.5 20.6 %collective-permute-start.8 = (bf16[48,3584]{1,0:T(8,128)(2,1)S(1)}, bf16[48,3584]{1,0:T(8,128)(2,1)S(1)}, u32[]{:S(2)}, u32[]{:S(2)}) collective-permute-start(bf16[48,3584]{1,0:T(8,128)(2,1)S(1)} %get-tuple-element.68), channel_id=1, source_target_pairs={{0,4},{1,5},{2,6},{3,7},{4,8},{5,9},{6,10},{7,11},{8,12},{9,13},{1... | collective-permute-start | bytes 1032200 | tf_op jit(solution)/shard_map/ppermute | solution.py:318
  28.1 19.0 %collective-permute-start.11 = (bf16[48,3584]{1,0:T(8,128)(2,1)S(1)}, bf16[48,3584]{1,0:T(8,128)(2,1)S(1)}, u32[]{:S(2)}, u32[]{:S(2)}) collective-permute-start(bf16[48,3584]{1,0:T(8,128)(2,1)S(1)} %get-tuple-element.70), channel_id=1, source_target_pairs={{0,12},{1,13},{2,14},{3,15},{4,0},{5,1},{6,2},{7,3},{8,4},{9,5},{1... | collective-permute-start | bytes 1032200 | tf_op jit(solution)/shard_map/ppermute | solution.py:318
  31.2 1.7 %copy-start.6 = (bf16[1,128,3584]{2,1,0:T(8,128)(2,1)}, bf16[1,128,3584]{2,1,0:T(8,128)(2,1)S(1)}, u32[]{:S(2)}) copy-start(bf16[1,128,3584]{2,1,0:T(8,128)(2,1)S(1)} %collective-permute-done.1) | copy-start | bytes 2752516
  31.3 1.6 %copy-start.8 = (bf16[1,768,256]{2,1,0:T(8,128)(2,1)S(1)}, bf16[1,768,256]{2,1,0:T(8,128)(2,1)}, u32[]{:S(2)}) copy-start(bf16[1,768,256]{2,1,0:T(8,128)(2,1)} %param.22) | copy-start | bytes 1179652
  31.3 1.6 %copy-start.9 = (bf16[1,768,256]{2,1,0:T(8,128)(2,1)S(1)}, bf16[1,768,256]{2,1,0:T(8,128)(2,1)}, u32[]{:S(2)}) copy-start(bf16[1,768,256]{2,1,0:T(8,128)(2,1)} %param.23) | copy-start | bytes 1179652
  34.3 17.8 %collective-permute-start.7 = (bf16[384,512]{1,0:T(8,128)(2,1)S(1)}, bf16[384,512]{1,0:T(8,128)(2,1)S(1)}, u32[]{:S(2)}, u32[]{:S(2)}) collective-permute-start(bf16[384,512]{1,0:T(8,128)(2,1)S(1)} %get-tuple-element.65), channel_id=1, source_target_pairs={{0,1},{1,0},{2,3},{3,2},{4,5},{5,4},{6,7},{7,6},{8,9},{9,8},{10,11... | collective-permute-start | bytes 1179656 | tf_op jit(solution)/shard_map/ppermute | solution.py:325
  47.1 22.5 %copy-start.2 = (bf16[1,3584,256]{2,1,0:T(8,128)(2,1)S(1)}, bf16[1,3584,256]{2,1,0:T(8,128)(2,1)}, u32[]{:S(2)}) copy-start(bf16[1,3584,256]{2,1,0:T(8,128)(2,1)} %param.24) | copy-start | bytes 5505028
  47.1 22.5 %copy-start.3 = (bf16[1,3584,256]{2,1,0:T(8,128)(2,1)S(1)}, bf16[1,3584,256]{2,1,0:T(8,128)(2,1)}, u32[]{:S(2)}) copy-start(bf16[1,3584,256]{2,1,0:T(8,128)(2,1)} %param.25) | copy-start | bytes 5505028
  47.2 16.7 %collective-permute-start.6 = (bf16[48,3584]{1,0:T(8,128)(2,1)S(1)}, bf16[48,3584]{1,0:T(8,128)(2,1)S(1)}, u32[]{:S(2)}, u32[]{:S(2)}) collective-permute-start(bf16[48,3584]{1,0:T(8,128)(2,1)S(1)} %get-tuple-element.62), channel_id=1, source_target_pairs={{0,8},{1,9},{2,10},{3,11},{4,12},{5,13},{6,14},{7,15},{8,0},{9,1},... | collective-permute-start | bytes 1032200 | tf_op jit(solution)/shard_map/ppermute | solution.py:318
  49.8 11.0 %collective-permute-start.12 = (bf16[48,3584]{1,0:T(8,128)(2,1)S(1)}, bf16[48,3584]{1,0:T(8,128)(2,1)S(1)}, u32[]{:S(2)}, u32[]{:S(2)}) collective-permute-start(bf16[48,3584]{1,0:T(8,128)(2,1)S(1)} %collective-permute-done.11.refs_1_), channel_id=1, source_target_pairs={{0,2},{1,3},{2,0},{3,1},{4,6},{5,7},{6,4},{7,5},{8,10},{9,11},{10,... | collective-permute-start | bytes 1032200 | tf_op jit(solution)/shard_map/ppermute | solution.py:322
  51.4 35.3 %collective-permute-start.17 = (bf16[128,3584]{1,0:T(8,128)(2,1)S(1)}, bf16[128,3584]{1,0:T(8,128)(2,1)S(1)}, u32[]{:S(2)}, u32[]{:S(2)}) collective-permute-start(bf16[128,3584]{1,0:T(8,128)(2,1)S(1)} %get-tuple-element.113), channel_id=1, source_target_pairs={{0,1},{1,0},{2,3},{3,2},{4,5},{5,4},{6,7},{7,6},{8,9},{9,8},{10,11... | collective-permute-start | bytes 2752520 | tf_op jit(solution)/shard_map/ppermute | solution.py:325
  51.5 35.2 %collective-permute-start.16 = (bf16[128,3584]{1,0:T(8,128)(2,1)S(1)}, bf16[128,3584]{1,0:T(8,128)(2,1)S(1)}, u32[]{:S(2)}, u32[]{:S(2)}) collective-permute-start(bf16[128,3584]{1,0:T(8,128)(2,1)S(1)} %get-tuple-element.114), channel_id=1, source_target_pairs={{0,1},{1,0},{2,3},{3,2},{4,5},{5,4},{6,7},{7,6},{8,9},{9,8},{10,11... | collective-permute-start | bytes 2752520 | tf_op jit(solution)/shard_map/ppermute | solution.py:325
  52.0 16.2 %collective-permute-start.9 = (bf16[48,3584]{1,0:T(8,128)(2,1)S(1)}, bf16[48,3584]{1,0:T(8,128)(2,1)S(1)}, u32[]{:S(2)}, u32[]{:S(2)}) collective-permute-start(bf16[48,3584]{1,0:T(8,128)(2,1)S(1)} %collective-permute-done.8.refs_0_), channel_id=1, source_target_pairs={{0,2},{1,3},{2,0},{3,1},{4,6},{5,7},{6,4},{7,5},{8,10},{9,11},{10,... | collective-permute-start | bytes 1032200 | tf_op jit(solution)/shard_map/ppermute | solution.py:322
  60.8 21.6 %collective-permute-start.13 = (bf16[48,3584]{1,0:T(8,128)(2,1)S(1)}, bf16[48,3584]{1,0:T(8,128)(2,1)S(1)}, u32[]{:S(2)}, u32[]{:S(2)}) collective-permute-start(bf16[48,3584]{1,0:T(8,128)(2,1)S(1)} %get-tuple-element.71.refs_1_), channel_id=1, source_target_pairs={{0,2},{1,3},{2,0},{3,1},{4,6},{5,7},{6,4},{7,5},{8,10},{9,11},{10,... | collective-permute-start | bytes 1032200 | tf_op jit(solution)/shard_map/ppermute | solution.py:322
  68.2 12.8 %collective-permute-start.10 = (bf16[48,3584]{1,0:T(8,128)(2,1)S(1)}, bf16[48,3584]{1,0:T(8,128)(2,1)S(1)}, u32[]{:S(2)}, u32[]{:S(2)}) collective-permute-start(bf16[48,3584]{1,0:T(8,128)(2,1)S(1)} %get-tuple-element.69.refs_0_), channel_id=1, source_target_pairs={{0,2},{1,3},{2,0},{3,1},{4,6},{5,7},{6,4},{7,5},{8,10},{9,11},{10,... | collective-permute-start | bytes 1032200 | tf_op jit(solution)/shard_map/ppermute | solution.py:322
  69.7 7.2 %collective-permute-start.20 = (bf16[48,3584]{1,0:T(8,128)(2,1)S(1)}, bf16[48,3584]{1,0:T(8,128)(2,1)S(1)}, u32[]{:S(2)}, u32[]{:S(2)}) collective-permute-start(bf16[48,3584]{1,0:T(8,128)(2,1)S(1)} %get-tuple-element.86), channel_id=1, source_target_pairs={{0,4},{1,5},{2,6},{3,7},{4,8},{5,9},{6,10},{7,11},{8,12},{9,13},{1... | collective-permute-start | bytes 1032200 | tf_op jit(solution)/shard_map/ppermute | solution.py:318
  76.9 17.5 %collective-permute-start.21 = (bf16[48,3584]{1,0:T(8,128)(2,1)S(1)}, bf16[48,3584]{1,0:T(8,128)(2,1)S(1)}, u32[]{:S(2)}, u32[]{:S(2)}) collective-permute-start(bf16[48,3584]{1,0:T(8,128)(2,1)S(1)} %get-tuple-element.87), channel_id=1, source_target_pairs={{0,12},{1,13},{2,14},{3,15},{4,0},{5,1},{6,2},{7,3},{8,4},{9,5},{1... | collective-permute-start | bytes 1032200 | tf_op jit(solution)/shard_map/ppermute | solution.py:318
  81.0 5.8 %copy-start.1 = (bf16[1,256,3584]{2,1,0:T(8,128)(2,1)S(1)}, bf16[1,256,3584]{2,1,0:T(8,128)(2,1)}, u32[]{:S(2)}) copy-start(bf16[1,256,3584]{2,1,0:T(8,128)(2,1)} %param.26) | copy-start | bytes 5505028
  81.0 5.8 %collective-permute-start.18 = (bf16[96,512]{1,0:T(8,128)(2,1)S(1)}, bf16[96,512]{1,0:T(8,128)(2,1)S(1)}, u32[]{:S(2)}, u32[]{:S(2)}) collective-permute-start(bf16[96,512]{1,0:T(8,128)(2,1)S(1)} %get-tuple-element.80), channel_id=1, source_target_pairs={{0,2},{1,3},{2,0},{3,1},{4,6},{5,7},{6,4},{7,5},{8,10},{9,11},{10,... | collective-permute-start | bytes 294920 | tf_op jit(solution)/shard_map/ppermute | solution.py:322
  86.1 5.5 %collective-permute-start.14 = (bf16[96,512]{1,0:T(8,128)(2,1)S(1)}, bf16[96,512]{1,0:T(8,128)(2,1)S(1)}, u32[]{:S(2)}, u32[]{:S(2)}) collective-permute-start(bf16[96,512]{1,0:T(8,128)(2,1)S(1)} %get-tuple-element.74), channel_id=1, source_target_pairs={{0,2},{1,3},{2,0},{3,1},{4,6},{5,7},{6,4},{7,5},{8,10},{9,11},{10,... | collective-permute-start | bytes 294920 | tf_op jit(solution)/shard_map/ppermute | solution.py:322
  89.5 23.7 %collective-permute-start.19 = (bf16[48,3584]{1,0:T(8,128)(2,1)S(1)}, bf16[48,3584]{1,0:T(8,128)(2,1)S(1)}, u32[]{:S(2)}, u32[]{:S(2)}) collective-permute-start(bf16[48,3584]{1,0:T(8,128)(2,1)S(1)} %get-tuple-element.82), channel_id=1, source_target_pairs={{0,12},{1,13},{2,14},{3,15},{4,0},{5,1},{6,2},{7,3},{8,4},{9,5},{1... | collective-permute-start | bytes 1032200 | tf_op jit(solution)/shard_map/ppermute | solution.py:318
  90.0 23.2 %collective-permute-start.23 = (bf16[48,3584]{1,0:T(8,128)(2,1)S(1)}, bf16[48,3584]{1,0:T(8,128)(2,1)S(1)}, u32[]{:S(2)}, u32[]{:S(2)}) collective-permute-start(bf16[48,3584]{1,0:T(8,128)(2,1)S(1)} %get-tuple-element.90), channel_id=1, source_target_pairs={{0,4},{1,5},{2,6},{3,7},{4,8},{5,9},{6,10},{7,11},{8,12},{9,13},{1... | collective-permute-start | bytes 1032200 | tf_op jit(solution)/shard_map/ppermute | solution.py:318
  98.5 8.2 %collective-permute-start.24 = (bf16[192,512]{1,0:T(8,128)(2,1)S(1)}, bf16[192,512]{1,0:T(8,128)(2,1)S(1)}, u32[]{:S(2)}, u32[]{:S(2)}) collective-permute-start(bf16[192,512]{1,0:T(8,128)(2,1)S(1)} %get-tuple-element.98), channel_id=1, source_target_pairs={{0,2},{1,3},{2,0},{3,1},{4,6},{5,7},{6,4},{7,5},{8,10},{9,11},{10,... | collective-permute-start | bytes 589832 | tf_op jit(solution)/shard_map/ppermute | solution.py:322
  100.0 18.2 %collective-permute-start.22 = (bf16[48,3584]{1,0:T(8,128)(2,1)S(1)}, bf16[48,3584]{1,0:T(8,128)(2,1)S(1)}, u32[]{:S(2)}, u32[]{:S(2)}) collective-permute-start(bf16[48,3584]{1,0:T(8,128)(2,1)S(1)} %get-tuple-element.88), channel_id=1, source_target_pairs={{0,8},{1,9},{2,10},{3,11},{4,12},{5,13},{6,14},{7,15},{8,0},{9,1},... | collective-permute-start | bytes 1032200 | tf_op jit(solution)/shard_map/ppermute | solution.py:318
  106.6 11.5 %copy-start.13 = (f32[1,128]{1,0:T(1,128)S(1)}, f32[1,128]{1,0:T(1,128)}, u32[]{:S(2)}) copy-start(f32[1,128]{1,0:T(1,128)} %weight.3) | copy-start | bytes 1540
  111.1 10.2 %collective-permute-start.28 = (bf16[48,3584]{1,0:T(8,128)(2,1)S(1)}, bf16[48,3584]{1,0:T(8,128)(2,1)S(1)}, u32[]{:S(2)}, u32[]{:S(2)}) collective-permute-start(bf16[48,3584]{1,0:T(8,128)(2,1)S(1)} %get-tuple-element.107), channel_id=1, source_target_pairs={{0,2},{1,3},{2,0},{3,1},{4,6},{5,7},{6,4},{7,5},{8,10},{9,11},{10,... | collective-permute-start | bytes 1032200 | tf_op jit(solution)/shard_map/ppermute | solution.py:322
  111.7 14.8 %collective-permute-start.25 = (bf16[48,3584]{1,0:T(8,128)(2,1)S(1)}, bf16[48,3584]{1,0:T(8,128)(2,1)S(1)}, u32[]{:S(2)}, u32[]{:S(2)}) collective-permute-start(bf16[48,3584]{1,0:T(8,128)(2,1)S(1)} %get-tuple-element.101), channel_id=1, source_target_pairs={{0,2},{1,3},{2,0},{3,1},{4,6},{5,7},{6,4},{7,5},{8,10},{9,11},{10,... | collective-permute-start | bytes 1032200 | tf_op jit(solution)/shard_map/ppermute | solution.py:322
  121.3 12.7 %collective-permute-start.30 = (bf16[48,3584]{1,0:T(8,128)(2,1)S(1)}, bf16[48,3584]{1,0:T(8,128)(2,1)S(1)}, u32[]{:S(2)}, u32[]{:S(2)}) collective-permute-start(bf16[48,3584]{1,0:T(8,128)(2,1)S(1)} %get-tuple-element.111), channel_id=1, source_target_pairs={{0,2},{1,3},{2,0},{3,1},{4,6},{5,7},{6,4},{7,5},{8,10},{9,11},{10,... | collective-permute-start | bytes 1032200 | tf_op jit(solution)/shard_map/ppermute | solution.py:322
  122.2 23.1 %collective-permute-start.29 = (bf16[48,3584]{1,0:T(8,128)(2,1)S(1)}, bf16[48,3584]{1,0:T(8,128)(2,1)S(1)}, u32[]{:S(2)}, u32[]{:S(2)}) collective-permute-start(bf16[48,3584]{1,0:T(8,128)(2,1)S(1)} %add_rows.6), channel_id=1, source_target_pairs={{0,8},{1,9},{2,10},{3,11},{4,12},{5,13},{6,14},{7,15},{8,0},{9,1},... | collective-permute-start | bytes 1032200 | tf_op jit(solution)/shard_map/ppermute | solution.py:318
  126.6 13.2 %collective-permute-start.26 = (bf16[48,3584]{1,0:T(8,128)(2,1)S(1)}, bf16[48,3584]{1,0:T(8,128)(2,1)S(1)}, u32[]{:S(2)}, u32[]{:S(2)}) collective-permute-start(bf16[48,3584]{1,0:T(8,128)(2,1)S(1)} %get-tuple-element.102), channel_id=1, source_target_pairs={{0,2},{1,3},{2,0},{3,1},{4,6},{5,7},{6,4},{7,5},{8,10},{9,11},{10,... | collective-permute-start | bytes 1032200 | tf_op jit(solution)/shard_map/ppermute | solution.py:322
  126.7 28.0 %collective-permute-start.27 = (bf16[48,3584]{1,0:T(8,128)(2,1)S(1)}, bf16[48,3584]{1,0:T(8,128)(2,1)S(1)}, u32[]{:S(2)}, u32[]{:S(2)}) collective-permute-start(bf16[48,3584]{1,0:T(8,128)(2,1)S(1)} %add_rows.5), channel_id=1, source_target_pairs={{0,12},{1,13},{2,14},{3,15},{4,0},{5,1},{6,2},{7,3},{8,4},{9,5},{1... | collective-permute-start | bytes 1032200 | tf_op jit(solution)/shard_map/ppermute | solution.py:318
  134.0 21.9 %collective-permute-start.31 = (bf16[48,3584]{1,0:T(8,128)(2,1)S(1)}, bf16[48,3584]{1,0:T(8,128)(2,1)S(1)}, u32[]{:S(2)}, u32[]{:S(2)}) collective-permute-start(bf16[48,3584]{1,0:T(8,128)(2,1)S(1)} %add_rows.7), channel_id=1, source_target_pairs={{0,4},{1,5},{2,6},{3,7},{4,8},{5,9},{6,10},{7,11},{8,12},{9,13},{1... | collective-permute-start | bytes 1032200 | tf_op jit(solution)/shard_map/ppermute | solution.py:318
  139.7 15.0 %copy-start.7 = (bf16[1,128,3584]{2,1,0:T(8,128)(2,1)S(1)}, bf16[1,128,3584]{2,1,0:T(8,128)(2,1)}, u32[]{:S(2)}) copy-start(bf16[1,128,3584]{2,1,0:T(8,128)(2,1)} %copy-done.6) | copy-start | bytes 2752516

commit v5 on v4

--- a/solution.py
+++ b/solution.py
@@ -12,7 +12,7 @@
 EARLY = (2,)
 DOWN_PARTS = 2
 RETURN_ORDER = (2, 1, 3, 0)
-FLOPS = {"grad_rows": 10000000000, "add_rows": 2000000000, "forward_end": 50000000000}
+FLOPS = {"backward_most": 1000000, "grad_rows": 10000000000, "add_rows": 2000000000, "forward_end": 50000000000}
 BF16 = jnp.bfloat16
 F32 = jnp.float32
 COLS = 896

time: 158 us -> 154 us (0.975)
  waiting for transfers between devices: 79.9 us -> 72.5 us
    ppermute x12, waiting for transfers between devices: 25 us -> 18.6 us  [to_plane(): return lax.ppermute(value, 'expert', pairs)]
  transfers between devices with their start and end apart: 32 -> 32, of which waited for: 15 -> 13; matrix products, arithmetic and copies ran while one was open for 1% -> 1% of each run, Pallas kernels for 23% -> 25%
where the time goes in v5:
time: 154 us; the launch traced here: 153 us
  waiting for transfers between devices  72.5 us (47%)
  Pallas kernels  40.5 us (26%)
  starting transfers between devices  37.8 us (25%)
    ppermute x12, waiting for transfers between devices, to_chip(): return lax.ppermute(value, 'expert', pairs)  40.6 us
    pallas_call x18, Pallas kernels, call(): pl.pallas_call(kernel, out_shape=outs, in_specs=in_specs, out_specs=out_s...  40.5 us
    ppermute x12, waiting for transfers between devices, to_plane(): return lax.ppermute(value, 'expert', pairs)  18.6 us
    ppermute x12, starting transfers between devices, to_plane(): return lax.ppermute(value, 'expert', pairs)  17.2 us
    ppermute x12, starting transfers between devices, to_chip(): return lax.ppermute(value, 'expert', pairs)  13.7 us
    ppermute x2, waiting for transfers between devices, shifted(): return lax.ppermute(value, axis, pairs)  13.3 us
    ppermute x2, starting transfers between devices, shifted(): return lax.ppermute(value, axis, pairs)  5.65 us
  transfers between devices with their start and end apart: 32, of which 13 were waited for; matrix products, arithmetic and copies ran while one was open for 1% of the time, Pallas kernels for 25%

profile of v5, /device:TPU:8, one launch (start us, length us, event | category | flops | bytes accessed | tf_op | source)
XLA Modules:
  0.0 153.2 jit_solution(8880353242690198435)
XLA Ops:
  0.6 0.1 collective-permute-start.2
  0.7 0.5 collective-permute-start.3
  1.2 0.1 collective-permute-start.4
  1.3 4.4 %collective-permute-start = (bf16[1,128,3584]{2,1,0:T(8,128)(2,1)}, bf16[1,128,3584]{2,1,0:T(8,128)(2,1)}, u32[]{:S(2)}, u32[]{:S(2)}) collective-permute-start(bf16[1,128,3584]{2,1,0:T(8,128)(2,1)} %param.15), channel_id=1, source_target_pairs={{0,16},{1,17},{2,18},{3,19},{4,20},{5,21},{6,22},{7,23},{8,24},{9,... | collective-permute-start | bytes 2752520 | tf_op jit(solution)/shard_map/ppermute | solution.py:43
  5.7 1.5 collective-permute-start.15
  7.2 0.7 stack.31.at_ref
  7.8 1.3 collective-permute-start.1
  9.1 3.0 %first_rows.1 = bf16[48,3584]{1,0:T(8,128)(2,1)} custom-call(s32[5]{0:T(128)} %stack.31.at_ref, s32[1,128]{1,0:T(1,128)} %bitcast.39, s32[1,128]{1,0:T(1,128)} %bitcast.18, bf16[128,3584]{1,0:T(8,128)(2,1)} %near.6, bf16[128,3584]{1,0:T(8,128)(2,1)} %near.7, f32[1,128]{1,0:T(1,128)} %b_weight.1, f32[1,3584]{1,0:T(1,128)} %steer.5), custom_call_target="tpu_custom_call" | custom-call | flops 5000000000 | bytes 100000 | tf_op jit(solution)/shard_map/first_rows/pallas_call | solution.py:48
  12.1 2.6 %collective-permute-start.5 = (bf16[48,3584]{1,0:T(8,128)(2,1)}, bf16[48,3584]{1,0:T(8,128)(2,1)S(1)}, u32[]{:S(2)}, u32[]{:S(2)}) collective-permute-start(bf16[48,3584]{1,0:T(8,128)(2,1)} %first_rows.1), channel_id=1, source_target_pairs={{0,8},{1,9},{2,10},{3,11},{4,12},{5,13},{6,14},{7,15},{8,0},{9,1},... | collective-permute-start | bytes 1032200 | tf_op jit(solution)/shard_map/ppermute | solution.py:318
  14.7 10.5 %collective-permute-done = bf16[1,128,3584]{2,1,0:T(8,128)(2,1)} collective-permute-done((bf16[1,128,3584]{2,1,0:T(8,128)(2,1)}, bf16[1,128,3584]{2,1,0:T(8,128)(2,1)}, u32[]{:S(2)}, u32[]{:S(2)}) %collective-permute-start) | collective-permute-done | bytes 917536 | tf_op jit(solution)/shard_map/ppermute | solution.py:43
  25.3 1.9 %forward_rows.1 = (bf16[48,3584]{1,0:T(8,128)(2,1)S(1)}, bf16[48,3584]{1,0:T(8,128)(2,1)S(1)}, bf16[48,3584]{1,0:T(8,128)(2,1)S(1)}, bf16[48,3584]{1,0:T(8,128)(2,1)S(1)}) custom-call(s32[5]{0:T(128)S(1)} %copy-done.1, s32[1,128]{1,0:T(1,128)S(1)} %bitcast.40, bf16[128,3584]{1,0:T(8,128)(2,1)S(1)} %copy-done.6, bf16[128,3584]{1,0:T(8,128)(2,1)} %bitcast.6.far), custom_call_target="tpu_custom_call" | custom-call | flops 5000000000 | bytes 100000 | tf_op jit(solution)/shard_map/forward_rows/pallas_call | solution.py:48
  27.2 1.6 %collective-permute-start.8 = (bf16[48,3584]{1,0:T(8,128)(2,1)S(1)}, bf16[48,3584]{1,0:T(8,128)(2,1)S(1)}, u32[]{:S(2)}, u32[]{:S(2)}) collective-permute-start(bf16[48,3584]{1,0:T(8,128)(2,1)S(1)} %get-tuple-element.68), channel_id=1, source_target_pairs={{0,4},{1,5},{2,6},{3,7},{4,8},{5,9},{6,10},{7,11},{8,12},{9,13},{1... | collective-permute-start | bytes 1032200 | tf_op jit(solution)/shard_map/ppermute | solution.py:318
  28.8 0.4 collective-permute-start.11
  29.3 2.8 %collective-permute-done.1 = bf16[1,128,3584]{2,1,0:T(8,128)(2,1)S(1)} collective-permute-done((bf16[1,128,3584]{2,1,0:T(8,128)(2,1)}, bf16[1,128,3584]{2,1,0:T(8,128)(2,1)S(1)}, u32[]{:S(2)}, u32[]{:S(2)}) %collective-permute-start.1) | collective-permute-done | bytes 917536 | tf_op jit(solution)/shard_map/ppermute | solution.py:43
  32.1 1.6 %backward_rows.1 = (bf16[48,3584]{1,0:T(8,128)(2,1)S(1)}, bf16[48,3584]{1,0:T(8,128)(2,1)S(1)}, bf16[48,3584]{1,0:T(8,128)(2,1)S(1)}, bf16[48,3584]{1,0:T(8,128)(2,1)S(1)}) custom-call(s32[5]{0:T(128)S(1)} %copy-done.1, s32[1,128]{1,0:T(1,128)S(1)} %bitcast.19, bf16[128,3584]{1,0:T(8,128)(2,1)S(1)} %copy-done, f32[1,128]{1,0:T(1,128)S(1)} %copy-done.10, ...), custom_call_target="tpu_custom_call" | custom-call | flops 5000000000 | bytes 100000 | tf_op jit(solution)/shard_map/backward_rows/pallas_call | solution.py:48
  33.7 1.3 saved_rows.1
  35.0 0.1 collective-permute-start.7
  35.1 12.8 %collective-permute-done.15.refs_0_.refs_6_ = bf16[256,3584]{1,0:T(8,128)(2,1)S(1)} collective-permute-done((bf16[256,3584]{1,0:T(8,128)(2,1)}, bf16[256,3584]{1,0:T(8,128)(2,1)S(1)}, u32[]{:S(2)}, u32[]{:S(2)}) %collective-permute-start.15) | collective-permute-done | bytes 1835040 | tf_op jit(solution)/shard_map/ppermute | solution.py:322
  48.0 2.7 %collective-permute-start.6 = (bf16[48,3584]{1,0:T(8,128)(2,1)S(1)}, bf16[48,3584]{1,0:T(8,128)(2,1)S(1)}, u32[]{:S(2)}, u32[]{:S(2)}) collective-permute-start(bf16[48,3584]{1,0:T(8,128)(2,1)S(1)} %get-tuple-element.62), channel_id=1, source_target_pairs={{0,8},{1,9},{2,10},{3,11},{4,12},{5,13},{6,14},{7,15},{8,0},{9,1},... | collective-permute-start | bytes 1032200 | tf_op jit(solution)/shard_map/ppermute | solution.py:318
  50.6 1.5 collective-permute-start.12
  52.1 0.1 fusion
  52.3 0.1 collective-permute-start.17
  52.3 0.5 collective-permute-start.16
  52.8 0.5 collective-permute-start.9
  53.4 8.3 %collective-permute-done.12.refs_3_ = bf16[48,3584]{1,0:T(8,128)(2,1)S(1)} collective-permute-done((bf16[48,3584]{1,0:T(8,128)(2,1)S(1)}, bf16[48,3584]{1,0:T(8,128)(2,1)S(1)}, u32[]{:S(2)}, u32[]{:S(2)}) %collective-permute-start.12) | collective-permute-done | bytes 344096 | tf_op jit(solution)/shard_map/ppermute | solution.py:322
  61.6 1.5 collective-permute-start.13
  63.1 1.6 %collective-permute-done.6 = bf16[48,3584]{1,0:T(8,128)(2,1)S(1)} collective-permute-done((bf16[48,3584]{1,0:T(8,128)(2,1)S(1)}, bf16[48,3584]{1,0:T(8,128)(2,1)S(1)}, u32[]{:S(2)}, u32[]{:S(2)}) %collective-permute-start.6) | collective-permute-done | bytes 344096 | tf_op jit(solution)/shard_map/ppermute | solution.py:318
  64.8 4.2 %collective-permute-done.9.refs_2_ = bf16[48,3584]{1,0:T(8,128)(2,1)S(1)} collective-permute-done((bf16[48,3584]{1,0:T(8,128)(2,1)S(1)}, bf16[48,3584]{1,0:T(8,128)(2,1)S(1)}, u32[]{:S(2)}, u32[]{:S(2)}) %collective-permute-start.9) | collective-permute-done | bytes 344096 | tf_op jit(solution)/shard_map/ppermute | solution.py:322
  69.0 1.5 collective-permute-start.10
  70.5 3.7 %hidden.3 = (bf16[96,512]{1,0:T(8,128)(2,1)S(1)}, bf16[96,512]{1,0:T(8,128)(2,1)S(1)}) custom-call(bf16[48,3584]{1,0:T(8,128)(2,1)S(1)} %collective-permute-done.8.refs_0_, bf16[48,3584]{1,0:T(8,128)(2,1)S(1)} %collective-permute-done.11.refs_1_, bf16[48,3584]{1,0:T(8,128)(2,1)S(1)} %collective-permute-done.9.refs_2_, ...), custom_call_target="tpu_custom_call" | custom-call | flops 5000000000 | bytes 100000 | tf_op jit(solution)/shard_map/hidden/pallas_call | solution.py:48
  74.2 3.6 %collective-permute-done.20.refs_1_ = bf16[48,3584]{1,0:T(8,128)(2,1)S(1)} collective-permute-done((bf16[48,3584]{1,0:T(8,128)(2,1)S(1)}, bf16[48,3584]{1,0:T(8,128)(2,1)S(1)}, u32[]{:S(2)}, u32[]{:S(2)}) %collective-permute-start.20) | collective-permute-done | bytes 344096 | tf_op jit(solution)/shard_map/ppermute | solution.py:318
  77.8 2.8 %collective-permute-start.21 = (bf16[48,3584]{1,0:T(8,128)(2,1)S(1)}, bf16[48,3584]{1,0:T(8,128)(2,1)S(1)}, u32[]{:S(2)}, u32[]{:S(2)}) collective-permute-start(bf16[48,3584]{1,0:T(8,128)(2,1)S(1)} %get-tuple-element.87), channel_id=1, source_target_pairs={{0,12},{1,13},{2,14},{3,15},{4,0},{5,1},{6,2},{7,3},{8,4},{9,5},{1... | collective-permute-start | bytes 1032200 | tf_op jit(solution)/shard_map/ppermute | solution.py:318
  80.6 1.2 collective-permute-done.10.refs_2_
  81.8 1.5 collective-permute-start.18
  83.3 3.6 %hidden.2 = (bf16[96,512]{1,0:T(8,128)(2,1)S(1)}, bf16[96,512]{1,0:T(8,128)(2,1)S(1)}) custom-call(bf16[48,3584]{1,0:T(8,128)(2,1)S(1)} %get-tuple-element.69.refs_0_, bf16[48,3584]{1,0:T(8,128)(2,1)S(1)} %get-tuple-element.71.refs_1_, bf16[48,3584]{1,0:T(8,128)(2,1)S(1)} %collective-permute-done.10.refs_2_, ...), custom_call_target="tpu_custom_call" | custom-call | flops 5000000000 | bytes 100000 | tf_op jit(solution)/shard_map/hidden/pallas_call | solution.py:48
  86.9 0.6 collective-permute-start.14
  87.6 2.8 %expert_out.3 = (bf16[48,3584]{1,0:T(8,128)(2,1)S(1)}, bf16[48,3584]{1,0:T(8,128)(2,1)S(1)}) custom-call(bf16[96,512]{1,0:T(8,128)(2,1)S(1)} %get-tuple-element.78.own, bf16[96,512]{1,0:T(8,128)(2,1)S(1)} %collective-permute-done.18.other, bf16[256,3584]{1,0:T(8,128)(2,1)S(1)} %bitcast.24, bf16[256,3584]{1,0:T(8,128)(2,1)} %collective-permute-done.4.d1.refs_5_, ...), custom_call_target="tpu_custom_call" | custom-call | flops 5000000000 | bytes 100000 | tf_op jit(solution)/shard_map/expert_out/pallas_call | solution.py:48
  90.4 0.5 collective-permute-start.19
  90.9 1.6 %collective-permute-start.23 = (bf16[48,3584]{1,0:T(8,128)(2,1)S(1)}, bf16[48,3584]{1,0:T(8,128)(2,1)S(1)}, u32[]{:S(2)}, u32[]{:S(2)}) collective-permute-start(bf16[48,3584]{1,0:T(8,128)(2,1)S(1)} %get-tuple-element.90), channel_id=1, source_target_pairs={{0,4},{1,5},{2,6},{3,7},{4,8},{5,9},{6,10},{7,11},{8,12},{9,13},{1... | collective-permute-start | bytes 1032200 | tf_op jit(solution)/shard_map/ppermute | solution.py:318
  92.4 4.0 %grad_hidden.1 = (f32[192,512]{1,0:T(8,128)S(1)}, bf16[192,512]{1,0:T(8,128)(2,1)S(1)}) custom-call(bf16[48,3584]{1,0:T(8,128)(2,1)S(1)} %get-tuple-element.93.refs_0_, bf16[48,3584]{1,0:T(8,128)(2,1)S(1)} %collective-permute-done.20.refs_1_, bf16[48,3584]{1,0:T(8,128)(2,1)S(1)} %get-tuple-element.115.refs_2_, ...), custom_call_target="tpu_custom_call" | custom-call | flops 5000000000 | bytes 100000 | tf_op jit(solution)/shard_map/grad_hidden/pallas_call | solution.py:48
  96.5 1.5 %collective-permute-start.24 = (bf16[192,512]{1,0:T(8,128)(2,1)S(1)}, bf16[192,512]{1,0:T(8,128)(2,1)S(1)}, u32[]{:S(2)}, u32[]{:S(2)}) collective-permute-start(bf16[192,512]{1,0:T(8,128)(2,1)S(1)} %get-tuple-element.98), channel_id=1, source_target_pairs={{0,2},{1,3},{2,0},{3,1},{4,6},{5,7},{6,4},{7,5},{8,10},{9,11},{10,... | collective-permute-start | bytes 589832 | tf_op jit(solution)/shard_map/ppermute | solution.py:322
  98.0 2.8 %expert_out.2 = (bf16[48,3584]{1,0:T(8,128)(2,1)S(1)}, bf16[48,3584]{1,0:T(8,128)(2,1)S(1)}) custom-call(bf16[96,512]{1,0:T(8,128)(2,1)S(1)} %get-tuple-element.72.own, bf16[96,512]{1,0:T(8,128)(2,1)S(1)} %collective-permute-done.14.other, bf16[256,3584]{1,0:T(8,128)(2,1)S(1)} %bitcast.26, bf16[256,3584]{1,0:T(8,128)(2,1)} %collective-permute-done.4.d1.refs_5_, ...), custom_call_target="tpu_custom_call" | custom-call | flops 5000000000 | bytes 100000 | tf_op jit(solution)/shard_map/expert_out/pallas_call | solution.py:48
  100.8 2.2 %collective-permute-start.22 = (bf16[48,3584]{1,0:T(8,128)(2,1)S(1)}, bf16[48,3584]{1,0:T(8,128)(2,1)S(1)}, u32[]{:S(2)}, u32[]{:S(2)}) collective-permute-start(bf16[48,3584]{1,0:T(8,128)(2,1)S(1)} %get-tuple-element.88), channel_id=1, source_target_pairs={{0,8},{1,9},{2,10},{3,11},{4,12},{5,13},{6,14},{7,15},{8,0},{9,1},... | collective-permute-start | bytes 1032200 | tf_op jit(solution)/shard_map/ppermute | solution.py:318
  103.0 4.5 %grad_rows.3 = (bf16[48,3584]{1,0:T(8,128)(2,1)S(1)}, bf16[48,3584]{1,0:T(8,128)(2,1)S(1)}, bf16[48,3584]{1,0:T(8,128)(2,1)S(1)}, bf16[48,3584]{1,0:T(8,128)(2,1)S(1)}) custom-call(bf16[192,512]{1,0:T(8,128)(2,1)S(1)} %collective-permute-done.24.grads, bf16[384,512]{1,0:T(8,128)(2,1)S(1)} %get-tuple-element.95.kept, ...), custom_call_target="tpu_custom_call" | custom-call | flops 10000000000 | bytes 100000 | tf_op jit(solution)/shard_map/grad_rows/pallas_call | solution.py:48
  107.4 0.8 collective-permute-start.28
  108.2 1.3 collective-permute-start.25
  109.5 4.5 %grad_rows.2 = (f32[48,3584]{1,0:T(8,128)S(1)}, f32[48,3584]{1,0:T(8,128)S(1)}, f32[48,3584]{1,0:T(8,128)S(1)}, f32[48,3584]{1,0:T(8,128)S(1)}) custom-call(f32[192,512]{1,0:T(8,128)S(1)} %get-tuple-element.94.grads, bf16[384,512]{1,0:T(8,128)(2,1)S(1)} %get-tuple-element.95.kept, bf16[384,512]{1,0:T(8,128)(2,1)S(1)} %collective-permute-done.7.got, ...), custom_call_target="tpu_custom_call" | custom-call | flops 10000000000 | bytes 100000 | tf_op jit(solution)/shard_map/grad_rows/pallas_call | solution.py:48
  114.0 4.5 %collective-permute-done.28.theirs = bf16[48,3584]{1,0:T(8,128)(2,1)S(1)} collective-permute-done((bf16[48,3584]{1,0:T(8,128)(2,1)S(1)}, bf16[48,3584]{1,0:T(8,128)(2,1)S(1)}, u32[]{:S(2)}, u32[]{:S(2)}) %collective-permute-start.28) | collective-permute-done | bytes 344096 | tf_op jit(solution)/shard_map/ppermute | solution.py:322
  118.5 0.7 collective-permute-start.30
  119.2 0.1 add_rows.6
  119.3 2.2 %collective-permute-start.29 = (bf16[48,3584]{1,0:T(8,128)(2,1)S(1)}, bf16[48,3584]{1,0:T(8,128)(2,1)S(1)}, u32[]{:S(2)}, u32[]{:S(2)}) collective-permute-start(bf16[48,3584]{1,0:T(8,128)(2,1)S(1)} %add_rows.6), channel_id=1, source_target_pairs={{0,8},{1,9},{2,10},{3,11},{4,12},{5,13},{6,14},{7,15},{8,0},{9,1},... | collective-permute-start | bytes 1032200 | tf_op jit(solution)/shard_map/ppermute | solution.py:318
  121.5 4.4 %collective-permute-done.25.theirs = bf16[48,3584]{1,0:T(8,128)(2,1)S(1)} collective-permute-done((bf16[48,3584]{1,0:T(8,128)(2,1)S(1)}, bf16[48,3584]{1,0:T(8,128)(2,1)S(1)}, u32[]{:S(2)}, u32[]{:S(2)}) %collective-permute-start.25) | collective-permute-done | bytes 344096 | tf_op jit(solution)/shard_map/ppermute | solution.py:322
  125.9 0.1 add_rows.5
  126.0 0.8 collective-permute-start.26
  126.7 0.5 collective-permute-start.27
  127.2 5.2 %collective-permute-done.30.theirs = bf16[48,3584]{1,0:T(8,128)(2,1)S(1)} collective-permute-done((bf16[48,3584]{1,0:T(8,128)(2,1)S(1)}, bf16[48,3584]{1,0:T(8,128)(2,1)S(1)}, u32[]{:S(2)}, u32[]{:S(2)}) %collective-permute-start.30) | collective-permute-done | bytes 344096 | tf_op jit(solution)/shard_map/ppermute | solution.py:322
  132.4 0.1 add_rows.7
  132.6 0.5 copy-done.12
  133.1 3.2 %forward_end.1 = (bf16[128,3584]{1,0:T(8,128)(2,1)}, f32[1,128]{1,0:T(1,128)}) custom-call(s32[5]{0:T(128)S(1)} %copy-done.1, s32[1,128]{1,0:T(1,128)S(1)} %bitcast.41, bf16[128,3584]{1,0:T(8,128)(2,1)S(1)} %copy-done.6, bf16[128,3584]{1,0:T(8,128)(2,1)} %bitcast.6.far, f32[1,128]{1,0:T(1,128)S(1)} %copy-done.12, f32[1,3584]{1,0:T(1,128)S(1)} %copy-done.9, ...), custom_call_target="tpu_custom_call" | custom-call | flops 49999998976 | bytes 100000 | tf_op jit(solution)/shard_map/forward_end/pallas_call | solution.py:48
  136.3 0.1 add_rows.4.refs_0_
  136.3 4.9 %collective-permute-done.29.refs_2_ = bf16[48,3584]{1,0:T(8,128)(2,1)S(1)} collective-permute-done((bf16[48,3584]{1,0:T(8,128)(2,1)S(1)}, bf16[48,3584]{1,0:T(8,128)(2,1)S(1)}, u32[]{:S(2)}, u32[]{:S(2)}) %collective-permute-start.29) | collective-permute-done | bytes 344096 | tf_op jit(solution)/shard_map/ppermute | solution.py:318
  141.2 8.5 %collective-permute-done.27.refs_1_ = bf16[48,3584]{1,0:T(8,128)(2,1)S(1)} collective-permute-done((bf16[48,3584]{1,0:T(8,128)(2,1)S(1)}, bf16[48,3584]{1,0:T(8,128)(2,1)S(1)}, u32[]{:S(2)}, u32[]{:S(2)}) %collective-permute-start.27) | collective-permute-done | bytes 344096 | tf_op jit(solution)/shard_map/ppermute | solution.py:318
  149.7 1.3 backward_most.1.most
  151.0 2.2 %backward_end.1 = bf16[128,3584]{1,0:T(8,128)(2,1)} custom-call(s32[5]{0:T(128)S(1)} %copy-done.1, s32[1,128]{1,0:T(1,128)S(1)} %bitcast.21, bf16[128,3584]{1,0:T(8,128)(2,1)S(1)} %backward_most.1.most, bf16[48,3584]{1,0:T(8,128)(2,1)S(1)} %collective-permute-done.31.back), custom_call_target="tpu_custom_call" | custom-call | flops 5000000000 | bytes 100000 | tf_op jit(solution)/shard_map/backward_end/pallas_call | solution.py:48
  (47 shorter events, 0.2 us)
Async XLA Ops:
  0.6 7.2 %collective-permute-start.2 = (bf16[3584,256]{1,0:T(8,128)(2,1)}, bf16[3584,256]{1,0:T(8,128)(2,1)}, u32[]{:S(2)}, u32[]{:S(2)}) collective-permute-start(bf16[3584,256]{1,0:T(8,128)(2,1)} %bitcast.27), channel_id=1, source_target_pairs={{0,1},{1,0},{2,3},{3,2},{4,5},{5,4},{6,7},{7,6},{8,9},{9,8},{10,11... | collective-permute-start | bytes 5505032 | tf_op jit(solution)/shard_map/ppermute | solution.py:325
  0.7 11.4 %collective-permute-start.3 = (bf16[3584,256]{1,0:T(8,128)(2,1)}, bf16[3584,256]{1,0:T(8,128)(2,1)}, u32[]{:S(2)}, u32[]{:S(2)}) collective-permute-start(bf16[3584,256]{1,0:T(8,128)(2,1)} %bitcast.32), channel_id=1, source_target_pairs={{0,1},{1,0},{2,3},{3,2},{4,5},{5,4},{6,7},{7,6},{8,9},{9,8},{10,11... | collective-permute-start | bytes 5505032 | tf_op jit(solution)/shard_map/ppermute | solution.py:325
  1.2 13.5 %collective-permute-start.4 = (bf16[256,3584]{1,0:T(8,128)(2,1)}, bf16[256,3584]{1,0:T(8,128)(2,1)}, u32[]{:S(2)}, u32[]{:S(2)}) collective-permute-start(bf16[256,3584]{1,0:T(8,128)(2,1)} %bitcast.22), channel_id=1, source_target_pairs={{0,1},{1,0},{2,3},{3,2},{4,5},{5,4},{6,7},{7,6},{8,9},{9,8},{10,11... | collective-permute-start | bytes 5505032 | tf_op jit(solution)/shard_map/ppermute | solution.py:325
  1.3 23.9 %collective-permute-start = (bf16[1,128,3584]{2,1,0:T(8,128)(2,1)}, bf16[1,128,3584]{2,1,0:T(8,128)(2,1)}, u32[]{:S(2)}, u32[]{:S(2)}) collective-permute-start(bf16[1,128,3584]{2,1,0:T(8,128)(2,1)} %param.15), channel_id=1, source_target_pairs={{0,16},{1,17},{2,18},{3,19},{4,20},{5,21},{6,22},{7,23},{8,24},{9,... | collective-permute-start | bytes 2752520 | tf_op jit(solution)/shard_map/ppermute | solution.py:43
  5.7 42.3 %collective-permute-start.15 = (bf16[256,3584]{1,0:T(8,128)(2,1)}, bf16[256,3584]{1,0:T(8,128)(2,1)S(1)}, u32[]{:S(2)}, u32[]{:S(2)}) collective-permute-start(bf16[256,3584]{1,0:T(8,128)(2,1)} %bitcast.23), channel_id=1, source_target_pairs={{0,2},{1,3},{2,0},{3,1},{4,6},{5,7},{6,4},{7,5},{8,10},{9,11},{10,... | collective-permute-start | bytes 5505032 | tf_op jit(solution)/shard_map/ppermute | solution.py:322
  7.8 24.2 %collective-permute-start.1 = (bf16[1,128,3584]{2,1,0:T(8,128)(2,1)}, bf16[1,128,3584]{2,1,0:T(8,128)(2,1)S(1)}, u32[]{:S(2)}, u32[]{:S(2)}) collective-permute-start(bf16[1,128,3584]{2,1,0:T(8,128)(2,1)} %param.19), channel_id=1, source_target_pairs={{16,0},{17,1},{18,2},{19,3},{20,4},{21,5},{22,6},{23,7},{24,8},{25... | collective-permute-start | bytes 2752520 | tf_op jit(solution)/shard_map/ppermute | solution.py:43
  9.1 16.1 %copy-start.1 = (s32[5]{0:T(128)S(1)}, s32[5]{0:T(128)}, u32[]{:S(2)}) copy-start(s32[5]{0:T(128)} %stack.31.at_ref) | copy-start | bytes 64
  9.1 16.1 %copy-start.6 = (bf16[128,3584]{1,0:T(8,128)(2,1)S(1)}, bf16[128,3584]{1,0:T(8,128)(2,1)}, u32[]{:S(2)}) copy-start(bf16[128,3584]{1,0:T(8,128)(2,1)} %near.6) | copy-start | bytes 2752516
  9.1 16.1 %copy-start.11 = (s32[1,128,1]{1,2,0:T(1,128)S(1)}, s32[1,128,1]{1,2,0:T(1,128)}, u32[]{:S(2)}) copy-start(s32[1,128,1]{1,2,0:T(1,128)} %param.16) | copy-start | bytes 1540
  12.1 35.9 %collective-permute-start.5 = (bf16[48,3584]{1,0:T(8,128)(2,1)}, bf16[48,3584]{1,0:T(8,128)(2,1)S(1)}, u32[]{:S(2)}, u32[]{:S(2)}) collective-permute-start(bf16[48,3584]{1,0:T(8,128)(2,1)} %first_rows.1), channel_id=1, source_target_pairs={{0,8},{1,9},{2,10},{3,11},{4,12},{5,13},{6,14},{7,15},{8,0},{9,1},... | collective-permute-start | bytes 1032200 | tf_op jit(solution)/shard_map/ppermute | solution.py:318
  25.2 6.8 %copy-start = (bf16[128,3584]{1,0:T(8,128)(2,1)S(1)}, bf16[128,3584]{1,0:T(8,128)(2,1)}, u32[]{:S(2)}) copy-start(bf16[128,3584]{1,0:T(8,128)(2,1)} %near.7) | copy-start | bytes 2752516
  25.2 6.8 %copy-start.2 = (s32[1,128,1]{1,2,0:T(1,128)S(1)}, s32[1,128,1]{1,2,0:T(1,128)}, u32[]{:S(2)}) copy-start(s32[1,128,1]{1,2,0:T(1,128)} %param.20) | copy-start | bytes 1540
  25.3 6.8 %copy-start.9 = (f32[1,3584]{1,0:T(1,128)S(1)}, f32[1,3584]{1,0:T(1,128)}, u32[]{:S(2)}) copy-start(f32[1,3584]{1,0:T(1,128)} %steer.5) | copy-start | bytes 43012
  25.3 6.8 %copy-start.10 = (f32[1,128]{1,0:T(1,128)S(1)}, f32[1,128]{1,0:T(1,128)}, u32[]{:S(2)}) copy-start(f32[1,128]{1,0:T(1,128)} %b_weight.1) | copy-start | bytes 1540
  27.2 20.8 %collective-permute-start.8 = (bf16[48,3584]{1,0:T(8,128)(2,1)S(1)}, bf16[48,3584]{1,0:T(8,128)(2,1)S(1)}, u32[]{:S(2)}, u32[]{:S(2)}) collective-permute-start(bf16[48,3584]{1,0:T(8,128)(2,1)S(1)} %get-tuple-element.68), channel_id=1, source_target_pairs={{0,4},{1,5},{2,6},{3,7},{4,8},{5,9},{6,10},{7,11},{8,12},{9,13},{1... | collective-permute-start | bytes 1032200 | tf_op jit(solution)/shard_map/ppermute | solution.py:318
  28.8 19.1 %collective-permute-start.11 = (bf16[48,3584]{1,0:T(8,128)(2,1)S(1)}, bf16[48,3584]{1,0:T(8,128)(2,1)S(1)}, u32[]{:S(2)}, u32[]{:S(2)}) collective-permute-start(bf16[48,3584]{1,0:T(8,128)(2,1)S(1)} %get-tuple-element.70), channel_id=1, source_target_pairs={{0,12},{1,13},{2,14},{3,15},{4,0},{5,1},{6,2},{7,3},{8,4},{9,5},{1... | collective-permute-start | bytes 1032200 | tf_op jit(solution)/shard_map/ppermute | solution.py:318
  32.1 1.6 %copy-start.7 = (bf16[1,768,256]{2,1,0:T(8,128)(2,1)S(1)}, bf16[1,768,256]{2,1,0:T(8,128)(2,1)}, u32[]{:S(2)}) copy-start(bf16[1,768,256]{2,1,0:T(8,128)(2,1)} %param.22) | copy-start | bytes 1179652
  32.1 1.6 %copy-start.8 = (bf16[1,768,256]{2,1,0:T(8,128)(2,1)S(1)}, bf16[1,768,256]{2,1,0:T(8,128)(2,1)}, u32[]{:S(2)}) copy-start(bf16[1,768,256]{2,1,0:T(8,128)(2,1)} %param.23) | copy-start | bytes 1179652
  35.0 17.8 %collective-permute-start.7 = (bf16[384,512]{1,0:T(8,128)(2,1)S(1)}, bf16[384,512]{1,0:T(8,128)(2,1)S(1)}, u32[]{:S(2)}, u32[]{:S(2)}) collective-permute-start(bf16[384,512]{1,0:T(8,128)(2,1)S(1)} %get-tuple-element.65), channel_id=1, source_target_pairs={{0,1},{1,0},{2,3},{3,2},{4,5},{5,4},{6,7},{7,6},{8,9},{9,8},{10,11... | collective-permute-start | bytes 1179656 | tf_op jit(solution)/shard_map/ppermute | solution.py:325
  48.0 22.5 %copy-start.4 = (bf16[1,3584,256]{2,1,0:T(8,128)(2,1)S(1)}, bf16[1,3584,256]{2,1,0:T(8,128)(2,1)}, u32[]{:S(2)}) copy-start(bf16[1,3584,256]{2,1,0:T(8,128)(2,1)} %param.24) | copy-start | bytes 5505028
  48.0 22.5 %copy-start.5 = (bf16[1,3584,256]{2,1,0:T(8,128)(2,1)S(1)}, bf16[1,3584,256]{2,1,0:T(8,128)(2,1)}, u32[]{:S(2)}) copy-start(bf16[1,3584,256]{2,1,0:T(8,128)(2,1)} %param.25) | copy-start | bytes 5505028
  48.0 16.7 %collective-permute-start.6 = (bf16[48,3584]{1,0:T(8,128)(2,1)S(1)}, bf16[48,3584]{1,0:T(8,128)(2,1)S(1)}, u32[]{:S(2)}, u32[]{:S(2)}) collective-permute-start(bf16[48,3584]{1,0:T(8,128)(2,1)S(1)} %get-tuple-element.62), channel_id=1, source_target_pairs={{0,8},{1,9},{2,10},{3,11},{4,12},{5,13},{6,14},{7,15},{8,0},{9,1},... | collective-permute-start | bytes 1032200 | tf_op jit(solution)/shard_map/ppermute | solution.py:318
  50.6 11.0 %collective-permute-start.12 = (bf16[48,3584]{1,0:T(8,128)(2,1)S(1)}, bf16[48,3584]{1,0:T(8,128)(2,1)S(1)}, u32[]{:S(2)}, u32[]{:S(2)}) collective-permute-start(bf16[48,3584]{1,0:T(8,128)(2,1)S(1)} %collective-permute-done.11.refs_1_), channel_id=1, source_target_pairs={{0,2},{1,3},{2,0},{3,1},{4,6},{5,7},{6,4},{7,5},{8,10},{9,11},{10,... | collective-permute-start | bytes 1032200 | tf_op jit(solution)/shard_map/ppermute | solution.py:322
  52.3 35.3 %collective-permute-start.17 = (bf16[128,3584]{1,0:T(8,128)(2,1)S(1)}, bf16[128,3584]{1,0:T(8,128)(2,1)S(1)}, u32[]{:S(2)}, u32[]{:S(2)}) collective-permute-start(bf16[128,3584]{1,0:T(8,128)(2,1)S(1)} %get-tuple-element.113), channel_id=1, source_target_pairs={{0,1},{1,0},{2,3},{3,2},{4,5},{5,4},{6,7},{7,6},{8,9},{9,8},{10,11... | collective-permute-start | bytes 2752520 | tf_op jit(solution)/shard_map/ppermute | solution.py:325
  52.3 35.2 %collective-permute-start.16 = (bf16[128,3584]{1,0:T(8,128)(2,1)S(1)}, bf16[128,3584]{1,0:T(8,128)(2,1)S(1)}, u32[]{:S(2)}, u32[]{:S(2)}) collective-permute-start(bf16[128,3584]{1,0:T(8,128)(2,1)S(1)} %get-tuple-element.114), channel_id=1, source_target_pairs={{0,1},{1,0},{2,3},{3,2},{4,5},{5,4},{6,7},{7,6},{8,9},{9,8},{10,11... | collective-permute-start | bytes 2752520 | tf_op jit(solution)/shard_map/ppermute | solution.py:325
  52.8 16.2 %collective-permute-start.9 = (bf16[48,3584]{1,0:T(8,128)(2,1)S(1)}, bf16[48,3584]{1,0:T(8,128)(2,1)S(1)}, u32[]{:S(2)}, u32[]{:S(2)}) collective-permute-start(bf16[48,3584]{1,0:T(8,128)(2,1)S(1)} %collective-permute-done.8.refs_0_), channel_id=1, source_target_pairs={{0,2},{1,3},{2,0},{3,1},{4,6},{5,7},{6,4},{7,5},{8,10},{9,11},{10,... | collective-permute-start | bytes 1032200 | tf_op jit(solution)/shard_map/ppermute | solution.py:322
  61.6 21.6 %collective-permute-start.13 = (bf16[48,3584]{1,0:T(8,128)(2,1)S(1)}, bf16[48,3584]{1,0:T(8,128)(2,1)S(1)}, u32[]{:S(2)}, u32[]{:S(2)}) collective-permute-start(bf16[48,3584]{1,0:T(8,128)(2,1)S(1)} %get-tuple-element.71.refs_1_), channel_id=1, source_target_pairs={{0,2},{1,3},{2,0},{3,1},{4,6},{5,7},{6,4},{7,5},{8,10},{9,11},{10,... | collective-permute-start | bytes 1032200 | tf_op jit(solution)/shard_map/ppermute | solution.py:322
  69.0 12.8 %collective-permute-start.10 = (bf16[48,3584]{1,0:T(8,128)(2,1)S(1)}, bf16[48,3584]{1,0:T(8,128)(2,1)S(1)}, u32[]{:S(2)}, u32[]{:S(2)}) collective-permute-start(bf16[48,3584]{1,0:T(8,128)(2,1)S(1)} %get-tuple-element.69.refs_0_), channel_id=1, source_target_pairs={{0,2},{1,3},{2,0},{3,1},{4,6},{5,7},{6,4},{7,5},{8,10},{9,11},{10,... | collective-permute-start | bytes 1032200 | tf_op jit(solution)/shard_map/ppermute | solution.py:322
  70.5 7.2 %collective-permute-start.20 = (bf16[48,3584]{1,0:T(8,128)(2,1)S(1)}, bf16[48,3584]{1,0:T(8,128)(2,1)S(1)}, u32[]{:S(2)}, u32[]{:S(2)}) collective-permute-start(bf16[48,3584]{1,0:T(8,128)(2,1)S(1)} %get-tuple-element.86), channel_id=1, source_target_pairs={{0,4},{1,5},{2,6},{3,7},{4,8},{5,9},{6,10},{7,11},{8,12},{9,13},{1... | collective-permute-start | bytes 1032200 | tf_op jit(solution)/shard_map/ppermute | solution.py:318
  77.8 14.7 %collective-permute-start.21 = (bf16[48,3584]{1,0:T(8,128)(2,1)S(1)}, bf16[48,3584]{1,0:T(8,128)(2,1)S(1)}, u32[]{:S(2)}, u32[]{:S(2)}) collective-permute-start(bf16[48,3584]{1,0:T(8,128)(2,1)S(1)} %get-tuple-element.87), channel_id=1, source_target_pairs={{0,12},{1,13},{2,14},{3,15},{4,0},{5,1},{6,2},{7,3},{8,4},{9,5},{1... | collective-permute-start | bytes 1032200 | tf_op jit(solution)/shard_map/ppermute | solution.py:318
  81.8 5.8 %copy-start.3 = (bf16[1,256,3584]{2,1,0:T(8,128)(2,1)S(1)}, bf16[1,256,3584]{2,1,0:T(8,128)(2,1)}, u32[]{:S(2)}) copy-start(bf16[1,256,3584]{2,1,0:T(8,128)(2,1)} %param.26) | copy-start | bytes 5505028
  81.8 5.8 %collective-permute-start.18 = (bf16[96,512]{1,0:T(8,128)(2,1)S(1)}, bf16[96,512]{1,0:T(8,128)(2,1)S(1)}, u32[]{:S(2)}, u32[]{:S(2)}) collective-permute-start(bf16[96,512]{1,0:T(8,128)(2,1)S(1)} %get-tuple-element.80), channel_id=1, source_target_pairs={{0,2},{1,3},{2,0},{3,1},{4,6},{5,7},{6,4},{7,5},{8,10},{9,11},{10,... | collective-permute-start | bytes 294920 | tf_op jit(solution)/shard_map/ppermute | solution.py:322
  86.9 11.1 %collective-permute-start.14 = (bf16[96,512]{1,0:T(8,128)(2,1)S(1)}, bf16[96,512]{1,0:T(8,128)(2,1)S(1)}, u32[]{:S(2)}, u32[]{:S(2)}) collective-permute-start(bf16[96,512]{1,0:T(8,128)(2,1)S(1)} %get-tuple-element.74), channel_id=1, source_target_pairs={{0,2},{1,3},{2,0},{3,1},{4,6},{5,7},{6,4},{7,5},{8,10},{9,11},{10,... | collective-permute-start | bytes 294920 | tf_op jit(solution)/shard_map/ppermute | solution.py:322
  90.4 28.9 %collective-permute-start.19 = (bf16[48,3584]{1,0:T(8,128)(2,1)S(1)}, bf16[48,3584]{1,0:T(8,128)(2,1)S(1)}, u32[]{:S(2)}, u32[]{:S(2)}) collective-permute-start(bf16[48,3584]{1,0:T(8,128)(2,1)S(1)} %get-tuple-element.82), channel_id=1, source_target_pairs={{0,12},{1,13},{2,14},{3,15},{4,0},{5,1},{6,2},{7,3},{8,4},{9,5},{1... | collective-permute-start | bytes 1032200 | tf_op jit(solution)/shard_map/ppermute | solution.py:318
  90.9 35.1 %collective-permute-start.23 = (bf16[48,3584]{1,0:T(8,128)(2,1)S(1)}, bf16[48,3584]{1,0:T(8,128)(2,1)S(1)}, u32[]{:S(2)}, u32[]{:S(2)}) collective-permute-start(bf16[48,3584]{1,0:T(8,128)(2,1)S(1)} %get-tuple-element.90), channel_id=1, source_target_pairs={{0,4},{1,5},{2,6},{3,7},{4,8},{5,9},{6,10},{7,11},{8,12},{9,13},{1... | collective-permute-start | bytes 1032200 | tf_op jit(solution)/shard_map/ppermute | solution.py:318
  96.5 6.5 %collective-permute-start.24 = (bf16[192,512]{1,0:T(8,128)(2,1)S(1)}, bf16[192,512]{1,0:T(8,128)(2,1)S(1)}, u32[]{:S(2)}, u32[]{:S(2)}) collective-permute-start(bf16[192,512]{1,0:T(8,128)(2,1)S(1)} %get-tuple-element.98), channel_id=1, source_target_pairs={{0,2},{1,3},{2,0},{3,1},{4,6},{5,7},{6,4},{7,5},{8,10},{9,11},{10,... | collective-permute-start | bytes 589832 | tf_op jit(solution)/shard_map/ppermute | solution.py:322
  100.8 31.7 %collective-permute-start.22 = (bf16[48,3584]{1,0:T(8,128)(2,1)S(1)}, bf16[48,3584]{1,0:T(8,128)(2,1)S(1)}, u32[]{:S(2)}, u32[]{:S(2)}) collective-permute-start(bf16[48,3584]{1,0:T(8,128)(2,1)S(1)} %get-tuple-element.88), channel_id=1, source_target_pairs={{0,8},{1,9},{2,10},{3,11},{4,12},{5,13},{6,14},{7,15},{8,0},{9,1},... | collective-permute-start | bytes 1032200 | tf_op jit(solution)/shard_map/ppermute | solution.py:318
  107.4 11.1 %collective-permute-start.28 = (bf16[48,3584]{1,0:T(8,128)(2,1)S(1)}, bf16[48,3584]{1,0:T(8,128)(2,1)S(1)}, u32[]{:S(2)}, u32[]{:S(2)}) collective-permute-start(bf16[48,3584]{1,0:T(8,128)(2,1)S(1)} %get-tuple-element.107), channel_id=1, source_target_pairs={{0,2},{1,3},{2,0},{3,1},{4,6},{5,7},{6,4},{7,5},{8,10},{9,11},{10,... | collective-permute-start | bytes 1032200 | tf_op jit(solution)/shard_map/ppermute | solution.py:322
  108.2 17.7 %collective-permute-start.25 = (bf16[48,3584]{1,0:T(8,128)(2,1)S(1)}, bf16[48,3584]{1,0:T(8,128)(2,1)S(1)}, u32[]{:S(2)}, u32[]{:S(2)}) collective-permute-start(bf16[48,3584]{1,0:T(8,128)(2,1)S(1)} %get-tuple-element.101), channel_id=1, source_target_pairs={{0,2},{1,3},{2,0},{3,1},{4,6},{5,7},{6,4},{7,5},{8,10},{9,11},{10,... | collective-permute-start | bytes 1032200 | tf_op jit(solution)/shard_map/ppermute | solution.py:322
  118.5 13.9 %collective-permute-start.30 = (bf16[48,3584]{1,0:T(8,128)(2,1)S(1)}, bf16[48,3584]{1,0:T(8,128)(2,1)S(1)}, u32[]{:S(2)}, u32[]{:S(2)}) collective-permute-start(bf16[48,3584]{1,0:T(8,128)(2,1)S(1)} %get-tuple-element.111), channel_id=1, source_target_pairs={{0,2},{1,3},{2,0},{3,1},{4,6},{5,7},{6,4},{7,5},{8,10},{9,11},{10,... | collective-permute-start | bytes 1032200 | tf_op jit(solution)/shard_map/ppermute | solution.py:322
  119.3 21.9 %collective-permute-start.29 = (bf16[48,3584]{1,0:T(8,128)(2,1)S(1)}, bf16[48,3584]{1,0:T(8,128)(2,1)S(1)}, u32[]{:S(2)}, u32[]{:S(2)}) collective-permute-start(bf16[48,3584]{1,0:T(8,128)(2,1)S(1)} %add_rows.6), channel_id=1, source_target_pairs={{0,8},{1,9},{2,10},{3,11},{4,12},{5,13},{6,14},{7,15},{8,0},{9,1},... | collective-permute-start | bytes 1032200 | tf_op jit(solution)/shard_map/ppermute | solution.py:318
  126.0 10.3 %collective-permute-start.26 = (bf16[48,3584]{1,0:T(8,128)(2,1)S(1)}, bf16[48,3584]{1,0:T(8,128)(2,1)S(1)}, u32[]{:S(2)}, u32[]{:S(2)}) collective-permute-start(bf16[48,3584]{1,0:T(8,128)(2,1)S(1)} %get-tuple-element.102), channel_id=1, source_target_pairs={{0,2},{1,3},{2,0},{3,1},{4,6},{5,7},{6,4},{7,5},{8,10},{9,11},{10,... | collective-permute-start | bytes 1032200 | tf_op jit(solution)/shard_map/ppermute | solution.py:322
  126.7 23.0 %collective-permute-start.27 = (bf16[48,3584]{1,0:T(8,128)(2,1)S(1)}, bf16[48,3584]{1,0:T(8,128)(2,1)S(1)}, u32[]{:S(2)}, u32[]{:S(2)}) collective-permute-start(bf16[48,3584]{1,0:T(8,128)(2,1)S(1)} %add_rows.5), channel_id=1, source_target_pairs={{0,12},{1,13},{2,14},{3,15},{4,0},{5,1},{6,2},{7,3},{8,4},{9,5},{1... | collective-permute-start | bytes 1032200 | tf_op jit(solution)/shard_map/ppermute | solution.py:318
  132.4 0.7 copy-start.12
  132.5 18.5 %collective-permute-start.31 = (bf16[48,3584]{1,0:T(8,128)(2,1)S(1)}, bf16[48,3584]{1,0:T(8,128)(2,1)S(1)}, u32[]{:S(2)}, u32[]{:S(2)}) collective-permute-start(bf16[48,3584]{1,0:T(8,128)(2,1)S(1)} %add_rows.7), channel_id=1, source_target_pairs={{0,4},{1,5},{2,6},{3,7},{4,8},{5,9},{6,10},{7,11},{8,12},{9,13},{1... | collective-permute-start | bytes 1032200 | tf_op jit(solution)/shard_map/ppermute | solution.py:318
